TPU v7x, 32 devices: a whole 2x2x4 slice. The times are simulated.
32 devices in a mesh: dp: 4 (over y, core), heads: 8 (over z, x).
Axes of the slice: x: 2, y: 2, z: 4, core: 2. Of those that a mesh axis runs over, the one named last changes fastest.
Arguments:
- block_input: float32 [4096, 2048], P(('dp', 'heads')), may hold values from -6 to 6
- output_grad: float32 [4096, 2048], P(('dp', 'heads'))
- lengths: int32 [4, 6], P('dp'), may hold values from 1 to 896, 1024 in all within a row
- norm_gains: float32 [5120], replicated, may hold values from 0.48 to 2.25
- norm_gains_first: float32 [5120], replicated
- norm_gains_second: float32 [5120], replicated, may hold values from 4096 to 16384
- query_down: float32 [2048, 1024], P('dp')
- query_down_first: float32 [2048, 1024], P('dp')
- query_down_second: float32 [2048, 1024], P('dp'), may hold values from 2621.44 to 10485.76
- key_value: float32 [2048, 512], P('dp')
- key_value_first: float32 [2048, 512], P('dp')
- key_value_second: float32 [2048, 512], P('dp'), may hold values from 16384 to 65536
- query_up: float32 [1024, 4096], P('dp', 'heads')
- query_up_first: float32 [1024, 4096], P('dp', 'heads')
- query_up_second: float32 [1024, 4096], P('dp', 'heads'), may hold values from 1024 to 4096
- head_merge: float32 [4096, 2048], P('heads', 'dp')
- head_merge_first: float32 [4096, 2048], P('heads', 'dp')
- head_merge_second: float32 [4096, 2048], P('heads', 'dp'), may hold values from 368.64 to 1474.56
- gate_weight: float32 [2048, 5632], P('dp', 'heads')
- gate_weight_first: float32 [2048, 5632], P('dp', 'heads')
- gate_weight_second: float32 [2048, 5632], P('dp', 'heads'), may hold values from 2621.44 to 10485.76
- up_weight: float32 [2048, 5632], P('dp', 'heads')
- up_weight_first: float32 [2048, 5632], P('dp', 'heads')
- up_weight_second: float32 [2048, 5632], P('dp', 'heads'), may hold values from 2621.44 to 10485.76
- down_weight: float32 [5632, 2048], P('heads', 'dp')
- down_weight_first: float32 [5632, 2048], P('heads', 'dp')
- down_weight_second: float32 [5632, 2048], P('heads', 'dp'), may hold values from 4096 to 16384
Outputs:
- block_output: float32 [4096, 2048], P(('dp', 'heads'))
- input_grad: float32 [4096, 2048], P(('dp', 'heads'))
- norm_gains_first_new: float32 [5120], replicated
- norm_gains_second_new: float32 [5120], replicated
- norm_gains_new: float32 [5120], replicated
- query_down_first_new: float32 [2048, 1024], P('dp')
- query_down_second_new: float32 [2048, 1024], P('dp')
- query_down_new: float32 [2048, 1024], P('dp')
- key_value_first_new: float32 [2048, 512], P('dp')
- key_value_second_new: float32 [2048, 512], P('dp')
- key_value_new: float32 [2048, 512], P('dp')
- query_up_first_new: float32 [1024, 4096], P('dp', 'heads')
- query_up_second_new: float32 [1024, 4096], P('dp', 'heads')
- query_up_new: float32 [1024, 4096], P('dp', 'heads')
- head_merge_first_new: float32 [4096, 2048], P('heads', 'dp')
- head_merge_second_new: float32 [4096, 2048], P('heads', 'dp')
- head_merge_new: float32 [4096, 2048], P('heads', 'dp')
- gate_weight_first_new: float32 [2048, 5632], P('dp', 'heads')
- gate_weight_second_new: float32 [2048, 5632], P('dp', 'heads')
- gate_weight_new: float32 [2048, 5632], P('dp', 'heads')
- up_weight_first_new: float32 [2048, 5632], P('dp', 'heads')
- up_weight_second_new: float32 [2048, 5632], P('dp', 'heads')
- up_weight_new: float32 [2048, 5632], P('dp', 'heads')
- down_weight_first_new: float32 [5632, 2048], P('heads', 'dp')
- down_weight_second_new: float32 [5632, 2048], P('heads', 'dp')
- down_weight_new: float32 [5632, 2048], P('heads', 'dp')
- norms: float32 [8, 2], replicated
All inputs are finite; a program needn't handle non-finite values.
Results may differ from a plain program's by a relative error of at most 0.0003.
Values sent between devices are 32-bit elements; how exact they have to be, the bound alone decides.
A program may use at most 256 MiB of HBM per device.

v0:
```python
import jax
import jax.numpy as jnp
from jax import lax
from jax.sharding import PartitionSpec as P

STEP_COUNT = 10


EPS_NORM = 1e-06
ROPE_BASE = 10000.0
BETA_ONE = 0.5
BETA_TWO = 0.6
ADAM_EPS = 1e-06
DECAY = 0.01
RATE = 0.5
HIGH = lax.Precision.HIGHEST


def matmul_high(left, right):
    return jnp.dot(left, right, precision=HIGH, preferred_element_type=jnp.float32)


def layout(lengths_row, row_index):
    doc_ends = jnp.cumsum(lengths_row)
    doc_starts = doc_ends - lengths_row
    segment = jnp.sum((row_index[:, None] >= doc_ends[None, :]).astype(jnp.int32), axis=1)
    doc_ids = jnp.arange(doc_ends.shape[0], dtype=jnp.int32)
    start_of = jnp.sum(
        jnp.where(segment[:, None] == doc_ids[None, :], doc_starts[None, :], 0), axis=1
    )
    return (segment, row_index - start_of)


def rotate(vector, position, sign):
    half_dim = vector.shape[-1] // 2
    frequency = ROPE_BASE ** (-jnp.arange(half_dim, dtype=jnp.float32) / half_dim)
    angles = position.astype(jnp.float32)[:, None] * frequency[None, :]
    angles = angles.reshape((angles.shape[0],) + (1,) * (vector.ndim - 2) + (half_dim,))
    cosine = jnp.cos(angles)
    sines = sign * jnp.sin(angles)
    front = vector[..., :half_dim]
    back_half = vector[..., half_dim:]
    return jnp.concatenate(
        [front * cosine - back_half * sines, back_half * cosine + front * sines], axis=-1
    )


def norm_back(upstream, normed, inverse, gain):
    scaled = upstream * gain
    return (
        inverse * (scaled - normed * jnp.mean(scaled * normed, axis=1, keepdims=True)),
        jnp.sum(upstream * normed, axis=0),
    )


def share_grads(part_down, part_pair, part_gains):
    return lax.psum((part_down, part_pair, part_gains), "heads")


def spread_grads(part_down, part_pair, part_up, part_merge, part_gate, part_upper, part_lower):
    return (
        lax.psum_scatter(part_down, "dp", scatter_dimension=0, tiled=True),
        lax.psum_scatter(part_pair, "dp", scatter_dimension=0, tiled=True),
        lax.psum_scatter(part_up, "dp", scatter_dimension=0, tiled=True),
        lax.psum_scatter(part_merge, "dp", scatter_dimension=1, tiled=True),
        lax.psum_scatter(part_gate, "dp", scatter_dimension=0, tiled=True),
        lax.psum_scatter(part_upper, "dp", scatter_dimension=0, tiled=True),
        lax.psum_scatter(part_lower, "dp", scatter_dimension=1, tiled=True),
    )


def moments(value, grad, first, second):
    first_new = BETA_ONE * first + (1.0 - BETA_ONE) * grad
    second_new = BETA_TWO * second + (1.0 - BETA_TWO) * grad * grad
    update = (
        first_new
        / (1.0 - BETA_ONE**STEP_COUNT)
        / (jnp.sqrt(second_new / (1.0 - BETA_TWO**STEP_COUNT)) + ADAM_EPS)
        + DECAY * value
    )
    return (first_new, second_new, update)


def on_device(
    block_input,
    output_grad,
    lengths,
    norm_gains,
    norm_gains_first,
    norm_gains_second,
    query_down,
    query_down_first,
    query_down_second,
    key_value,
    key_value_first,
    key_value_second,
    query_up,
    query_up_first,
    query_up_second,
    head_merge,
    head_merge_first,
    head_merge_second,
    gate_weight,
    gate_weight_first,
    gate_weight_second,
    up_weight,
    up_weight_first,
    up_weight_second,
    down_weight,
    down_weight_first,
    down_weight_second,
):
    tok_rows = block_input.shape[0]
    model_dim = block_input.shape[1]
    latent_dim = query_down.shape[1]
    head_dim = key_value.shape[1] // 2
    local_heads = query_up.shape[1] // head_dim
    heads_count = lax.axis_size("heads")
    group_rows = tok_rows * heads_count
    scale = head_dim ** (-0.5)
    wide_down, wide_pair, wide_up, wide_merge, wide_gate, wide_upper, wide_lower = (
        lax.all_gather(query_down, "dp", axis=0, tiled=True),
        lax.all_gather(key_value, "dp", axis=0, tiled=True),
        lax.all_gather(query_up, "dp", axis=0, tiled=True),
        lax.all_gather(head_merge, "dp", axis=1, tiled=True),
        lax.all_gather(gate_weight, "dp", axis=0, tiled=True),
        lax.all_gather(up_weight, "dp", axis=0, tiled=True),
        lax.all_gather(down_weight, "dp", axis=1, tiled=True),
    )
    group_index = jnp.arange(group_rows, dtype=jnp.int32)
    segment, position = layout(lengths[0], group_index)
    local_position = lax.dynamic_slice_in_dim(
        position, lax.axis_index("heads") * tok_rows, tok_rows
    )
    gain_attn = norm_gains[:model_dim]
    gain_query = norm_gains[model_dim : model_dim + latent_dim]
    gain_ffn = norm_gains[model_dim + latent_dim :]
    inv_one = lax.rsqrt(jnp.mean(block_input * block_input, axis=1, keepdims=True) + EPS_NORM)
    normed_one = block_input * inv_one
    hidden_one = normed_one * gain_attn
    latent_raw = matmul_high(hidden_one, wide_down)
    inv_query = lax.rsqrt(jnp.mean(latent_raw * latent_raw, axis=1, keepdims=True) + EPS_NORM)
    latent_hat = latent_raw * inv_query
    latent = latent_hat * gain_query
    pair_local = matmul_high(hidden_one, wide_pair)
    key_local = rotate(pair_local[:, :head_dim], local_position, 1.0)
    value_local = pair_local[:, head_dim:]
    latent_all, key_all, value_all = (
        lax.all_gather(latent, "heads", axis=0, tiled=True),
        lax.all_gather(key_local, "heads", axis=0, tiled=True),
        lax.all_gather(value_local, "heads", axis=0, tiled=True),
    )
    query_rot = rotate(
        matmul_high(latent_all, wide_up).reshape(group_rows, local_heads, head_dim), position, 1.0
    )
    block_rows = min(512, group_rows)
    n_blocks = group_rows // block_rows
    query_blocks = query_rot.reshape(n_blocks, block_rows, local_heads, head_dim)
    index_blocks = group_index.reshape(n_blocks, block_rows)
    segment_blocks = segment.reshape(n_blocks, block_rows)

    def block_scores(query_block, row_block, seg_block):
        scores = jnp.einsum("qhd,kd->hqk", query_block, key_all, precision=HIGH) * scale
        allowed = (seg_block[:, None] == segment[None, :]) & (
            group_index[None, :] <= row_block[:, None]
        )
        return jnp.where(allowed[None], scores, -1e30)

    def forward_block(inputs):
        query_block, row_block, seg_block = inputs
        scores = block_scores(query_block, row_block, seg_block)
        row_max = jnp.max(scores, axis=2, keepdims=True)
        expo = jnp.exp(scores - row_max)
        denom = jnp.sum(expo, axis=2, keepdims=True)
        mixed_block = jnp.einsum("hqk,kd->qhd", expo / denom, value_all, precision=HIGH)
        return (mixed_block, (row_max + jnp.log(denom))[..., 0])

    mixed_blocks, lse_blocks = lax.map(forward_block, (query_blocks, index_blocks, segment_blocks))
    mixed_heads = mixed_blocks.reshape(group_rows, local_heads * head_dim)
    middle = block_input + lax.psum_scatter(
        matmul_high(mixed_heads, wide_merge), "heads", scatter_dimension=0, tiled=True
    )
    inv_two = lax.rsqrt(jnp.mean(middle * middle, axis=1, keepdims=True) + EPS_NORM)
    normed_two = middle * inv_two
    hidden_two = normed_two * gain_ffn
    hidden_all = lax.all_gather(hidden_two, "heads", axis=0, tiled=True)
    gate_pre = matmul_high(hidden_all, wide_gate)
    up_pre = matmul_high(hidden_all, wide_upper)
    sig_gate = jax.nn.sigmoid(gate_pre)
    silu_gate = gate_pre * sig_gate
    activ = silu_gate * up_pre
    block_output = middle + lax.psum_scatter(
        matmul_high(activ, wide_lower), "heads", scatter_dimension=0, tiled=True
    )
    grad_all = lax.all_gather(output_grad, "heads", axis=0, tiled=True)
    d_activ = matmul_high(grad_all, wide_lower.T)
    grad_lower = matmul_high(activ.T, grad_all)
    d_gate_pre = d_activ * up_pre * (sig_gate * (1.0 + gate_pre * (1.0 - sig_gate)))
    d_up_pre = d_activ * silu_gate
    grad_gate = matmul_high(hidden_all.T, d_gate_pre)
    grad_upper = matmul_high(hidden_all.T, d_up_pre)
    d_hidden_two = lax.psum_scatter(
        matmul_high(d_gate_pre, wide_gate.T) + matmul_high(d_up_pre, wide_upper.T),
        "heads",
        scatter_dimension=0,
        tiled=True,
    )
    d_normed_mid, grad_gain_ffn = norm_back(d_hidden_two, normed_two, inv_two, gain_ffn)
    d_middle = output_grad + d_normed_mid
    middle_all = lax.all_gather(d_middle, "heads", axis=0, tiled=True)
    grad_merge = matmul_high(mixed_heads.T, middle_all)
    d_mixed = matmul_high(middle_all, wide_merge.T).reshape(
        n_blocks, block_rows, local_heads, head_dim
    )

    def backward_block(running, inputs):
        query_block, row_block, seg_block, grad_block, out_block, lse_block = inputs
        scores = block_scores(query_block, row_block, seg_block)
        probs = jnp.exp(scores - lse_block[..., None])
        d_probs = jnp.einsum("qhd,kd->hqk", grad_block, value_all, precision=HIGH)
        delta = jnp.sum(grad_block * out_block, axis=2)
        d_scores = probs * (d_probs - delta.T[:, :, None])
        d_query = jnp.einsum("hqk,kd->qhd", d_scores, key_all, precision=HIGH) * scale
        d_key = jnp.einsum("hqk,qhd->kd", d_scores, query_block, precision=HIGH) * scale
        d_value = jnp.einsum("hqk,qhd->kd", probs, grad_block, precision=HIGH)
        return ((running[0] + d_key, running[1] + d_value), d_query)

    zero_rows = jnp.zeros((group_rows, head_dim), jnp.float32)
    (d_key_sum, d_value_sum), d_query_blocks = lax.scan(
        backward_block,
        (zero_rows, zero_rows),
        (query_blocks, index_blocks, segment_blocks, d_mixed, mixed_blocks, lse_blocks),
    )
    d_query_pre = rotate(
        d_query_blocks.reshape(group_rows, local_heads, head_dim), position, -1.0
    ).reshape(group_rows, local_heads * head_dim)
    grad_up = matmul_high(latent_all.T, d_query_pre)
    d_latent_all = matmul_high(d_query_pre, wide_up.T)
    d_latent, d_key_local, d_value_local = (
        lax.psum_scatter(d_latent_all, "heads", scatter_dimension=0, tiled=True),
        lax.psum_scatter(d_key_sum, "heads", scatter_dimension=0, tiled=True),
        lax.psum_scatter(d_value_sum, "heads", scatter_dimension=0, tiled=True),
    )
    d_pair = jnp.concatenate([rotate(d_key_local, local_position, -1.0), d_value_local], axis=1)
    d_latent_raw, grad_gain_query = norm_back(d_latent, latent_hat, inv_query, gain_query)
    grad_down = matmul_high(hidden_one.T, d_latent_raw)
    grad_pair = matmul_high(hidden_one.T, d_pair)
    d_hidden_one = matmul_high(d_latent_raw, wide_down.T) + matmul_high(d_pair, wide_pair.T)
    d_normed_in, grad_gain_attn = norm_back(d_hidden_one, normed_one, inv_one, gain_attn)
    input_grad = d_middle + d_normed_in
    grad_gains = jnp.concatenate([grad_gain_attn, grad_gain_query, grad_gain_ffn])
    spread = spread_grads(
        grad_down, grad_pair, grad_up, grad_merge, grad_gate, grad_upper, grad_lower
    )
    shared = share_grads(spread[0], spread[1], grad_gains)
    reduced = (shared[0], shared[1]) + tuple(spread[2:])
    gains_total = lax.psum(shared[2], "dp")
    values = (
        norm_gains,
        query_down,
        key_value,
        query_up,
        head_merge,
        gate_weight,
        up_weight,
        down_weight,
    )
    firsts = (
        norm_gains_first,
        query_down_first,
        key_value_first,
        query_up_first,
        head_merge_first,
        gate_weight_first,
        up_weight_first,
        down_weight_first,
    )
    seconds = (
        norm_gains_second,
        query_down_second,
        key_value_second,
        query_up_second,
        head_merge_second,
        gate_weight_second,
        up_weight_second,
        down_weight_second,
    )
    grads = (
        gains_total,
        reduced[0],
        reduced[1],
        reduced[2],
        reduced[3],
        reduced[4],
        reduced[5],
        reduced[6],
    )
    stepped = [moments(values[slot], grads[slot], firsts[slot], seconds[slot]) for slot in range(8)]
    replica_share = [1.0, 1.0 / heads_count, 1.0 / heads_count, 1.0, 1.0, 1.0, 1.0, 1.0]
    square_rows = jnp.stack(
        [
            jnp.stack(
                [jnp.sum(values[slot] * values[slot]), jnp.sum(stepped[slot][2] * stepped[slot][2])]
            )
            * replica_share[slot]
            for slot in range(1, 8)
        ]
    )
    summed = lax.psum(square_rows, ("dp", "heads"))
    gains_row = jnp.stack(
        [jnp.sum(norm_gains * norm_gains), jnp.sum(stepped[0][2] * stepped[0][2])]
    )
    norm_table = jnp.sqrt(jnp.concatenate([gains_row[None, :], summed], axis=0))
    new_values = [
        values[slot] - RATE * (norm_table[slot, 0] / norm_table[slot, 1]) * stepped[slot][2]
        for slot in range(8)
    ]
    return (
        block_output,
        input_grad,
        stepped[0][0],
        stepped[0][1],
        new_values[0],
        stepped[1][0],
        stepped[1][1],
        new_values[1],
        stepped[2][0],
        stepped[2][1],
        new_values[2],
        stepped[3][0],
        stepped[3][1],
        new_values[3],
        stepped[4][0],
        stepped[4][1],
        new_values[4],
        stepped[5][0],
        stepped[5][1],
        new_values[5],
        stepped[6][0],
        stepped[6][1],
        new_values[6],
        stepped[7][0],
        stepped[7][1],
        new_values[7],
        norm_table,
    )


def solution(mesh):
    placed = (
        P(("dp", "heads"), None),
        P(("dp", "heads"), None),
        P("dp", None),
        P(),
        P(),
        P(),
        P("dp", None),
        P("dp", None),
        P("dp", None),
        P("dp", None),
        P("dp", None),
        P("dp", None),
        P("dp", "heads"),
        P("dp", "heads"),
        P("dp", "heads"),
        P("heads", "dp"),
        P("heads", "dp"),
        P("heads", "dp"),
        P("dp", "heads"),
        P("dp", "heads"),
        P("dp", "heads"),
        P("dp", "heads"),
        P("dp", "heads"),
        P("dp", "heads"),
        P("heads", "dp"),
        P("heads", "dp"),
        P("heads", "dp"),
    )
    return jax.shard_map(
        on_device,
        mesh=mesh,
        in_specs=placed,
        out_specs=(
            P(("dp", "heads"), None),
            P(("dp", "heads"), None),
            P(),
            P(),
            P(),
            P("dp", None),
            P("dp", None),
            P("dp", None),
            P("dp", None),
            P("dp", None),
            P("dp", None),
            P("dp", "heads"),
            P("dp", "heads"),
            P("dp", "heads"),
            P("heads", "dp"),
            P("heads", "dp"),
            P("heads", "dp"),
            P("dp", "heads"),
            P("dp", "heads"),
            P("dp", "heads"),
            P("dp", "heads"),
            P("dp", "heads"),
            P("dp", "heads"),
            P("heads", "dp"),
            P("heads", "dp"),
            P("heads", "dp"),
            P(),
        ),
        check_vma=False,
    )
```

profile of v0, /device:TPU:0, one launch (start us, length us, event | category | flops | bytes accessed | tf_op | source)
XLA Modules:
  0.0 2282.3 jit_solution(14847732091090255238)
XLA Ops:
  9.7 60.9 %all-gather.14.cloned.1.call-done = f32[2048,1024]{1,0:T(8,128)} async-done(((f32[512,1024]{1,0:T(8,128)}), f32[2048,1024]{1,0:T(8,128)}) %all-gather.14.cloned.1.call-update) | async-done | bytes 8388624 | tf_op jit(solution)/shard_map/all_gather | solution.py:122
  80.4 26.3 %all-gather.20.cloned.1.call-done = f32[2048,512]{1,0:T(8,128)} async-done(((f32[512,512]{1,0:T(8,128)}), f32[2048,512]{1,0:T(8,128)}) %all-gather.20.cloned.1.call-update) | async-done | bytes 4194320 | tf_op jit(solution)/shard_map/all_gather | solution.py:123
  130.9 76.0 %all-gather.16.cloned.1.call-done = f32[1024,1024]{1,0:T(8,128)} async-done(((f32[128,1024]{1,0:T(8,128)}), f32[1024,1024]{1,0:T(8,128)}) %all-gather.16.cloned.1.call-update) | async-done | bytes 4194320 | tf_op jit(solution)/shard_map/all_gather | solution.py:149
  247.9 41.5 %all-gather.24.cloned.1.call-done = f32[1024,256]{1,0:T(8,128)} async-done(((f32[128,256]{1,0:T(8,128)}), f32[1024,256]{1,0:T(8,128)}) %all-gather.24.cloned.1.call-update) | async-done | bytes 1048592 | tf_op jit(solution)/shard_map/all_gather | solution.py:151
  289.4 25.9 %while.28 = (s32[]{:T(128)}, f32[2,512,2,256]{3,1,2,0:T(8,128)}, f32[2,2,512]{2,1,0:T(2,128)S(1)}, s32[2,512]{1,0:T(2,128)S(1)}, s32[1024]{0:T(1024)S(1)}, /*ind...) while((s32[]{:T(128)}, f32[2,512,2,256]{3,1,2,0:T(8,128)}, ...), condition=%wide.region_8.9_spmd.clone, body=%wide.region_5.8_spmd.clone.sunk | while | flops 6455557120 | bytes 23118476 | solution.py:178
  344.3 147.1 %reduce-scatter.14.cloned.1.call-done = f32[128,2048]{1,0:T(8,128)} async-done(((f32[1024,2048]{1,0:T(8,128)}), f32[128,2048]{1,0:T(8,128)}) %reduce-scatter.14.cloned.1.call-update) | async-done | bytes 1048592 | tf_op jit(solution)/shard_map/reduce_scatter | solution.py:180
  494.7 40.7 %all-gather.34.cloned.1.call-done = f32[704,2048]{1,0:T(8,128)} async-done(((f32[704,512]{1,0:T(8,128)}), f32[704,2048]{1,0:T(8,128)}) %all-gather.34.cloned.1.call-update) | async-done | bytes 5767184 | tf_op jit(solution)/shard_map/all_gather | solution.py:128
  535.4 127.2 %all-gather.36.cloned.1.call-done = f32[1024,2048]{1,0:T(8,128)} async-done(((f32[128,2048]{1,0:T(8,128)}), f32[1024,2048]{1,0:T(8,128)}) %all-gather.36.cloned.1.call-update) | async-done | bytes 8388624 | tf_op jit(solution)/shard_map/all_gather | solution.py:195
  705.9 127.7 %all-gather.28.cloned.1.call-done = f32[1024,2048]{1,0:T(8,128)} async-done(((f32[128,2048]{1,0:T(8,128)}), f32[1024,2048]{1,0:T(8,128)}) %all-gather.28.cloned.1.call-update) | async-done | bytes 8388624 | tf_op jit(solution)/shard_map/all_gather | solution.py:186
  946.2 26.7 %fusion.71 = f32[1024,2048]{1,0:T(8,128)} fusion(f32[704,2048]{1,0:T(8,128)} %all-gather.34.cloned.1.call-done, f32[1024,704]{0,1:T(8,128)} %fusion.135, f32[1024,704]{0,1:T(8,128)} %copy-done.62), kind=kOutput, calls=%fused_computation.105 | convolution fusion | flops 17720344576 | bytes 19922944 | tf_op jit(solution)/shard_map/dot_general | solution.py:20
  972.9 122.4 %reduce-scatter.18.cloned.1.call-done = f32[128,2048]{1,0:T(8,128)} async-done(((f32[1024,2048]{1,0:T(8,128)}), f32[128,2048]{1,0:T(8,128)}) %reduce-scatter.18.cloned.1.call-update) | async-done | bytes 1048592 | tf_op jit(solution)/shard_map/reduce_scatter | solution.py:202
  1096.9 149.9 %reduce-scatter.16.cloned.1.call-done = f32[128,2048]{1,0:T(8,128)} async-done(((f32[1024,2048]{1,0:T(8,128)}), f32[128,2048]{1,0:T(8,128)}) %reduce-scatter.16.cloned.1.call-update) | async-done | bytes 1048592 | tf_op jit(solution)/shard_map/reduce_scatter | solution.py:192
  1250.1 124.0 %all-gather.38.cloned.1.call-done = f32[1024,2048]{1,0:T(8,128)} async-done(((f32[128,2048]{1,0:T(8,128)}), f32[1024,2048]{1,0:T(8,128)}) %all-gather.38.cloned.1.call-update) | async-done | bytes 8388624 | tf_op jit(solution)/shard_map/all_gather | solution.py:210
  1393.0 75.9 %while.29 = (s32[]{:T(128)}, f32[1024,256]{1,0:T(8,128)}, f32[1024,256]{1,0:T(8,128)}, f32[2,512,2,256]{3,1,0,2:T(8,128)}, s32[2,512]{1,0:T(2,128)S(1)}, /*index...) while((s32[]{:T(128)}, f32[1024,256]{1,0:T(8,128)}, ...), condition=%wide.region_16.17_spmd.clone, body=%wide.region_14.16_spmd.clone.sunk | while | flops 16118184960 | bytes 106472760 | solution.py:229
  1603.1 84.8 %reduce-scatter.20.cloned.1.call-done = f32[128,1024]{1,0:T(8,128)} async-done(((f32[1024,1024]{1,0:T(8,128)}), f32[128,1024]{1,0:T(8,128)}) %reduce-scatter.20.cloned.1.call-update) | async-done | bytes 524304 | tf_op jit(solution)/shard_map/reduce_scatter | solution.py:240
  1752.3 50.2 %reduce-scatter.36.cloned.1.call-done = f32[512,704]{0,1:T(8,128)} async-done(((f32[2048,704]{0,1:T(8,128)}), f32[512,704]{0,1:T(8,128)}) %reduce-scatter.36.cloned.1.call-update) | async-done | bytes 1441808 | tf_op jit(solution)/shard_map/reduce_scatter | solution.py:67
  1810.4 49.6 %reduce-scatter.34.cloned.1.call-done = f32[512,704]{0,1:T(8,128)} async-done(((f32[2048,704]{0,1:T(8,128)}), f32[512,704]{0,1:T(8,128)}) %reduce-scatter.34.cloned.1.call-update) | async-done | bytes 1441808 | tf_op jit(solution)/shard_map/reduce_scatter | solution.py:66
  1866.0 41.2 %reduce-scatter.28.cloned.1.call-done = f32[512,512]{1,0:T(8,128)} async-done(((f32[2048,512]{1,0:T(8,128)}), f32[512,512]{1,0:T(8,128)}) %reduce-scatter.28.cloned.1.call-update) | async-done | bytes 1048592 | tf_op jit(solution)/shard_map/reduce_scatter | solution.py:63
  1907.2 74.2 %reduce-scatter.26.cloned.1.call-done = f32[512,1024]{1,0:T(8,128)} async-done(((f32[2048,1024]{1,0:T(8,128)}), f32[512,1024]{1,0:T(8,128)}) %reduce-scatter.26.cloned.1.call-update) | async-done | bytes 2097168 | tf_op jit(solution)/shard_map/reduce_scatter | solution.py:62
  1983.2 33.0 %reduce-scatter.30.cloned.1.call-done = f32[256,512]{1,0:T(8,128)} async-done(((f32[1024,512]{1,0:T(8,128)}), f32[256,512]{1,0:T(8,128)}) %reduce-scatter.30.cloned.1.call-update) | async-done | bytes 524304 | tf_op jit(solution)/shard_map/reduce_scatter | solution.py:64
  2021.0 42.1 %reduce-scatter.32.cloned.1.call-done = f32[512,512]{1,0:T(8,128)} async-done(((f32[512,2048]{1,0:T(8,128)}), f32[512,512]{1,0:T(8,128)}) %reduce-scatter.32.cloned.1.call-update) | async-done | bytes 1048592 | tf_op jit(solution)/shard_map/reduce_scatter | solution.py:65
  2086.5 38.6 %psum.35 = f32[5120]{0:T(1024)S(1)} all-reduce(f32[5120]{0:T(1024)S(1)} %pad_maximum_fusion.6), channel_id=1, replica_groups=mesh['dp'=4,'heads'=8] {'heads'}, use_global_device_ids=true, to_apply=%region_25.26 | all-reduce | flops 5120 | bytes 40960 | tf_op jit(solution)/shard_map/psum | solution.py:57
  2141.3 55.9 %all-reduce.3.cloned.1.call-done = (f32[512,1024]{1,0:T(8,128)}, f32[512,512]{1,0:T(8,128)}) async-done(((f32[512,1024]{1,0:T(8,128)}, f32[512,512]{1,0:T(8,128)}), (f32[512,1024]{1,0:T(8,128)}, f32[512,512]{1,0:T(8,128)})) %all-reduce.3.cloned.1.call-update) | async-done | bytes 3145744 | tf_op jit(solution)/shard_map/psum | solution.py:57
  2211.2 39.1 %psum.39 = f32[7,2]{0,1:T(2,128)S(1)} all-reduce(f32[7,2]{0,1:T(2,128)S(1)} %stack.121), channel_id=1, replica_groups=mesh['dp'=4,'heads'=8] {'dp','heads'}, use_global_device_ids=true, to_apply=%region_52.53 | all-reduce | flops 14 | bytes 112 | tf_op jit(solution)/shard_map/psum | solution.py:309
  (337 shorter events, 676.2 us)
Async XLA Ops:
  9.4 197.5 %all-gather.16.cloned.1.call-start = ((), (), s32[]{:S(2)}) async-start(), calls=%async_computation.14 | async-start | bytes 4718592 | tf_op jit(solution)/shard_map/all_gather | solution.py:149
  79.9 168.1 %all-gather.22.cloned.1.call-start = ((), (), s32[]{:S(2)}) async-start(), calls=%async_computation.17 | async-start | bytes 1179648 | tf_op jit(solution)/shard_map/all_gather | solution.py:150
  112.4 177.0 %all-gather.24.cloned.1.call-start = ((), (), s32[]{:S(2)}) async-start(), calls=%async_computation.18 | async-start | bytes 1179648 | tf_op jit(solution)/shard_map/all_gather | solution.py:151
  113.2 211.1 %all-gather.26.cloned.1.call-start = ((), (), s32[]{:S(2)}) async-start(), calls=%async_computation.19 | async-start | bytes 5242880 | tf_op jit(solution)/shard_map/all_gather | solution.py:125
  113.9 377.4 %reduce-scatter.14.cloned.1.call-start = ((), (), s32[]{:S(2)}) async-start(), calls=%async_computation.20 | async-start | bytes 9437184 | tf_op jit(solution)/shard_map/reduce_scatter | solution.py:180
  342.2 193.3 %all-gather.34.cloned.1.call-start = ((), (), s32[]{:S(2)}) async-start(), calls=%async_computation.24 | async-start | bytes 7208960 | tf_op jit(solution)/shard_map/all_gather | solution.py:128
  342.9 319.7 %all-gather.36.cloned.1.call-start = ((), (), s32[]{:S(2)}) async-start(), calls=%async_computation.26 | async-start | bytes 9437184 | tf_op jit(solution)/shard_map/all_gather | solution.py:195
  343.5 362.4 %all-gather.32.cloned.1.call-start = ((), (), s32[]{:S(2)}) async-start(), calls=%async_computation.23 | async-start | bytes 7208960 | tf_op jit(solution)/shard_map/all_gather | solution.py:127
  344.2 489.4 %all-gather.28.cloned.1.call-start = ((), (), s32[]{:S(2)}) async-start(), calls=%async_computation.21 | async-start | bytes 9437184 | tf_op jit(solution)/shard_map/all_gather | solution.py:186
  493.9 382.9 %all-gather.30.cloned.1.call-start = ((), (), s32[]{:S(2)}) async-start(), calls=%async_computation.22 | async-start | bytes 7208960 | tf_op jit(solution)/shard_map/all_gather | solution.py:126
  494.7 600.6 %reduce-scatter.18.cloned.1.call-start = ((), (), s32[]{:S(2)}) async-start(), calls=%async_computation.27 | async-start | bytes 9437184 | tf_op jit(solution)/shard_map/reduce_scatter | solution.py:202
  946.1 300.7 %reduce-scatter.16.cloned.1.call-start = ((), (), s32[]{:S(2)}) async-start(), calls=%async_computation.25 | async-start | bytes 9437184 | tf_op jit(solution)/shard_map/reduce_scatter | solution.py:192
  972.9 401.3 %all-gather.38.cloned.1.call-start = ((), (), s32[]{:S(2)}) async-start(), calls=%async_computation.28 | async-start | bytes 9437184 | tf_op jit(solution)/shard_map/all_gather | solution.py:210
  1250.0 319.5 %reduce-scatter.22.cloned.1.call-start = ((), (), s32[]{:S(2)}) async-start(), calls=%async_computation.30 | async-start | bytes 1179648 | tf_op jit(solution)/shard_map/reduce_scatter | solution.py:241
  1468.9 128.0 %reduce-scatter.24.cloned.1.call-start = ((), (), s32[]{:S(2)}) async-start(), calls=%async_computation.31 | async-start | bytes 1179648 | tf_op jit(solution)/shard_map/reduce_scatter | solution.py:242
  1469.4 218.5 %reduce-scatter.20.cloned.1.call-start = ((), (), s32[]{:S(2)}) async-start(), calls=%async_computation.29 | async-start | bytes 4718592 | tf_op jit(solution)/shard_map/reduce_scatter | solution.py:240
  1491.6 253.3 %reduce-scatter.38.cloned.1.call-start = ((), (), s32[]{:S(2)}) async-start(), calls=%async_computation.38 | async-start | bytes 7208960 | tf_op jit(solution)/shard_map/reduce_scatter | solution.py:68
  1517.6 284.9 %reduce-scatter.36.cloned.1.call-start = ((), (), s32[]{:S(2)}) async-start(), calls=%async_computation.37 | async-start | bytes 7208960 | tf_op jit(solution)/shard_map/reduce_scatter | solution.py:67
  1543.7 316.2 %reduce-scatter.34.cloned.1.call-start = ((), (), s32[]{:S(2)}) async-start(), calls=%async_computation.36 | async-start | bytes 7208960 | tf_op jit(solution)/shard_map/reduce_scatter | solution.py:66
  1569.4 337.8 %reduce-scatter.28.cloned.1.call-start = ((), (), s32[]{:S(2)}) async-start(), calls=%async_computation.33 | async-start | bytes 5242880 | tf_op jit(solution)/shard_map/reduce_scatter | solution.py:63
  1603.0 378.4 %reduce-scatter.26.cloned.1.call-start = ((), (), s32[]{:S(2)}) async-start(), calls=%async_computation.32 | async-start | bytes 10485760 | tf_op jit(solution)/shard_map/reduce_scatter | solution.py:62
  1700.3 315.9 %reduce-scatter.30.cloned.1.call-start = ((), (), s32[]{:S(2)}) async-start(), calls=%async_computation.34 | async-start | bytes 2621440 | tf_op jit(solution)/shard_map/reduce_scatter | solution.py:64
  1717.4 345.7 %reduce-scatter.32.cloned.1.call-start = ((), (), s32[]{:S(2)}) async-start(), calls=%async_computation.35 | async-start | bytes 5242880 | tf_op jit(solution)/shard_map/reduce_scatter | solution.py:65
  1734.9 462.3 %all-reduce.3.cloned.1.call-start = ((), (), s32[]{:S(2)}) async-start(), calls=%async_computation.39 | async-start | bytes 6291456 | tf_op jit(solution)/shard_map/psum | solution.py:57
  (74 other events, 2612.9 us)
Sparse Core Ops, SparseCore 0:
  9.6 60.9 all-gather.13
  72.2 34.4 all-gather.19
  133.5 73.3 all-gather.15
  209.5 38.4 all-gather.21
  250.5 38.8 all-gather.23
  342.3 149.0 reduce-scatter.13
  493.0 42.4 all-gather.33
  537.6 124.9 all-gather.35
  664.2 41.5 all-gather.31
  708.6 124.9 all-gather.27
  835.2 41.5 all-gather.29
  946.2 149.0 reduce-scatter.17
  1098.8 147.9 reduce-scatter.15
  1250.1 123.9 all-gather.37
  1469.0 61.5 reduce-scatter.21
  1534.4 62.4 reduce-scatter.23
  1600.9 86.9 reduce-scatter.19
  1690.3 54.5 reduce-scatter.37
  1747.6 54.8 reduce-scatter.35
  1805.1 54.8 reduce-scatter.33
  1862.7 44.5 reduce-scatter.27
  1909.7 71.7 reduce-scatter.25
  2018.5 44.4 reduce-scatter.31
  2067.0 130.0 all-reduce.2
  (3 shorter events, 87.1 us)
where the time goes:
time: 2290 us; the launch traced here: 2280 us
  waiting for transfers between devices  1600 us (70%)
  matrix products  442 us (19%)
  other arithmetic  94.3 us (4%)
  blocking collectives  88.3 us (4%)
  local copies, waits for them, and re-layouts  30.6 us (1%)
  between operations  25.6 us (1%)
    dot_general x21, matrix products, matmul_high(): jnp.dot(left, right, precision=HIGH, preferred_element_type=jnp.float32)  357 us
    reduce_scatter x1, waiting for transfers between devices, on_device(): lax.psum_scatter(matmul_high(activ, wide_lower), 'heads', scatter_dimensi...  150 us
    reduce_scatter x1, waiting for transfers between devices, on_device(): lax.psum_scatter(matmul_high(mixed_heads, wide_merge), 'heads', scatter_d...  147 us
    all_gather x1, waiting for transfers between devices, on_device(): hidden_all = lax.all_gather(hidden_two, 'heads', axis=0, tiled=True)  128 us
    all_gather x1, waiting for transfers between devices, on_device(): grad_all = lax.all_gather(output_grad, 'heads', axis=0, tiled=True)  127 us
    all_gather x1, waiting for transfers between devices, on_device(): middle_all = lax.all_gather(d_middle, 'heads', axis=0, tiled=True)  124 us
    reduce_scatter x1, waiting for transfers between devices, on_device(): lax.psum_scatter(matmul_high(d_gate_pre, wide_gate.T) + matmul_high(d_up_...  122 us
    reduce_scatter x1, waiting for transfers between devices, on_device(): lax.psum_scatter(d_latent_all, 'heads', scatter_dimension=0, tiled=True)  84.8 us
  transfers between devices with their start and end apart: 27, of which 26 were waited for; matrix products, arithmetic and copies ran while one was open for 15% of the time, Pallas kernels for 0%

commit v1 on v0

--- a/solution.py
+++ b/solution.py
@@ -1,6 +1,10 @@
+import functools
+
 import jax
 import jax.numpy as jnp
 from jax import lax
+from jax.experimental import pallas as pl
+from jax.experimental.pallas import tpu as pltpu
 from jax.sharding import PartitionSpec as P
 
 STEP_COUNT = 10
@@ -13,7 +17,162 @@
 ADAM_EPS = 1e-06
 DECAY = 0.01
 RATE = 0.5
-HIGH = lax.Precision.HIGHEST
+HIGH = lax.Precision.HIGH
+MESH = pl.DeviceIdType.MESH
+RING_Z = 4
+
+
+def head_at(spot, n):
+    wide = n // RING_Z
+    back = (spot + n - RING_Z) // n
+    rest = jnp.maximum(spot - RING_Z, 0)
+    row, step = rest // (wide - 1), rest % (wide - 1)
+    odd = row % 2
+    column = (1 - odd) * (1 + step) + odd * (wide - 1 - step)
+    return (1 - back) * (spot * wide) + back * ((RING_Z - 1 - row) * wide + column)
+
+
+def spot_of(head, n):
+    wide = n // RING_Z
+    row = RING_Z - 1 - head // wide
+    column = head % wide
+    odd = row % 2
+    step = (1 - odd) * (column - 1) + odd * (wide - 1 - column)
+    back = (column + wide - 1) // wide
+    return (1 - back) * (head // wide) + back * (RING_Z + row * (wide - 1) + step)
+
+
+def ring_places(n):
+    me = lax.axis_index("heads")
+    spot = spot_of(me, n)
+    return me, lambda k: head_at(lax.rem(spot + k + 2 * n, n), n)
+
+
+def greet(right, left):
+    bar = pltpu.get_barrier_semaphore()
+    for other in (right, left):
+        pl.semaphore_signal(bar, inc=1, device_id={"heads": other}, device_id_type=MESH)
+    pl.semaphore_wait(bar, 2)
+
+
+def push(src, dst, send, recv, other):
+    copy = pltpu.make_async_remote_copy(
+        src_ref=src, dst_ref=dst, send_sem=send, recv_sem=recv, device_id={"heads": other}, device_id_type=MESH
+    )
+    copy.start()
+    return copy
+
+
+def gather_body(n, cuts, x_ref, o_ref, own_sem, send_sem, recv_sem):
+    me, at = ring_places(n)
+    sides = (at(1), at(-1))
+    greet(*sides)
+    rows = x_ref.shape[0]
+    half = rows // 2
+    piece = half // cuts
+    own = pltpu.make_async_copy(x_ref, o_ref.at[pl.ds(me * rows, rows)], own_sem)
+    own.start()
+    copies = {}
+    for step in range(n - 1):
+        for cut in range(cuts):
+            for way in (0, 1):
+                if step > 0:
+                    copies[way, step - 1, cut].wait_recv()
+                off = way * half + cut * piece
+                origin = at(-step) if way == 0 else at(step)
+                dst = o_ref.at[pl.ds(origin * rows + off, piece)]
+                src = x_ref.at[pl.ds(off, piece)] if step == 0 else dst
+                copies[way, step, cut] = push(
+                    src, dst, send_sem.at[way, step, cut], recv_sem.at[way, step, cut], sides[way]
+                )
+    for cut in range(cuts):
+        for way in (0, 1):
+            copies[way, n - 2, cut].wait_recv()
+    for copy in copies.values():
+        copy.wait_send()
+    own.wait()
+
+
+def cost(micros):
+    return pl.CostEstimate(flops=0, bytes_accessed=int(micros * 3.0e6), transcendentals=0)
+
+
+def ring_gather(x, n, number, cuts=2):
+    rows, columns = x.shape
+    cuts = min(cuts, rows // 16)
+    return pl.pallas_call(
+        functools.partial(gather_body, n, cuts),
+        out_shape=jax.ShapeDtypeStruct((n * rows, columns), x.dtype),
+        in_specs=[pl.BlockSpec(memory_space=pl.ANY)],
+        out_specs=pl.BlockSpec(memory_space=pl.ANY),
+        scratch_shapes=[
+            pltpu.SemaphoreType.DMA,
+            pltpu.SemaphoreType.DMA((2, n - 1, cuts)),
+            pltpu.SemaphoreType.DMA((2, n - 1, cuts)),
+        ],
+        compiler_params=pltpu.CompilerParams(collective_id=number, has_side_effects=True),
+        cost_estimate=cost(75.0 * columns / 2048),
+        name=f"ring_gather_{number}",
+    )(x)
+
+
+def scatter_body(n, cuts, x_ref, o_ref, held, send_sem, recv_sem):
+    me, at = ring_places(n)
+    sides = (at(1), at(-1))
+    greet(*sides)
+    rows = o_ref.shape[0]
+    half = rows // 2
+    piece = half // cuts
+    copies = {}
+    for step in range(n - 1):
+        for cut in range(cuts):
+            for way in (0, 1):
+                owner = at(-1 - step) if way == 0 else at(1 + step)
+                part = x_ref.at[pl.ds(pl.multiple_of(owner * rows + way * half + cut * piece, piece), piece)]
+                here = pl.ds(cut * piece, piece)
+                src = part
+                if step > 0:
+                    copies[way, step - 1, cut].wait_recv()
+                    src = held.at[way, step - 1, here]
+                    src[...] += part[...]
+                copies[way, step, cut] = push(
+                    src,
+                    held.at[way, step, here],
+                    send_sem.at[way, step, cut],
+                    recv_sem.at[way, step, cut],
+                    sides[way],
+                )
+    for cut in range(cuts):
+        for way in (0, 1):
+            copies[way, n - 2, cut].wait_recv()
+            off = way * half + cut * piece
+            o_ref[pl.ds(off, piece)] = (
+                x_ref[pl.ds(pl.multiple_of(me * rows + off, piece), piece)]
+                + held[way, n - 2, pl.ds(cut * piece, piece)]
+            )
+    for copy in copies.values():
+        copy.wait_send()
+
+
+def ring_scatter(x, n, number, cuts=4):
+    rows, columns = x.shape[0] // n, x.shape[1]
+    cuts = min(cuts, rows // 16)
+    return pl.pallas_call(
+        functools.partial(scatter_body, n, cuts),
+        out_shape=jax.ShapeDtypeStruct((rows, columns), x.dtype),
+        in_specs=[pl.BlockSpec(memory_space=pltpu.VMEM)],
+        out_specs=pl.BlockSpec(memory_space=pltpu.VMEM),
+        scratch_shapes=[
+            pltpu.VMEM((2, n - 1, rows // 2, columns), x.dtype),
+            pltpu.SemaphoreType.DMA((2, n - 1, cuts)),
+            pltpu.SemaphoreType.DMA((2, n - 1, cuts)),
+        ],
+        compiler_params=pltpu.CompilerParams(
+            collective_id=number, has_side_effects=True, vmem_limit_bytes=40 << 20
+        ),
+        cost_estimate=cost(75.0 * columns / 2048),
+        name=f"ring_scatter_{number}",
+    )(x)
 
 
 def matmul_high(left, right):
@@ -21,7 +180,8 @@
 
 
 def layout(lengths_row, row_index):
-    doc_ends = jnp.cumsum(lengths_row)
+    upto = jnp.arange(lengths_row.shape[0], dtype=jnp.int32)
+    doc_ends = jnp.sum(jnp.where(upto[None, :] <= upto[:, None], lengths_row[None, :], 0), axis=1)
     doc_starts = doc_ends - lengths_row
     segment = jnp.sum((row_index[:, None] >= doc_ends[None, :]).astype(jnp.int32), axis=1)
     doc_ids = jnp.arange(doc_ends.shape[0], dtype=jnp.int32)
@@ -51,10 +211,6 @@
         inverse * (scaled - normed * jnp.mean(scaled * normed, axis=1, keepdims=True)),
         jnp.sum(upstream * normed, axis=0),
     )
-
-
-def share_grads(part_down, part_pair, part_gains):
-    return lax.psum((part_down, part_pair, part_gains), "heads")
 
 
 def spread_grads(part_down, part_pair, part_up, part_merge, part_gate, part_upper, part_lower):
@@ -127,6 +283,7 @@
         lax.all_gather(up_weight, "dp", axis=0, tiled=True),
         lax.all_gather(down_weight, "dp", axis=1, tiled=True),
     )
+    grad_all = ring_gather(output_grad, heads_count, 5)
     group_index = jnp.arange(group_rows, dtype=jnp.int32)
     segment, position = layout(lengths[0], group_index)
     local_position = lax.dynamic_slice_in_dim(
@@ -145,11 +302,12 @@
     pair_local = matmul_high(hidden_one, wide_pair)
     key_local = rotate(pair_local[:, :head_dim], local_position, 1.0)
     value_local = pair_local[:, head_dim:]
-    latent_all, key_all, value_all = (
-        lax.all_gather(latent, "heads", axis=0, tiled=True),
-        lax.all_gather(key_local, "heads", axis=0, tiled=True),
-        lax.all_gather(value_local, "heads", axis=0, tiled=True),
-    )
+    packed_all = ring_gather(
+        jnp.concatenate([latent, key_local, value_local], axis=1), heads_count, 1
+    )
+    latent_all = packed_all[:, :latent_dim]
+    key_all = packed_all[:, latent_dim : latent_dim + head_dim]
+    value_all = packed_all[:, latent_dim + head_dim :]
     query_rot = rotate(
         matmul_high(latent_all, wide_up).reshape(group_rows, local_heads, head_dim), position, 1.0
     )
@@ -177,37 +335,29 @@
 
     mixed_blocks, lse_blocks = lax.map(forward_block, (query_blocks, index_blocks, segment_blocks))
     mixed_heads = mixed_blocks.reshape(group_rows, local_heads * head_dim)
-    middle = block_input + lax.psum_scatter(
-        matmul_high(mixed_heads, wide_merge), "heads", scatter_dimension=0, tiled=True
-    )
+    middle = block_input + ring_scatter(matmul_high(mixed_heads, wide_merge), heads_count, 2)
     inv_two = lax.rsqrt(jnp.mean(middle * middle, axis=1, keepdims=True) + EPS_NORM)
     normed_two = middle * inv_two
     hidden_two = normed_two * gain_ffn
-    hidden_all = lax.all_gather(hidden_two, "heads", axis=0, tiled=True)
+    hidden_all = ring_gather(hidden_two, heads_count, 3)
     gate_pre = matmul_high(hidden_all, wide_gate)
     up_pre = matmul_high(hidden_all, wide_upper)
     sig_gate = jax.nn.sigmoid(gate_pre)
     silu_gate = gate_pre * sig_gate
     activ = silu_gate * up_pre
-    block_output = middle + lax.psum_scatter(
-        matmul_high(activ, wide_lower), "heads", scatter_dimension=0, tiled=True
-    )
-    grad_all = lax.all_gather(output_grad, "heads", axis=0, tiled=True)
+    block_output = middle + ring_scatter(matmul_high(activ, wide_lower), heads_count, 4)
     d_activ = matmul_high(grad_all, wide_lower.T)
     grad_lower = matmul_high(activ.T, grad_all)
     d_gate_pre = d_activ * up_pre * (sig_gate * (1.0 + gate_pre * (1.0 - sig_gate)))
     d_up_pre = d_activ * silu_gate
     grad_gate = matmul_high(hidden_all.T, d_gate_pre)
     grad_upper = matmul_high(hidden_all.T, d_up_pre)
-    d_hidden_two = lax.psum_scatter(
-        matmul_high(d_gate_pre, wide_gate.T) + matmul_high(d_up_pre, wide_upper.T),
-        "heads",
-        scatter_dimension=0,
-        tiled=True,
+    d_hidden_two = ring_scatter(
+        matmul_high(d_gate_pre, wide_gate.T) + matmul_high(d_up_pre, wide_upper.T), heads_count, 6
     )
     d_normed_mid, grad_gain_ffn = norm_back(d_hidden_two, normed_two, inv_two, gain_ffn)
     d_middle = output_grad + d_normed_mid
-    middle_all = lax.all_gather(d_middle, "heads", axis=0, tiled=True)
+    middle_all = ring_gather(d_middle, heads_count, 7)
     grad_merge = matmul_high(mixed_heads.T, middle_all)
     d_mixed = matmul_high(middle_all, wide_merge.T).reshape(
         n_blocks, block_rows, local_heads, head_dim
@@ -236,11 +386,12 @@
     ).reshape(group_rows, local_heads * head_dim)
     grad_up = matmul_high(latent_all.T, d_query_pre)
     d_latent_all = matmul_high(d_query_pre, wide_up.T)
-    d_latent, d_key_local, d_value_local = (
-        lax.psum_scatter(d_latent_all, "heads", scatter_dimension=0, tiled=True),
-        lax.psum_scatter(d_key_sum, "heads", scatter_dimension=0, tiled=True),
-        lax.psum_scatter(d_value_sum, "heads", scatter_dimension=0, tiled=True),
-    )
+    packed_grad = ring_scatter(
+        jnp.concatenate([d_latent_all, d_key_sum, d_value_sum], axis=1), heads_count, 8
+    )
+    d_latent = packed_grad[:, :latent_dim]
+    d_key_local = packed_grad[:, latent_dim : latent_dim + head_dim]
+    d_value_local = packed_grad[:, latent_dim + head_dim :]
     d_pair = jnp.concatenate([rotate(d_key_local, local_position, -1.0), d_value_local], axis=1)
     d_latent_raw, grad_gain_query = norm_back(d_latent, latent_hat, inv_query, gain_query)
     grad_down = matmul_high(hidden_one.T, d_latent_raw)
@@ -252,9 +403,11 @@
     spread = spread_grads(
         grad_down, grad_pair, grad_up, grad_merge, grad_gate, grad_upper, grad_lower
     )
-    shared = share_grads(spread[0], spread[1], grad_gains)
-    reduced = (shared[0], shared[1]) + tuple(spread[2:])
-    gains_total = lax.psum(shared[2], "dp")
+    shared = ring_gather(
+        ring_scatter(jnp.concatenate([spread[0], spread[1]], axis=1), heads_count, 9), heads_count, 10
+    )
+    reduced = (shared[:, :latent_dim], shared[:, latent_dim:]) + tuple(spread[2:])
+    gains_total = lax.psum(grad_gains, ("dp", "heads"))
     values = (
         norm_gains,
         query_down,

time: 2290 us -> 1390 us (0.61)
  waiting for transfers between devices: 1600 us -> 211 us
  Pallas kernels: 0 us -> 679 us
  matrix products: 442 us -> 290 us
  blocking collectives: 88.3 us -> 39.7 us
    pallas_call x0 -> x10, Pallas kernels: none -> 679 us  [the longest x5 342 us: ring_gather(): pl.pallas_call(functools.partial(gather_body, n, cuts), out_shape=jax.Sha...]
    reduce_scatter x6 -> x0, waiting for transfers between devices: 530 us -> none  [the longest x1 150 us: on_device(): lax.psum_scatter(matmul_high(activ, wide_lower), 'heads', scatter_dimensi...]
    all_gather x6 -> x0, waiting for transfers between devices: 521 us -> none  [the longest x1 128 us: on_device(): hidden_all = lax.all_gather(hidden_two, 'heads', axis=0, tiled=True)]
    dot_general x21, matrix products: 357 us -> 225 us  [matmul_high(): jnp.dot(left, right, precision=HIGH, preferred_element_type=jnp.float32)]
    psum x1 -> x0, waiting for transfers between devices: 55.9 us -> none  [share_grads(): return lax.psum((part_down, part_pair, part_gains), 'heads')]
    psum x3 -> x1, blocking collectives: 88.3 us -> 39.7 us  [on_device(): gains_total = lax.psum(grad_gains, ('dp', 'heads'))]
    reduce_scatter x1, waiting for transfers between devices: 42.1 us -> 0.01 us  [spread_grads(): lax.psum_scatter(part_merge, 'dp', scatter_dimension=1, tiled=True)]
    all_gather x1, waiting for transfers between devices: 40.7 us -> 0.02 us  [on_device(): lax.all_gather(down_weight, 'dp', axis=1, tiled=True)]
  transfers between devices with their start and end apart: 27 -> 14, of which waited for: 26 -> 5; matrix products, arithmetic and copies ran while one was open for 15% -> 17% of each run, Pallas kernels for 0% -> 27%
where the time goes in v1:
time: 1390 us; the launch traced here: 1380 us
  Pallas kernels  679 us (49%)
  matrix products  290 us (21%)
  waiting for transfers between devices  211 us (15%)
  other arithmetic  90.9 us (7%)
  local copies, waits for them, and re-layouts  41.8 us (3%)
  blocking collectives  39.7 us (3%)
  between operations  25.6 us (2%)
    pallas_call x5, Pallas kernels, ring_gather(): pl.pallas_call(functools.partial(gather_body, n, cuts), out_shape=jax.Sha...  342 us
    pallas_call x5, Pallas kernels, ring_scatter(): pl.pallas_call(functools.partial(scatter_body, n, cuts), out_shape=jax.Sh...  337 us
    dot_general x21, matrix products, matmul_high(): jnp.dot(left, right, precision=HIGH, preferred_element_type=jnp.float32)  225 us
    reduce_scatter x1, waiting for transfers between devices, spread_grads(): lax.psum_scatter(part_down, 'dp', scatter_dimension=0, tiled=True)  74.2 us
    reduce_scatter x1, waiting for transfers between devices, spread_grads(): lax.psum_scatter(part_gate, 'dp', scatter_dimension=0, tiled=True)  49.1 us
    reduce_sum x7, other arithmetic, on_device(): jnp.sum(stepped[slot][2] * stepped[slot][2])  39.7 us
    psum x1, blocking collectives, on_device(): gains_total = lax.psum(grad_gains, ('dp', 'heads'))  39.7 us
    reduce_scatter x1, waiting for transfers between devices, spread_grads(): lax.psum_scatter(part_pair, 'dp', scatter_dimension=0, tiled=True)  38.5 us
  transfers between devices with their start and end apart: 14, of which 5 were waited for; matrix products, arithmetic and copies ran while one was open for 17% of the time, Pallas kernels for 27%

profile of v1, /device:TPU:0, one launch (start us, length us, event | category | flops | bytes accessed | tf_op | source)
XLA Modules:
  0.0 1379.6 jit_solution(5013283933251563610)
XLA Ops:
  12.7 84.6 %ring_gather_5.1 = f32[1024,2048]{1,0:T(8,128)} custom-call(f32[128,2048]{1,0:T(8,128)} %x_ref.1), custom_call_target="tpu_custom_call" | custom-call | bytes 225000000 | tf_op jit(solution)/shard_map/ring_gather_5/pallas_call | solution.py:103
  105.0 14.6 %fusion.140 = f32[1024,704]{0,1:T(8,128)} fusion(f32[1024,2048]{1,0:T(8,128)} %ring_gather_5.1, f32[704,2048]{1,0:T(8,128)} %all-gather.20.cloned.1.call-done), kind=kOutput, calls=%fused_computation.244 | convolution fusion | flops 8858370048 | bytes 17039360 | tf_op jit(solution)/shard_map/dot_general | solution.py:179
  119.6 32.1 %all-gather.8.cloned.1.call-done = f32[2048,1024]{1,0:T(8,128)} async-done(((f32[512,1024]{1,0:T(8,128)}), f32[2048,1024]{1,0:T(8,128)}) %all-gather.8.cloned.1.call-update) | async-done | bytes 8388624 | tf_op jit(solution)/shard_map/all_gather | solution.py:278
  159.7 63.7 %ring_gather_1.1 = f32[1024,1536]{1,0:T(8,128)} custom-call(f32[128,1536]{1,0:T(8,128)} %pad_maximum_fusion.4.x_ref), custom_call_target="tpu_custom_call" | custom-call | bytes 168750000 | tf_op jit(solution)/shard_map/ring_gather_1/pallas_call | solution.py:103
  241.2 21.1 %while.28 = (s32[]{:T(128)}, f32[2,512,2,256]{3,1,2,0:T(8,128)}, f32[2,2,512]{2,1,0:T(2,128)S(1)}, s32[2,512]{1,0:T(2,128)S(1)}, s32[1024]{0:T(1024)S(1)}, /*ind...) while((s32[]{:T(128)}, f32[2,512,2,256]{3,1,2,0:T(8,128)}, ...), condition=%wide.region_8.9_spmd.clone, body=%wide.region_5.8_spmd.clone.sunk | while | flops 3234331648 | bytes 18924652 | solution.py:336
  277.1 83.4 %ring_scatter_2.1 = f32[128,2048]{1,0:T(8,128)S(1)} custom-call(f32[1024,2048]{1,0:T(8,128)S(1)} %fusion.137.x_ref), custom_call_target="tpu_custom_call" | custom-call | bytes 225000000 | tf_op jit(solution)/shard_map/ring_scatter_2/pallas_call | solution.py:160
  361.8 81.0 %ring_gather_3.1 = f32[1024,2048]{1,0:T(8,128)} custom-call(f32[128,2048]{1,0:T(8,128)} %multiply_multiply_fusion.7.x_ref), custom_call_target="tpu_custom_call" | custom-call | bytes 225000000 | tf_op jit(solution)/shard_map/ring_gather_3/pallas_call | solution.py:103
  442.8 14.4 %fusion.139 = f32[1024,704]{0,1:T(8,128)} fusion(f32[1024,2048]{1,0:T(8,128)} %ring_gather_3.1, f32[2048,704]{0,1:T(8,128)} %all-gather.18.cloned.1.call-done), kind=kOutput, calls=%fused_computation.243 | convolution fusion | flops 8858370048 | bytes 17039360 | tf_op jit(solution)/shard_map/dot_general | solution.py:179
  485.4 80.1 %ring_scatter_4.1 = f32[128,2048]{1,0:T(8,128)S(1)} custom-call(f32[1024,2048]{1,0:T(8,128)S(1)} %fusion.75.x_ref), custom_call_target="tpu_custom_call" | custom-call | bytes 225000000 | tf_op jit(solution)/shard_map/ring_scatter_4/pallas_call | solution.py:160
  565.6 17.7 %fusion.120 = f32[1024,2048]{1,0:T(8,128)} fusion(f32[2048,704]{0,1:T(8,128)} %all-gather.16.cloned.1.call-done, f32[1024,704]{0,1:T(8,128)} %copy-done.57, f32[1024,704]{0,1:T(8,128)S(1)} %copy-done.55, f32[1024,704]{0,1:T(8,128)} %fusion.139), kind=kOutput, calls=%fused_computation.236 | convolution fusion | flops 8864858112 | bytes 22806528 | tf_op jit(solution)/shard_map/dot_general | solution.py:179
  583.3 15.0 %convolution_add_fusion.x_ref = f32[1024,2048]{1,0:T(8,128)S(1)} fusion(f32[1024,2048]{1,0:T(8,128)} %fusion.120, f32[2048,704]{0,1:T(8,128)S(1)} %bitcast.251, f32[1024,704]{0,1:T(8,128)S(1)} %copy-done.55, f32[1024,704]{0,1:T(8,128)} %copy-done.57), kind=kOutput, calls=%fused_computation.72 | convolution fusion | flops 8864071680 | bytes 28311552 | tf_op jit(solution)/shard_map/dot_general | solution.py:179
  598.4 79.2 %ring_scatter_6.1 = f32[128,2048]{1,0:T(8,128)S(1)} custom-call(f32[1024,2048]{1,0:T(8,128)S(1)} %convolution_add_fusion.x_ref), custom_call_target="tpu_custom_call" | custom-call | bytes 225000000 | tf_op jit(solution)/shard_map/ring_scatter_6/pallas_call | solution.py:160
  679.6 78.0 %ring_gather_7.1 = f32[1024,2048]{1,0:T(8,128)} custom-call(f32[128,2048]{1,0:T(8,128)} %get-tuple-element.510.x_ref), custom_call_target="tpu_custom_call" | custom-call | bytes 225000000 | tf_op jit(solution)/shard_map/ring_gather_7/pallas_call | solution.py:103
  772.6 59.4 %while.29 = (s32[]{:T(128)}, f32[1024,256]{1,0:T(8,128)}, f32[1024,256]{1,0:T(8,128)}, f32[2,512,2,256]{3,1,0,2:T(8,128)}, s32[2,512]{1,0:T(2,128)S(1)}, /*index...) while((s32[]{:T(128)}, f32[1024,256]{1,0:T(8,128)}, ...), condition=%wide.region_13.14_spmd.clone, body=%wide.region_11.13_spmd.clone.sunk | while | flops 8065121280 | bytes 93890296 | solution.py:379
  859.4 14.8 %fusion.73 = f32[704,2048]{1,0:T(8,128)} fusion(f32[1024,2048]{1,0:T(8,128)} %ring_gather_5.1, f32[1024,704]{0,1:T(8,128)} %fusion.139, f32[1024,704]{0,1:T(8,128)S(1)} %copy-done.58), kind=kOutput, calls=%fused_computation.110 | convolution fusion | flops 8861974528 | bytes 19922944 | tf_op jit(solution)/shard_map/dot_general | solution.py:179
  876.0 14.4 %fusion.70 = f32[2048,704]{0,1:T(8,128)} fusion(f32[1024,2048]{1,0:T(8,128)} %ring_gather_3.1, f32[1024,704]{0,1:T(8,128)S(1)} %copy-done.56, f32[1024,704]{0,1:T(8,128)} %copy-done.57), kind=kOutput, calls=%fused_computation.107 | convolution fusion | flops 8861974528 | bytes 19922944 | tf_op jit(solution)/shard_map/dot_general | solution.py:179
  890.5 15.7 %fusion.119 = f32[2048,704]{0,1:T(8,128)} fusion(f32[1024,2048]{1,0:T(8,128)} %ring_gather_3.1, f32[1024,704]{0,1:T(8,128)} %copy-done.57, f32[1024,704]{0,1:T(8,128)S(1)} %copy-done.56, f32[1024,704]{0,1:T(8,128)} %fusion.139), kind=kOutput, calls=%fused_computation.235 | convolution fusion | flops 8864858112 | bytes 22806528 | tf_op jit(solution)/shard_map/dot_general | solution.py:179
  921.5 59.5 %ring_scatter_8.1 = f32[128,1536]{1,0:T(8,128)S(1)} custom-call(f32[1024,1536]{1,0:T(8,128)S(1)} %pad_maximum_fusion.x_ref), custom_call_target="tpu_custom_call" | custom-call | bytes 168750000 | tf_op jit(solution)/shard_map/ring_scatter_8/pallas_call | solution.py:160
  1047.3 49.1 %reduce-scatter.16.cloned.1.call-done = f32[512,704]{0,1:T(8,128)} async-done(((f32[2048,704]{0,1:T(8,128)}), f32[512,704]{0,1:T(8,128)}) %reduce-scatter.16.cloned.1.call-update) | async-done | bytes 1441808 | tf_op jit(solution)/shard_map/reduce_scatter | solution.py:222
  1105.2 38.5 %reduce-scatter.10.cloned.1.call-done = f32[512,512]{1,0:T(8,128)} async-done(((f32[2048,512]{1,0:T(8,128)}), f32[512,512]{1,0:T(8,128)}) %reduce-scatter.10.cloned.1.call-update) | async-done | bytes 1048592 | tf_op jit(solution)/shard_map/reduce_scatter | solution.py:219
  1143.7 74.2 %reduce-scatter.8.cloned.1.call-done = f32[512,1024]{1,0:T(8,128)} async-done(((f32[2048,1024]{1,0:T(8,128)}), f32[512,1024]{1,0:T(8,128)}) %reduce-scatter.8.cloned.1.call-update) | async-done | bytes 2097168 | tf_op jit(solution)/shard_map/reduce_scatter | solution.py:218
  1220.1 34.5 %ring_scatter_9.1.x_ref = f32[64,1536]{1,0:T(8,128)S(1)} custom-call(f32[512,1536]{1,0:T(8,128)S(1)} %pad_maximum_fusion.1.x_ref), custom_call_target="tpu_custom_call" | custom-call | bytes 168750000 | tf_op jit(solution)/shard_map/ring_scatter_9/pallas_call | solution.py:160
  1255.4 35.2 %ring_gather_10.1 = f32[512,1536]{1,0:T(8,128)} custom-call(f32[64,1536]{1,0:T(8,128)} %copy-done), custom_call_target="tpu_custom_call" | custom-call | bytes 168750000 | tf_op jit(solution)/shard_map/ring_gather_10/pallas_call | solution.py:103
  1306.1 39.7 %all-reduce = (f32[5120]{0:T(1024)}, f32[7,2]{0,1:T(2,128)S(1)}) all-reduce(f32[5120]{0:T(1024)} %pad_maximum_fusion.8, f32[7,2]{0,1:T(2,128)S(1)} %stack.121), channel_id=1, replica_groups=mesh['dp'=4,'heads'=8] {'dp','heads'}, use_global_device_ids=true, to_apply=%region_19.20 | all-reduce | flops 5134 | bytes 41072 | tf_op jit(solution)/shard_map/psum | solution.py:410
  (300 shorter events, 333.8 us)
Async XLA Ops:
  7.2 93.1 %all-gather.10.cloned.1.call-start = ((), (), s32[]{:S(2)}) async-start(), calls=%async_computation.8 | async-start | bytes 5242880 | tf_op jit(solution)/shard_map/all_gather | solution.py:279
  7.9 97.0 %all-gather.20.cloned.1.call-start = ((), (), s32[]{:S(2)}) async-start(), calls=%async_computation.13 | async-start | bytes 7208960 | tf_op jit(solution)/shard_map/all_gather | solution.py:284
  8.7 143.0 %all-gather.8.cloned.1.call-start = ((), (), s32[]{:S(2)}) async-start(), calls=%async_computation.7 | async-start | bytes 10485760 | tf_op jit(solution)/shard_map/all_gather | solution.py:278
  9.5 213.9 %all-gather.12.cloned.1.call-start = ((), (), s32[]{:S(2)}) async-start(), calls=%async_computation.9 | async-start | bytes 2621440 | tf_op jit(solution)/shard_map/all_gather | solution.py:280
  10.0 256.9 %all-gather.14.cloned.1.call-start = ((), (), s32[]{:S(2)}) async-start(), calls=%async_computation.10 | async-start | bytes 5242880 | tf_op jit(solution)/shard_map/all_gather | solution.py:281
  10.6 432.1 %all-gather.18.cloned.1.call-start = ((), (), s32[]{:S(2)}) async-start(), calls=%async_computation.12 | async-start | bytes 7208960 | tf_op jit(solution)/shard_map/all_gather | solution.py:283
  11.2 446.0 %all-gather.16.cloned.1.call-start = ((), (), s32[]{:S(2)}) async-start(), calls=%async_computation.11 | async-start | bytes 7208960 | tf_op jit(solution)/shard_map/all_gather | solution.py:282
  11.9 994.4 %reduce-scatter.12.cloned.1.call-start = ((), (), s32[]{:S(2)}) async-start(), calls=%async_computation.16 | async-start | bytes 2621440 | tf_op jit(solution)/shard_map/reduce_scatter | solution.py:220
  12.0 139.7 %copy-start.36 = (f32[2048]{0:T(1024)}, f32[2048]{0:T(1024)S(1)}, u32[]{:S(2)}) copy-start(f32[2048]{0:T(1024)S(1)} %get-tuple-element.520) | copy-start | bytes 24580
  12.0 145.8 %copy-start.42 = (f32[1024]{0:T(1024)}, f32[1024]{0:T(1024)S(1)}, u32[]{:S(2)}) copy-start(f32[1024]{0:T(1024)S(1)} %slice.112) | copy-start | bytes 12292
  12.3 92.3 %copy-start.50 = (f32[128]{0:T(128)}, f32[128]{0:T(128)S(1)}, u32[]{:S(2)}) copy-start(f32[128]{0:T(128)S(1)} %multiply_power_fusion) | copy-start | bytes 1540
  12.5 139.2 %copy-start.46 = (f32[128]{0:T(128)}, f32[128]{0:T(128)S(1)}, u32[]{:S(2)}) copy-start(f32[128]{0:T(128)S(1)} %add_rsqrt_fusion.2) | copy-start | bytes 1540
  100.3 135.2 %copy-start.25 = (f32[1024,128]{1,0:T(8,128)}, f32[1024,128]{1,0:T(8,128)S(1)}, u32[]{:S(2)}) copy-start(f32[1024,128]{1,0:T(8,128)S(1)} %get-tuple-element.523) | copy-start | bytes 1572868
  157.8 65.5 %copy-start.48 = (f32[128]{0:T(128)}, f32[128]{0:T(128)S(1)}, u32[]{:S(2)}) copy-start(f32[128]{0:T(128)S(1)} %add_rsqrt_fusion.1) | copy-start | bytes 1540
  485.4 80.2 %copy-start.55 = (f32[1024,704]{0,1:T(8,128)S(1)}, f32[1024,704]{0,1:T(8,128)}, u32[]{:S(2)}) copy-start(f32[1024,704]{0,1:T(8,128)} %fusion.140) | copy-start | bytes 8650756
  485.4 97.9 %slice-start.1 = ((s8[5767168]{0:T(1024)(128)(4,1)}), s8[4194304]{0:T(1024)(128)(4,1)S(1)}, s32[]{:S(2)}) async-start(s8[5767168]{0:T(1024)(128)(4,1)} %bitcast.250), calls=%async_computation.22 | async-start | bytes 8388608
  598.4 79.6 %copy-start.29 = (f32[128,2048]{1,0:T(8,128)S(1)}, f32[128,2048]{1,0:T(8,128)}, u32[]{:S(2)}) copy-start(f32[128,2048]{1,0:T(8,128)} %x_ref.1) | copy-start | bytes 3145732
  846.8 164.3 %reduce-scatter.14.cloned.1.call-start = ((), (), s32[]{:S(2)}) async-start(), calls=%async_computation.17 | async-start | bytes 5242880 | tf_op jit(solution)/shard_map/reduce_scatter | solution.py:221
  857.6 160.7 %reduce-scatter.20.cloned.1.call-start = ((), (), s32[]{:S(2)}) async-start(), calls=%async_computation.20 | async-start | bytes 7208960 | tf_op jit(solution)/shard_map/reduce_scatter | solution.py:224
  874.2 165.0 %reduce-scatter.18.cloned.1.call-start = ((), (), s32[]{:S(2)}) async-start(), calls=%async_computation.19 | async-start | bytes 7208960 | tf_op jit(solution)/shard_map/reduce_scatter | solution.py:223
  890.5 206.0 %reduce-scatter.16.cloned.1.call-start = ((), (), s32[]{:S(2)}) async-start(), calls=%async_computation.18 | async-start | bytes 7208960 | tf_op jit(solution)/shard_map/reduce_scatter | solution.py:222
  906.3 237.4 %reduce-scatter.10.cloned.1.call-start = ((), (), s32[]{:S(2)}) async-start(), calls=%async_computation.15 | async-start | bytes 5242880 | tf_op jit(solution)/shard_map/reduce_scatter | solution.py:219
  985.4 232.5 %reduce-scatter.8.cloned.1.call-start = ((), (), s32[]{:S(2)}) async-start(), calls=%async_computation.14 | async-start | bytes 10485760 | tf_op jit(solution)/shard_map/reduce_scatter | solution.py:218
  1220.1 70.5 %copy-start.8 = (f32[512,1024]{1,0:T(8,128)S(1)}, f32[512,1024]{1,0:T(8,128)}, u32[]{:S(2)}) copy-start(f32[512,1024]{1,0:T(8,128)} %param.37) | copy-start | bytes 6291460
  (56 other events, 635.9 us)
Sparse Core Ops, SparseCore 0:
  9.6 37.1 all-gather.9
  48.4 43.3 all-gather.19
  93.4 58.2 all-gather.7
  153.1 22.5 all-gather.11
  177.2 34.4 all-gather.13
  213.1 43.4 all-gather.17
  258.1 43.3 all-gather.15
  847.0 30.0 reduce-scatter.11
  879.7 44.4 reduce-scatter.13
  926.6 54.8 reduce-scatter.19
  984.2 54.9 reduce-scatter.17
  1041.6 54.7 reduce-scatter.15
  1099.1 44.5 reduce-scatter.9
  1146.1 71.7 reduce-scatter.7

commit v2 on v1

--- a/solution.py
+++ b/solution.py
@@ -48,53 +48,171 @@
     return me, lambda k: head_at(lax.rem(spot + k + 2 * n, n), n)
 
 
-def greet(right, left):
+def others(axis):
+    count = lax.axis_size(axis)
+    me = lax.axis_index(axis)
+    return [lax.rem(me + k, count) for k in range(1, count)]
+
+
+def greet(names):
     bar = pltpu.get_barrier_semaphore()
-    for other in (right, left):
-        pl.semaphore_signal(bar, inc=1, device_id={"heads": other}, device_id_type=MESH)
-    pl.semaphore_wait(bar, 2)
-
-
-def push(src, dst, send, recv, other):
+    for name in names:
+        pl.semaphore_signal(bar, inc=1, device_id=name, device_id_type=MESH)
+    pl.semaphore_wait(bar, len(names))
+
+
+def push(src, dst, send, recv, name):
     copy = pltpu.make_async_remote_copy(
-        src_ref=src, dst_ref=dst, send_sem=send, recv_sem=recv, device_id={"heads": other}, device_id_type=MESH
+        src_ref=src, dst_ref=dst, send_sem=send, recv_sem=recv, device_id=name, device_id_type=MESH
     )
     copy.start()
     return copy
 
 
-def gather_body(n, cuts, x_ref, o_ref, own_sem, send_sem, recv_sem):
-    me, at = ring_places(n)
-    sides = (at(1), at(-1))
-    greet(*sides)
-    rows = x_ref.shape[0]
-    half = rows // 2
-    piece = half // cuts
-    own = pltpu.make_async_copy(x_ref, o_ref.at[pl.ds(me * rows, rows)], own_sem)
-    own.start()
-    copies = {}
-    for step in range(n - 1):
-        for cut in range(cuts):
+class Ring:
+    def __init__(self, n, cuts, x_ref, o_ref, sems):
+        self.n, self.cuts, self.x, self.o = n, cuts, x_ref, o_ref
+        self.own_sem, self.send_sem, self.recv_sem = sems
+        self.me, self.at = ring_places(n)
+        self.sides = ({"heads": self.at(1)}, {"heads": self.at(-1)})
+        self.copies = {}
+
+    def begin(self):
+        rows = self.x.shape[0]
+        self.own = pltpu.make_async_copy(self.x, self.o.at[pl.ds(self.me * rows, rows)], self.own_sem)
+        self.own.start()
+
+    def step(self, step):
+        rows = self.x.shape[0]
+        half = rows // 2
+        piece = half // self.cuts
+        for cut in range(self.cuts):
             for way in (0, 1):
                 if step > 0:
-                    copies[way, step - 1, cut].wait_recv()
+                    self.copies[way, step - 1, cut].wait_recv()
                 off = way * half + cut * piece
-                origin = at(-step) if way == 0 else at(step)
-                dst = o_ref.at[pl.ds(origin * rows + off, piece)]
-                src = x_ref.at[pl.ds(off, piece)] if step == 0 else dst
-                copies[way, step, cut] = push(
-                    src, dst, send_sem.at[way, step, cut], recv_sem.at[way, step, cut], sides[way]
+                origin = self.at(-step) if way == 0 else self.at(step)
+                dst = self.o.at[pl.ds(origin * rows + off, piece)]
+                src = self.x.at[pl.ds(off, piece)] if step == 0 else dst
+                self.copies[way, step, cut] = push(
+                    src, dst, self.send_sem.at[way, step, cut], self.recv_sem.at[way, step, cut], self.sides[way]
                 )
-    for cut in range(cuts):
-        for way in (0, 1):
-            copies[way, n - 2, cut].wait_recv()
-    for copy in copies.values():
-        copy.wait_send()
-    own.wait()
+
+    def end(self):
+        for cut in range(self.cuts):
+            for way in (0, 1):
+                self.copies[way, self.n - 2, cut].wait_recv()
+        for copy in self.copies.values():
+            copy.wait_send()
+        self.own.wait()
+
+    @staticmethod
+    def scratch(n, cuts):
+        return [
+            pltpu.SemaphoreType.DMA,
+            pltpu.SemaphoreType.DMA((2, n - 1, cuts)),
+            pltpu.SemaphoreType.DMA((2, n - 1, cuts)),
+        ]
+
+
+class Spread:
+    def __init__(self, dp, x_ref, o_ref, sems):
+        self.x, self.o, self.ny = x_ref, o_ref, dp // 2
+        self.own_sem, self.y_send, self.y_recv, self.core_send, self.core_recv = sems
+        me = lax.axis_index("dp")
+        self.y, self.core = me // 2, me % 2
+        self.me = me
+        self.mate = {"dp": self.y * 2 + 1 - self.core}
+        self.next = {"dp": lax.rem(self.y + 1, self.ny) * 2 + self.core}
+        self.rows = x_ref.shape[0]
+
+    def block(self, owner):
+        return self.o.at[pl.ds(owner * self.rows, self.rows)]
+
+    def begin(self):
+        self.own = pltpu.make_async_copy(self.x, self.block(self.me), self.own_sem)
+        self.own.start()
+        self.y_copies = [push(self.x, self.block(self.me), self.y_send.at[0], self.y_recv.at[0], self.next)]
+        self.core_copies = [push(self.x, self.block(self.me), self.core_send.at[0], self.core_recv.at[0], self.mate)]
+
+    def end(self):
+        for k in range(1, self.ny):
+            self.y_copies[k - 1].wait_recv()
+            held = self.block(lax.rem(self.y - k + self.ny, self.ny) * 2 + self.core)
+            if k < self.ny - 1:
+                self.y_copies.append(push(held, held, self.y_send.at[k], self.y_recv.at[k], self.next))
+            self.core_copies.append(push(held, held, self.core_send.at[k], self.core_recv.at[k], self.mate))
+        for copy in self.core_copies:
+            copy.wait_recv()
+        for copy in self.y_copies + self.core_copies:
+            copy.wait_send()
+        self.own.wait()
+
+    @staticmethod
+    def scratch(dp):
+        ny = dp // 2
+        return [
+            pltpu.SemaphoreType.DMA,
+            pltpu.SemaphoreType.DMA((ny - 1,)),
+            pltpu.SemaphoreType.DMA((ny - 1,)),
+            pltpu.SemaphoreType.DMA((ny,)),
+            pltpu.SemaphoreType.DMA((ny,)),
+        ]
+
+
+class Swap:
+    def __init__(self, dp, out, x_ref, o_ref, sems):
+        self.dp, self.out, self.x, self.o = dp, out, x_ref, o_ref
+        self.own_sem, self.send_sem, self.recv_sem = sems
+        self.me = lax.axis_index("dp")
+
+    def part(self, ref, index, by_columns):
+        if by_columns:
+            size = ref.shape[1] // self.dp
+            return ref.at[:, pl.ds(pl.multiple_of(index * size, size), size)]
+        size = ref.shape[0] // self.dp
+        return ref.at[pl.ds(pl.multiple_of(index * size, size), size)]
+
+    def begin(self):
+        mine = self.part(self.o, self.me, not self.out)
+        self.own = pltpu.make_async_copy(self.part(self.x, self.me, self.out), mine, self.own_sem)
+        self.own.start()
+        self.copies = [
+            push(self.part(self.x, other, self.out), mine, self.send_sem.at[k], self.recv_sem.at[k], {"dp": other})
+            for k, other in enumerate(others("dp"))
+        ]
+
+    def end(self):
+        for copy in self.copies:
+            copy.wait_recv()
+        for copy in self.copies:
+            copy.wait_send()
+        self.own.wait()
+
+    @staticmethod
+    def scratch(dp):
+        return [
+            pltpu.SemaphoreType.DMA,
+            pltpu.SemaphoreType.DMA((dp - 1,)),
+            pltpu.SemaphoreType.DMA((dp - 1,)),
+        ]
 
 
 def cost(micros):
     return pl.CostEstimate(flops=0, bytes_accessed=int(micros * 3.0e6), transcendentals=0)
+
+
+def spaces(count, space=pl.ANY):
+    return [pl.BlockSpec(memory_space=space)] * count
+
+
+def gather_body(n, cuts, x_ref, o_ref, *sems):
+    ring = Ring(n, cuts, x_ref, o_ref, sems)
+    greet(ring.sides)
+    ring.begin()
+    for step in range(n - 1):
+        ring.step(step)
+    ring.end()
 
 
 def ring_gather(x, n, number, cuts=2):
@@ -103,55 +221,129 @@
     return pl.pallas_call(
         functools.partial(gather_body, n, cuts),
         out_shape=jax.ShapeDtypeStruct((n * rows, columns), x.dtype),
-        in_specs=[pl.BlockSpec(memory_space=pl.ANY)],
+        in_specs=spaces(1, pltpu.VMEM),
         out_specs=pl.BlockSpec(memory_space=pl.ANY),
-        scratch_shapes=[
-            pltpu.SemaphoreType.DMA,
-            pltpu.SemaphoreType.DMA((2, n - 1, cuts)),
-            pltpu.SemaphoreType.DMA((2, n - 1, cuts)),
-        ],
+        scratch_shapes=Ring.scratch(n, cuts),
         compiler_params=pltpu.CompilerParams(collective_id=number, has_side_effects=True),
         cost_estimate=cost(75.0 * columns / 2048),
         name=f"ring_gather_{number}",
     )(x)
 
 
-def scatter_body(n, cuts, x_ref, o_ref, held, send_sem, recv_sem):
-    me, at = ring_places(n)
-    sides = (at(1), at(-1))
-    greet(*sides)
-    rows = o_ref.shape[0]
-    half = rows // 2
-    piece = half // cuts
-    copies = {}
+def opening_body(n, dp, cuts, grad, down, pair, hidden, grad_all, wide_down, wide_pair, hidden_turn, *sems):
+    ring = Ring(n, cuts, grad, grad_all, sems[:3])
+    parts = [
+        Spread(dp, down, wide_down, sems[3:8]),
+        Spread(dp, pair, wide_pair, sems[8:13]),
+        Swap(dp, True, hidden, hidden_turn, sems[13:16]),
+    ]
+    greet(list(ring.sides) + [{"dp": other} for other in others("dp")])
+    for part in parts:
+        part.begin()
+    ring.begin()
     for step in range(n - 1):
-        for cut in range(cuts):
+        ring.step(step)
+    for part in parts:
+        part.end()
+    ring.end()
+
+
+def opening(grad, down, pair, hidden, n, dp, number, cuts=2):
+    def full(x, times):
+        return jax.ShapeDtypeStruct((x.shape[0] * times, x.shape[1]), x.dtype)
+
+    turned = jax.ShapeDtypeStruct((hidden.shape[0] * dp, hidden.shape[1] // dp), hidden.dtype)
+    return pl.pallas_call(
+        functools.partial(opening_body, n, dp, cuts),
+        out_shape=(full(grad, n), full(down, dp), full(pair, dp), turned),
+        in_specs=spaces(4, pltpu.VMEM),
+        out_specs=tuple(spaces(4)),
+        scratch_shapes=Ring.scratch(n, cuts) + Spread.scratch(dp) * 2 + Swap.scratch(dp),
+        compiler_params=pltpu.CompilerParams(collective_id=number, has_side_effects=True),
+        cost_estimate=cost(80.0),
+        name="opening",
+    )(grad, down, pair, hidden)
+
+
+def spread_body(dp, x_ref, o_ref, *sems):
+    part = Spread(dp, x_ref, o_ref, sems)
+    greet([{"dp": other} for other in others("dp")])
+    part.begin()
+    part.end()
+
+
+def dp_gather(x, dp, number):
+    return pl.pallas_call(
+        functools.partial(spread_body, dp),
+        out_shape=jax.ShapeDtypeStruct((x.shape[0] * dp, x.shape[1]), x.dtype),
+        in_specs=spaces(1, pltpu.VMEM),
+        out_specs=pl.BlockSpec(memory_space=pl.ANY),
+        scratch_shapes=Spread.scratch(dp),
+        compiler_params=pltpu.CompilerParams(collective_id=number, has_side_effects=True),
+        cost_estimate=cost(20.0),
+        name=f"dp_gather_{number}",
+    )(x)
+
+
+class RingSum:
+    def __init__(self, n, cuts, x_ref, o_ref, held, sems):
+        self.n, self.cuts, self.x, self.o, self.held = n, cuts, x_ref, o_ref, held
+        self.send_sem, self.recv_sem = sems
+        self.me, self.at = ring_places(n)
+        self.sides = ({"heads": self.at(1)}, {"heads": self.at(-1)})
+        self.copies = {}
+        self.rows = x_ref.shape[0] // n
+        self.half = self.rows // 2
+        self.piece = self.half // cuts
+
+    def mine(self, owner, way, cut):
+        return pl.ds(pl.multiple_of(owner * self.rows + way * self.half + cut * self.piece, 8), self.piece)
+
+    def step(self, step):
+        for cut in range(self.cuts):
             for way in (0, 1):
-                owner = at(-1 - step) if way == 0 else at(1 + step)
-                part = x_ref.at[pl.ds(pl.multiple_of(owner * rows + way * half + cut * piece, piece), piece)]
-                here = pl.ds(cut * piece, piece)
-                src = part
+                owner = self.at(-1 - step) if way == 0 else self.at(1 + step)
+                src = self.x.at[self.mine(owner, way, cut)]
+                here = pl.ds(cut * self.piece, self.piece)
                 if step > 0:
-                    copies[way, step - 1, cut].wait_recv()
-                    src = held.at[way, step - 1, here]
-                    src[...] += part[...]
-                copies[way, step, cut] = push(
+                    self.copies[way, step - 1, cut].wait_recv()
+                    total = self.held.at[way, step - 1, here]
+                    total[...] += src[...]
+                    src = total
+                self.copies[way, step, cut] = push(
                     src,
-                    held.at[way, step, here],
-                    send_sem.at[way, step, cut],
-                    recv_sem.at[way, step, cut],
-                    sides[way],
+                    self.held.at[way, step, here],
+                    self.send_sem.at[way, step, cut],
+                    self.recv_sem.at[way, step, cut],
+                    self.sides[way],
                 )
-    for cut in range(cuts):
-        for way in (0, 1):
-            copies[way, n - 2, cut].wait_recv()
-            off = way * half + cut * piece
-            o_ref[pl.ds(off, piece)] = (
-                x_ref[pl.ds(pl.multiple_of(me * rows + off, piece), piece)]
-                + held[way, n - 2, pl.ds(cut * piece, piece)]
-            )
-    for copy in copies.values():
-        copy.wait_send()
+
+    def end(self):
+        for cut in range(self.cuts):
+            for way in (0, 1):
+                self.copies[way, self.n - 2, cut].wait_recv()
+                self.o[pl.ds(way * self.half + cut * self.piece, self.piece)] = (
+                    self.x[self.mine(self.me, way, cut)]
+                    + self.held[way, self.n - 2, pl.ds(cut * self.piece, self.piece)]
+                )
+        for copy in self.copies.values():
+            copy.wait_send()
+
+    @staticmethod
+    def scratch(n, cuts, rows, columns):
+        return [
+            pltpu.VMEM((2, n - 1, rows // 2, columns), jnp.float32),
+            pltpu.SemaphoreType.DMA((2, n - 1, cuts)),
+            pltpu.SemaphoreType.DMA((2, n - 1, cuts)),
+        ]
+
+
+def scatter_body(n, cuts, x_ref, o_ref, held, *sems):
+    ring = RingSum(n, cuts, x_ref, o_ref, held, sems)
+    greet(ring.sides)
+    for step in range(n - 1):
+        ring.step(step)
+    ring.end()
 
 
 def ring_scatter(x, n, number, cuts=4):
@@ -160,18 +352,110 @@
     return pl.pallas_call(
         functools.partial(scatter_body, n, cuts),
         out_shape=jax.ShapeDtypeStruct((rows, columns), x.dtype),
-        in_specs=[pl.BlockSpec(memory_space=pltpu.VMEM)],
+        in_specs=spaces(1, pltpu.VMEM),
         out_specs=pl.BlockSpec(memory_space=pltpu.VMEM),
-        scratch_shapes=[
-            pltpu.VMEM((2, n - 1, rows // 2, columns), x.dtype),
-            pltpu.SemaphoreType.DMA((2, n - 1, cuts)),
-            pltpu.SemaphoreType.DMA((2, n - 1, cuts)),
-        ],
+        scratch_shapes=RingSum.scratch(n, cuts, rows, columns),
         compiler_params=pltpu.CompilerParams(
             collective_id=number, has_side_effects=True, vmem_limit_bytes=40 << 20
         ),
         cost_estimate=cost(75.0 * columns / 2048),
         name=f"ring_scatter_{number}",
+    )(x)
+
+
+def turn_body(n, dp, cuts, x_ref, hidden, o_ref, hidden_turn, held, *sems):
+    ring = RingSum(n, cuts, x_ref, o_ref, held, sems[:2])
+    swap = Swap(dp, False, hidden, hidden_turn, sems[2:])
+    greet(list(ring.sides) + [{"dp": other} for other in others("dp")])
+    swap.begin()
+    for step in range(n - 1):
+        ring.step(step)
+    swap.end()
+    ring.end()
+
+
+def scatter_and_turn(x, hidden, n, dp, number, cuts=2):
+    rows, columns = x.shape[0] // n, x.shape[1]
+    cuts = min(cuts, rows // 16)
+    return pl.pallas_call(
+        functools.partial(turn_body, n, dp, cuts),
+        out_shape=(
+            jax.ShapeDtypeStruct((rows, columns), x.dtype),
+            jax.ShapeDtypeStruct((hidden.shape[0] // dp, hidden.shape[1] * dp), x.dtype),
+        ),
+        in_specs=spaces(2, pltpu.VMEM),
+        out_specs=(pl.BlockSpec(memory_space=pltpu.VMEM), pl.BlockSpec(memory_space=pl.ANY)),
+        scratch_shapes=RingSum.scratch(n, cuts, rows, columns) + Swap.scratch(dp),
+        compiler_params=pltpu.CompilerParams(
+            collective_id=number, has_side_effects=True, vmem_limit_bytes=40 << 20
+        ),
+        cost_estimate=cost(35.0),
+        name="scatter_and_turn",
+    )(x, hidden)
+
+
+class Total:
+    def __init__(self, axis, x_ref, held, sems):
+        self.x, self.held = x_ref, held
+        self.send_sem, self.recv_sem = sems
+        self.names = [{axis: other} for other in others(axis)]
+        self.count = lax.axis_size(axis)
+
+    def begin(self):
+        self.copies = [
+            push(self.x, self.held.at[k], self.send_sem.at[k], self.recv_sem.at[k], name)
+            for k, name in enumerate(self.names)
+        ]
+
+    def end(self):
+        for copy in self.copies:
+            copy.wait_recv()
+        for copy in self.copies:
+            copy.wait_send()
+
+    @staticmethod
+    def scratch(count, shape):
+        return [
+            pltpu.VMEM((count - 1,) + shape, jnp.float32),
+            pltpu.SemaphoreType.DMA((count - 1,)),
+            pltpu.SemaphoreType.DMA((count - 1,)),
+        ]
+
+
+def in_order(axis, own, held):
+    count = lax.axis_size(axis)
+    me = lax.axis_index(axis)
+    total = None
+    for device in range(count):
+        term = jnp.where(me == device, own, jnp.zeros_like(own))
+        for k in range(1, count):
+            term = term + jnp.where(lax.rem(me - k + count, count) == device, held[k - 1], jnp.zeros_like(own))
+        total = term if total is None else total + term
+    return total
+
+
+def sum_body(x_ref, o_ref, middle, held_heads, hs, hr, held_dp, ds, dr):
+    first = Total("heads", x_ref, held_heads, (hs, hr))
+    second = Total("dp", middle, held_dp, (ds, dr))
+    greet(first.names + second.names)
+    first.begin()
+    first.end()
+    middle[...] = in_order("heads", x_ref[...], held_heads)
+    second.begin()
+    second.end()
+    o_ref[...] = in_order("dp", middle[...], held_dp)
+
+
+def sum_all(x, n, dp, number):
+    return pl.pallas_call(
+        sum_body,
+        out_shape=jax.ShapeDtypeStruct(x.shape, x.dtype),
+        in_specs=spaces(1, pltpu.VMEM),
+        out_specs=pl.BlockSpec(memory_space=pltpu.VMEM),
+        scratch_shapes=[pltpu.VMEM(x.shape, x.dtype)] + Total.scratch(n, x.shape) + Total.scratch(dp, x.shape),
+        compiler_params=pltpu.CompilerParams(collective_id=number, has_side_effects=True),
+        cost_estimate=cost(8.0),
+        name=f"sum_all_{number}",
     )(x)
 
 
@@ -213,16 +497,8 @@
     )
 
 
-def spread_grads(part_down, part_pair, part_up, part_merge, part_gate, part_upper, part_lower):
-    return (
-        lax.psum_scatter(part_down, "dp", scatter_dimension=0, tiled=True),
-        lax.psum_scatter(part_pair, "dp", scatter_dimension=0, tiled=True),
-        lax.psum_scatter(part_up, "dp", scatter_dimension=0, tiled=True),
-        lax.psum_scatter(part_merge, "dp", scatter_dimension=1, tiled=True),
-        lax.psum_scatter(part_gate, "dp", scatter_dimension=0, tiled=True),
-        lax.psum_scatter(part_upper, "dp", scatter_dimension=0, tiled=True),
-        lax.psum_scatter(part_lower, "dp", scatter_dimension=1, tiled=True),
-    )
+def owned(part, axis):
+    return lax.psum_scatter(part, "dp", scatter_dimension=axis, tiled=True)
 
 
 def moments(value, grad, first, second):
@@ -272,18 +548,9 @@
     head_dim = key_value.shape[1] // 2
     local_heads = query_up.shape[1] // head_dim
     heads_count = lax.axis_size("heads")
+    dp_count = lax.axis_size("dp")
     group_rows = tok_rows * heads_count
     scale = head_dim ** (-0.5)
-    wide_down, wide_pair, wide_up, wide_merge, wide_gate, wide_upper, wide_lower = (
-        lax.all_gather(query_down, "dp", axis=0, tiled=True),
-        lax.all_gather(key_value, "dp", axis=0, tiled=True),
-        lax.all_gather(query_up, "dp", axis=0, tiled=True),
-        lax.all_gather(head_merge, "dp", axis=1, tiled=True),
-        lax.all_gather(gate_weight, "dp", axis=0, tiled=True),
-        lax.all_gather(up_weight, "dp", axis=0, tiled=True),
-        lax.all_gather(down_weight, "dp", axis=1, tiled=True),
-    )
-    grad_all = ring_gather(output_grad, heads_count, 5)
     group_index = jnp.arange(group_rows, dtype=jnp.int32)
     segment, position = layout(lengths[0], group_index)
     local_position = lax.dynamic_slice_in_dim(
@@ -295,6 +562,14 @@
     inv_one = lax.rsqrt(jnp.mean(block_input * block_input, axis=1, keepdims=True) + EPS_NORM)
     normed_one = block_input * inv_one
     hidden_one = normed_one * gain_attn
+    grad_all, wide_down, wide_pair, hidden_turn = opening(
+        output_grad, query_down, key_value, hidden_one, heads_count, dp_count, 5
+    )
+    query_up_in, head_merge_in, gate_in, upper_in, lower_in, grad_all = lax.optimization_barrier(
+        (query_up, head_merge, gate_weight, up_weight, down_weight, grad_all)
+    )
+    wide_up = lax.all_gather(query_up_in, "dp", axis=0, tiled=True)
+    wide_merge = lax.all_gather(head_merge_in, "dp", axis=1, tiled=True)
     latent_raw = matmul_high(hidden_one, wide_down)
     inv_query = lax.rsqrt(jnp.mean(latent_raw * latent_raw, axis=1, keepdims=True) + EPS_NORM)
     latent_hat = latent_raw * inv_query
@@ -305,6 +580,10 @@
     packed_all = ring_gather(
         jnp.concatenate([latent, key_local, value_local], axis=1), heads_count, 1
     )
+    gate_in, upper_in, lower_in, packed_all = lax.optimization_barrier((gate_in, upper_in, lower_in, packed_all))
+    wide_gate = lax.all_gather(gate_in, "dp", axis=0, tiled=True)
+    wide_upper = lax.all_gather(upper_in, "dp", axis=0, tiled=True)
+    wide_lower = lax.all_gather(lower_in, "dp", axis=1, tiled=True)
     latent_all = packed_all[:, :latent_dim]
     key_all = packed_all[:, latent_dim : latent_dim + head_dim]
     value_all = packed_all[:, latent_dim + head_dim :]
@@ -345,20 +624,34 @@
     sig_gate = jax.nn.sigmoid(gate_pre)
     silu_gate = gate_pre * sig_gate
     activ = silu_gate * up_pre
-    block_output = middle + ring_scatter(matmul_high(activ, wide_lower), heads_count, 4)
+    part_output, grad_lower = lax.optimization_barrier(
+        (matmul_high(activ, wide_lower), matmul_high(activ.T, grad_all))
+    )
+    grad_lower = owned(grad_lower, 1)
+    block_output = middle + ring_scatter(part_output, heads_count, 4)
     d_activ = matmul_high(grad_all, wide_lower.T)
-    grad_lower = matmul_high(activ.T, grad_all)
     d_gate_pre = d_activ * up_pre * (sig_gate * (1.0 + gate_pre * (1.0 - sig_gate)))
     d_up_pre = d_activ * silu_gate
-    grad_gate = matmul_high(hidden_all.T, d_gate_pre)
-    grad_upper = matmul_high(hidden_all.T, d_up_pre)
-    d_hidden_two = ring_scatter(
-        matmul_high(d_gate_pre, wide_gate.T) + matmul_high(d_up_pre, wide_upper.T), heads_count, 6
-    )
+    part_two, grad_gate, block_output = lax.optimization_barrier(
+        (
+            matmul_high(d_gate_pre, wide_gate.T) + matmul_high(d_up_pre, wide_upper.T),
+            matmul_high(hidden_all.T, d_gate_pre),
+            block_output,
+        )
+    )
+    grad_gate = owned(grad_gate, 0)
+    part_two, grad_lower = lax.optimization_barrier((part_two, grad_lower))
+    d_hidden_two = ring_scatter(part_two, heads_count, 6)
+    d_hidden_two, grad_upper = lax.optimization_barrier(
+        (d_hidden_two, matmul_high(hidden_all.T, d_up_pre))
+    )
+    grad_upper = owned(grad_upper, 0)
     d_normed_mid, grad_gain_ffn = norm_back(d_hidden_two, normed_two, inv_two, gain_ffn)
     d_middle = output_grad + d_normed_mid
+    d_middle, grad_gate = lax.optimization_barrier((d_middle, grad_gate))
     middle_all = ring_gather(d_middle, heads_count, 7)
-    grad_merge = matmul_high(mixed_heads.T, middle_all)
+    part_merge, grad_upper = lax.optimization_barrier((matmul_high(mixed_heads.T, middle_all), grad_upper))
+    grad_merge = owned(part_merge, 1)
     d_mixed = matmul_high(middle_all, wide_merge.T).reshape(
         n_blocks, block_rows, local_heads, head_dim
     )
@@ -384,30 +677,31 @@
     d_query_pre = rotate(
         d_query_blocks.reshape(group_rows, local_heads, head_dim), position, -1.0
     ).reshape(group_rows, local_heads * head_dim)
-    grad_up = matmul_high(latent_all.T, d_query_pre)
     d_latent_all = matmul_high(d_query_pre, wide_up.T)
-    packed_grad = ring_scatter(
-        jnp.concatenate([d_latent_all, d_key_sum, d_value_sum], axis=1), heads_count, 8
-    )
+    packed_part, grad_up = lax.optimization_barrier(
+        (
+            jnp.concatenate([d_latent_all, d_key_sum, d_value_sum], axis=1),
+            matmul_high(latent_all.T, d_query_pre),
+        )
+    )
+    grad_up, grad_merge = lax.optimization_barrier((grad_up, grad_merge))
+    grad_up = owned(grad_up, 0)
+    packed_grad = ring_scatter(packed_part, heads_count, 8)
     d_latent = packed_grad[:, :latent_dim]
     d_key_local = packed_grad[:, latent_dim : latent_dim + head_dim]
     d_value_local = packed_grad[:, latent_dim + head_dim :]
     d_pair = jnp.concatenate([rotate(d_key_local, local_position, -1.0), d_value_local], axis=1)
     d_latent_raw, grad_gain_query = norm_back(d_latent, latent_hat, inv_query, gain_query)
-    grad_down = matmul_high(hidden_one.T, d_latent_raw)
-    grad_pair = matmul_high(hidden_one.T, d_pair)
-    d_hidden_one = matmul_high(d_latent_raw, wide_down.T) + matmul_high(d_pair, wide_pair.T)
+    raw, grad_merge = lax.optimization_barrier((jnp.concatenate([d_latent_raw, d_pair], axis=1), grad_merge))
+    raw_all = dp_gather(raw, dp_count, 11)
+    part_shared = matmul_high(hidden_turn.T, raw_all)
+    d_hidden_turn = matmul_high(raw_all, jnp.concatenate([query_down, key_value], axis=1).T)
+    shared_cut, d_hidden_one = scatter_and_turn(part_shared, d_hidden_turn, heads_count, dp_count, 9)
+    shared = ring_gather(shared_cut, heads_count, 10)
     d_normed_in, grad_gain_attn = norm_back(d_hidden_one, normed_one, inv_one, gain_attn)
     input_grad = d_middle + d_normed_in
     grad_gains = jnp.concatenate([grad_gain_attn, grad_gain_query, grad_gain_ffn])
-    spread = spread_grads(
-        grad_down, grad_pair, grad_up, grad_merge, grad_gate, grad_upper, grad_lower
-    )
-    shared = ring_gather(
-        ring_scatter(jnp.concatenate([spread[0], spread[1]], axis=1), heads_count, 9), heads_count, 10
-    )
-    reduced = (shared[:, :latent_dim], shared[:, latent_dim:]) + tuple(spread[2:])
-    gains_total = lax.psum(grad_gains, ("dp", "heads"))
+    gains_total = sum_all(grad_gains.reshape(-1, 128), heads_count, dp_count, 12).reshape(-1)
     values = (
         norm_gains,
         query_down,
@@ -440,13 +734,13 @@
     )
     grads = (
         gains_total,
-        reduced[0],
-        reduced[1],
-        reduced[2],
-        reduced[3],
-        reduced[4],
-        reduced[5],
-        reduced[6],
+        shared[:, :latent_dim],
+        shared[:, latent_dim:],
+        grad_up,
+        grad_merge,
+        grad_gate,
+        grad_upper,
+        grad_lower,
     )
     stepped = [moments(values[slot], grads[slot], firsts[slot], seconds[slot]) for slot in range(8)]
     replica_share = [1.0, 1.0 / heads_count, 1.0 / heads_count, 1.0, 1.0, 1.0, 1.0, 1.0]
@@ -459,7 +753,8 @@
             for slot in range(1, 8)
         ]
     )
-    summed = lax.psum(square_rows, ("dp", "heads"))
+    square_tile = jnp.zeros((8, 128), jnp.float32).at[:7, :2].set(square_rows)
+    summed = sum_all(square_tile, heads_count, dp_count, 13)[:7, :2]
     gains_row = jnp.stack(
         [jnp.sum(norm_gains * norm_gains), jnp.sum(stepped[0][2] * stepped[0][2])]
     )

time: 1390 us -> 1170 us (0.84)
  waiting for transfers between devices: 211 us -> 1.9 us
  Pallas kernels: 679 us -> 740 us
  matrix products: 290 us -> 249 us
  blocking collectives: 39.7 us -> 0 us
    pallas_call x0 -> x5, Pallas kernels: none -> 180 us  [the longest x1 87.6 us: opening(): pl.pallas_call(functools.partial(opening_body, n, dp, cuts), out_shape=(f...]
    reduce_scatter x7 -> x5, waiting for transfers between devices: 175 us -> 0.01 us  [owned(): return lax.psum_scatter(part, 'dp', scatter_dimension=axis, tiled=True)]
    pallas_call x5 -> x4, Pallas kernels: 342 us -> 262 us  [ring_gather(): pl.pallas_call(functools.partial(gather_body, n, cuts), out_shape=jax.Sha...]
    psum x1 -> x0, blocking collectives: 39.7 us -> none  [on_device(): gains_total = lax.psum(grad_gains, ('dp', 'heads'))]
    pallas_call x5 -> x4, Pallas kernels: 337 us -> 297 us  [ring_scatter(): pl.pallas_call(functools.partial(scatter_body, n, cuts), out_shape=jax.Sh...]
    all_gather x7 -> x5, waiting for transfers between devices: 32.2 us -> 0.03 us  [the longest x1 0.02 us: on_device(): wide_gate = lax.all_gather(gate_in, 'dp', axis=0, tiled=True)]
    dot_general x21 -> x19, matrix products: 225 us -> 209 us  [matmul_high(): jnp.dot(left, right, precision=HIGH, preferred_element_type=jnp.float32)]
  transfers between devices with their start and end apart: 14 -> 10, of which waited for: 5 -> 0; matrix products, arithmetic and copies ran while one was open for 17% -> 28% of each run, Pallas kernels for 27% -> 55%
where the time goes in v2:
time: 1170 us; the launch traced here: 1160 us
  Pallas kernels  740 us (63%)
  matrix products  249 us (21%)
  other arithmetic  91.3 us (8%)
  local copies, waits for them, and re-layouts  50.3 us (4%)
  between operations  25.9 us (2%)
    pallas_call x4, Pallas kernels, ring_scatter(): pl.pallas_call(functools.partial(scatter_body, n, cuts), out_shape=jax.Sh...  297 us
    pallas_call x4, Pallas kernels, ring_gather(): pl.pallas_call(functools.partial(gather_body, n, cuts), out_shape=jax.Sha...  262 us
    dot_general x19, matrix products, matmul_high(): jnp.dot(left, right, precision=HIGH, preferred_element_type=jnp.float32)  209 us
    pallas_call x1, Pallas kernels, opening(): pl.pallas_call(functools.partial(opening_body, n, dp, cuts), out_shape=(f...  87.6 us
    pallas_call x1, Pallas kernels, scatter_and_turn(): pl.pallas_call(functools.partial(turn_body, n, dp, cuts), out_shape=(jax....  36 us
    pallas_call x1, Pallas kernels, dp_gather(): pl.pallas_call(functools.partial(spread_body, dp), out_shape=jax.ShapeDty...  34.7 us
    reduce_sum x7, other arithmetic, on_device(): jnp.sum(stepped[slot][2] * stepped[slot][2])  30.2 us
  transfers between devices with their start and end apart: 10, of which 0 were waited for; matrix products, arithmetic and copies ran while one was open for 28% of the time, Pallas kernels for 55%

profile of v2, /device:TPU:0, one launch (start us, length us, event | category | flops | bytes accessed | tf_op | source)
XLA Modules:
  0.0 1159.8 jit_solution(4451529617518655280)
XLA Ops:
  12.3 87.6 %opening.1 = (f32[1024,2048]{1,0:T(8,128)}, f32[2048,1024]{1,0:T(8,128)}, f32[2048,512]{1,0:T(8,128)}, f32[512,512]{1,0:T(8,128)}) custom-call(f32[128,2048]{1,0:T(8,128)} %grad.1, f32[512,1024]{1,0:T(8,128)} %down.1, f32[512,512]{1,0:T(8,128)} %pair.1, f32[128,2048]{1,0:T(8,128)} %multiply_multiply_fusion.8.hidden), custom_call_target="tpu_custom_call" | custom-call | bytes 240000000 | tf_op jit(solution)/shard_map/opening/pallas_call | solution.py:256
  113.9 64.3 %ring_gather_1.1 = f32[1024,1536]{1,0:T(8,128)} custom-call(f32[128,1536]{1,0:T(8,128)} %pad_maximum_fusion.3.x_ref), custom_call_target="tpu_custom_call" | custom-call | bytes 168750000 | tf_op jit(solution)/shard_map/ring_gather_1/pallas_call | solution.py:221
  200.1 18.8 %while.29 = (s32[]{:T(128)}, f32[2,512,2,256]{3,1,2,0:T(8,128)}, f32[2,2,512]{2,1,0:T(2,128)S(1)}, s32[2,512]{1,0:T(2,128)S(1)}, s32[1024]{0:T(1024)S(1)}, /*ind...) while((s32[]{:T(128)}, f32[2,512,2,256]{3,1,2,0:T(8,128)}, ...), condition=%wide.region_8.9_spmd.clone, body=%wide.region_5.8_spmd.clone.sunk | while | flops 3234331648 | bytes 39895248 | solution.py:615
  234.0 81.1 %ring_scatter_2.1 = f32[128,2048]{1,0:T(8,128)S(1)} custom-call(f32[1024,2048]{1,0:T(8,128)S(1)} %fusion.121.x_ref), custom_call_target="tpu_custom_call" | custom-call | bytes 225000000 | tf_op jit(solution)/shard_map/ring_scatter_2/pallas_call | solution.py:352
  316.5 81.3 %ring_gather_3.1 = f32[1024,2048]{1,0:T(8,128)} custom-call(f32[128,2048]{1,0:T(8,128)} %multiply_multiply_fusion.7.x_ref), custom_call_target="tpu_custom_call" | custom-call | bytes 225000000 | tf_op jit(solution)/shard_map/ring_gather_3/pallas_call | solution.py:221
  397.8 14.4 %fusion.123 = f32[1024,704]{0,1:T(8,128)} fusion(f32[1024,2048]{1,0:T(8,128)} %ring_gather_3.1, f32[2048,704]{0,1:T(8,128)} %all-gather.14.cloned.1.call-done), kind=kOutput, calls=%fused_computation.227 | convolution fusion | flops 8858370048 | bytes 17039360 | tf_op jit(solution)/shard_map/dot_general | solution.py:463
  412.1 13.0 %fusion.122 = f32[1024,704]{0,1:T(8,128)S(1)} fusion(f32[1024,2048]{1,0:T(8,128)} %ring_gather_3.1, f32[2048,704]{0,1:T(8,128)} %all-gather.12.cloned.1.call-done), kind=kOutput, calls=%fused_computation.226 | convolution fusion | flops 8858370048 | bytes 17039360 | tf_op jit(solution)/shard_map/dot_general | solution.py:463
  426.8 13.7 %fusion.74 = f32[704,2048]{1,0:T(8,128)} fusion(f32[1024,2048]{1,0:T(8,128)} %get-tuple-element.202, f32[1024,704]{0,1:T(8,128)S(1)} %fusion.122, f32[1024,704]{0,1:T(8,128)S(1)} %copy-done.75), kind=kOutput, calls=%fused_computation.109 | convolution fusion | flops 8861974528 | bytes 19922944 | tf_op jit(solution)/shard_map/dot_general | solution.py:463
  440.5 16.4 %fusion.76.x_ref = f32[1024,2048]{1,0:T(8,128)} fusion(f32[704,2048]{1,0:T(8,128)} %all-gather.6.cloned.1.call-done, f32[1024,704]{0,1:T(8,128)} %copy-done.79, f32[1024,704]{0,1:T(8,128)} %fusion.123), kind=kOutput, calls=%fused_computation.111 | convolution fusion | flops 8861974528 | bytes 19922944 | tf_op jit(solution)/shard_map/dot_general | solution.py:463
  460.3 79.6 %ring_scatter_4.1 = f32[128,2048]{1,0:T(8,128)S(1)} custom-call(f32[1024,2048]{1,0:T(8,128)S(1)} %copy-done.2), custom_call_target="tpu_custom_call" | custom-call | bytes 225000000 | tf_op jit(solution)/shard_map/ring_scatter_4/pallas_call | solution.py:352
  541.0 14.3 %fusion.120 = f32[1024,704]{0,1:T(8,128)} fusion(f32[1024,2048]{1,0:T(8,128)} %get-tuple-element.202, f32[704,2048]{1,0:T(8,128)S(1)} %copy-done.73), kind=kOutput, calls=%fused_computation.224 | convolution fusion | flops 8858370048 | bytes 17039360 | tf_op jit(solution)/shard_map/dot_general | solution.py:463
  555.3 15.8 %fusion.102 = f32[1024,2048]{1,0:T(8,128)} fusion(f32[2048,704]{0,1:T(8,128)S(1)} %bitcast.272, f32[1024,704]{0,1:T(8,128)S(1)} %copy-done.76, f32[1024,704]{0,1:T(8,128)} %fusion.120, f32[1024,704]{0,1:T(8,128)} %copy-done.79), kind=kOutput, calls=%fused_computation.218 | convolution fusion | flops 8864858112 | bytes 22806528 | tf_op jit(solution)/shard_map/dot_general | solution.py:463
  571.2 13.7 %fusion.101 = f32[2048,704]{0,1:T(8,128)} fusion(f32[1024,2048]{1,0:T(8,128)S(1)} %bitcast.260, f32[1024,704]{0,1:T(8,128)S(1)} %copy-done.77, f32[1024,704]{0,1:T(8,128)S(1)} %copy-done.78, f32[1024,704]{0,1:T(8,128)} %copy-done.79), kind=kOutput, calls=%fused_computation.217 | convolution fusion | flops 8864858112 | bytes 22806528 | tf_op jit(solution)/shard_map/dot_general | solution.py:463
  584.9 17.4 %convolution_add_fusion.x_ref = f32[1024,2048]{1,0:T(8,128)} fusion(f32[1024,2048]{1,0:T(8,128)} %fusion.102, f32[2048,704]{0,1:T(8,128)} %all-gather.12.cloned.1.call-done, f32[1024,704]{0,1:T(8,128)} %fusion.120, f32[1024,704]{0,1:T(8,128)} %fusion.123), kind=kOutput, calls=%fused_computation.72 | convolution fusion | flops 8864071680 | bytes 28311552 | tf_op jit(solution)/shard_map/dot_general | solution.py:463
  602.3 15.6 %fusion.78 = f32[2048,704]{0,1:T(8,128)} fusion(f32[1024,2048]{1,0:T(8,128)} %ring_gather_3.1, f32[1024,704]{0,1:T(8,128)} %fusion.120, f32[1024,704]{0,1:T(8,128)} %fusion.123), kind=kOutput, calls=%fused_computation.113 | convolution fusion | flops 8861974528 | bytes 19922944 | tf_op jit(solution)/shard_map/dot_general | solution.py:463
  621.3 79.0 %ring_scatter_6.1 = f32[128,2048]{1,0:T(8,128)S(1)} custom-call(f32[1024,2048]{1,0:T(8,128)S(1)} %copy-done.1), custom_call_target="tpu_custom_call" | custom-call | bytes 225000000 | tf_op jit(solution)/shard_map/ring_scatter_6/pallas_call | solution.py:352
  703.2 79.3 %ring_gather_7.1 = f32[1024,2048]{1,0:T(8,128)} custom-call(f32[128,2048]{1,0:T(8,128)} %multiply_add_fusion.8.x_ref), custom_call_target="tpu_custom_call" | custom-call | bytes 225000000 | tf_op jit(solution)/shard_map/ring_gather_7/pallas_call | solution.py:221
  782.5 11.4 fusion.124
  809.7 38.0 %while.30 = (s32[]{:T(128)}, f32[1024,256]{1,0:T(8,128)}, f32[1024,256]{1,0:T(8,128)}, f32[2,512,2,256]{3,1,0,2:T(8,128)}, s32[2,512]{1,0:T(2,128)S(1)}, /*index...) while((s32[]{:T(128)}, f32[1024,256]{1,0:T(8,128)}, ...), condition=%wide.region_15.16_spmd.clone, body=%wide.region_13.15_spmd.clone.sunk | while | flops 8065121280 | bytes 89694616 | solution.py:672
  879.9 57.8 %ring_scatter_8.1 = f32[128,1536]{1,0:T(8,128)S(1)} custom-call(f32[1024,1536]{1,0:T(8,128)S(1)} %copy-done), custom_call_target="tpu_custom_call" | custom-call | bytes 168750000 | tf_op jit(solution)/shard_map/ring_scatter_8/pallas_call | solution.py:352
  959.2 34.7 %dp_gather_11.1 = f32[512,1536]{1,0:T(8,128)} custom-call(f32[128,1536]{1,0:T(8,128)} %pad_maximum_fusion.4.x_ref), custom_call_target="tpu_custom_call" | custom-call | bytes 60000000 | tf_op jit(solution)/shard_map/dp_gather_11/pallas_call | solution.py:276
  1001.8 36.0 %scatter_and_turn.1 = (f32[64,1536]{1,0:T(8,128)S(1)}, f32[128,2048]{1,0:T(8,128)S(1)}) custom-call(f32[512,1536]{1,0:T(8,128)S(1)} %fusion.127.x_ref, f32[512,512]{1,0:T(8,128)S(1)} %fusion.65.hidden), custom_call_target="tpu_custom_call" | custom-call | bytes 105000000 | tf_op jit(solution)/shard_map/scatter_and_turn/pallas_call | solution.py:380
  1039.5 11.0 sum_all_12.1
  1054.0 37.6 %ring_gather_10.1 = f32[512,1536]{1,0:T(8,128)} custom-call(f32[64,1536]{1,0:T(8,128)} %copy-done.3), custom_call_target="tpu_custom_call" | custom-call | bytes 168750000 | tf_op jit(solution)/shard_map/ring_gather_10/pallas_call | solution.py:221
  (352 shorter events, 258.2 us)
Async XLA Ops:
  7.2 178.5 %all-gather.8.cloned.1.call-start = ((), (), s32[]{:S(2)}) async-start(), calls=%async_computation.6 | async-start | bytes 2621440 | tf_op jit(solution)/shard_map/all_gather | solution.py:571
  12.3 89.2 %copy-start.20 = (f32[128,2048]{1,0:T(8,128)S(1)}, f32[128,2048]{1,0:T(8,128)}, u32[]{:S(2)}) copy-start(f32[128,2048]{1,0:T(8,128)} %multiply_multiply_fusion.8.hidden) | copy-start | bytes 3145732
  100.0 124.4 %all-gather.10.cloned.1.call-start = ((), (), s32[]{:S(2)}) async-start(), calls=%async_computation.7 | async-start | bytes 5242880 | tf_op jit(solution)/shard_map/all_gather | solution.py:572
  100.7 297.0 %all-gather.14.cloned.1.call-start = ((), (), s32[]{:S(2)}) async-start(), calls=%async_computation.9 | async-start | bytes 7208960 | tf_op jit(solution)/shard_map/all_gather | solution.py:584
  105.0 74.7 %copy-start.67 = (f32[128]{0:T(128)}, f32[128]{0:T(128)S(1)}, u32[]{:S(2)}) copy-start(f32[128]{0:T(128)S(1)} %multiply_power_fusion) | copy-start | bytes 1540
  112.0 66.1 %copy-start.65 = (f32[128]{0:T(128)}, f32[128]{0:T(128)S(1)}, u32[]{:S(2)}) copy-start(f32[128]{0:T(128)S(1)} %add_rsqrt_fusion.1) | copy-start | bytes 1540
  178.2 233.9 %all-gather.12.cloned.1.call-start = ((), (), s32[]{:S(2)}) async-start(), calls=%async_computation.8 | async-start | bytes 7208960 | tf_op jit(solution)/shard_map/all_gather | solution.py:585
  178.8 261.7 %all-gather.6.cloned.1.call-start = ((), (), s32[]{:S(2)}) async-start(), calls=%async_computation.5 | async-start | bytes 7208960 | tf_op jit(solution)/shard_map/all_gather | solution.py:586
  179.4 438.5 %reduce-scatter.6.cloned.1.call-start = ((), (), s32[]{:S(2)}) async-start(), calls=%async_computation.10 | async-start | bytes 7208960 | tf_op jit(solution)/shard_map/reduce_scatter | solution.py:501
  233.9 81.2 %copy-start.13 = (f32[128,2048]{1,0:T(8,128)S(1)}, f32[128,2048]{1,0:T(8,128)}, u32[]{:S(2)}) copy-start(f32[128,2048]{1,0:T(8,128)} %param.33) | copy-start | bytes 3145732
  456.9 246.3 %reduce-scatter.8.cloned.1.call-start = ((), (), s32[]{:S(2)}) async-start(), calls=%async_computation.11 | async-start | bytes 7208960 | tf_op jit(solution)/shard_map/reduce_scatter | solution.py:501
  460.3 80.7 %copy-start.73 = (f32[704,2048]{1,0:T(8,128)S(1)}, f32[704,2048]{1,0:T(8,128)}, u32[]{:S(2)}) copy-start(f32[704,2048]{1,0:T(8,128)} %all-gather.6.cloned.1.call-done) | copy-start | bytes 17301508
  602.2 205.8 %reduce-scatter.10.cloned.1.call-start = ((), (), s32[]{:S(2)}) async-start(), calls=%async_computation.12 | async-start | bytes 7208960 | tf_op jit(solution)/shard_map/reduce_scatter | solution.py:501
  700.3 248.8 %reduce-scatter.12.cloned.1.call-start = ((), (), s32[]{:S(2)}) async-start(), calls=%async_computation.13 | async-start | bytes 5242880 | tf_op jit(solution)/shard_map/reduce_scatter | solution.py:501
  808.1 301.1 %reduce-scatter.14.cloned.1.call-start = ((), (), s32[]{:S(2)}) async-start(), calls=%async_computation.14 | async-start | bytes 2621440 | tf_op jit(solution)/shard_map/reduce_scatter | solution.py:501
  879.9 57.8 %copy-start.23 = (f32[704,512]{1,0:T(8,128)S(1)}, f32[704,512]{1,0:T(8,128)}, u32[]{:S(2)}) copy-start(f32[704,512]{1,0:T(8,128)} %param.57) | copy-start | bytes 4325380
  879.9 57.8 %copy-start.43 = (f32[704,512]{1,0:T(8,128)S(1)}, f32[704,512]{1,0:T(8,128)}, u32[]{:S(2)}) copy-start(f32[704,512]{1,0:T(8,128)} %param.58) | copy-start | bytes 4325380
  879.9 57.8 %copy-start.44 = (f32[704,512]{1,0:T(8,128)S(1)}, f32[704,512]{1,0:T(8,128)}, u32[]{:S(2)}) copy-start(f32[704,512]{1,0:T(8,128)} %param.59) | copy-start | bytes 4325380
  879.9 57.8 %copy-start.49 = (f32[704,512]{1,0:T(8,128)S(1)}, f32[704,512]{1,0:T(8,128)}, u32[]{:S(2)}) copy-start(f32[704,512]{1,0:T(8,128)} %reduce-scatter.6.cloned.1.call-done) | copy-start | bytes 4325380
  956.0 37.9 %copy-start.11 = (f32[512,1024]{1,0:T(8,128)S(1)}, f32[512,1024]{1,0:T(8,128)}, u32[]{:S(2)}) copy-start(f32[512,1024]{1,0:T(8,128)} %down.1) | copy-start | bytes 6291460
  956.0 37.9 %copy-start.21 = (f32[512,512]{1,0:T(8,128)S(1)}, f32[512,512]{1,0:T(8,128)}, u32[]{:S(2)}) copy-start(f32[512,512]{1,0:T(8,128)} %pair.1) | copy-start | bytes 3145732
  1001.7 48.8 %copy-start.57 = (f32[5120]{0:T(1024)S(1)}, f32[5120]{0:T(1024)}, u32[]{:S(2)}) copy-start(f32[5120]{0:T(1024)} %param.36) | copy-start | bytes 61444
  1001.7 48.8 %copy-start.63 = (f32[5120]{0:T(1024)S(1)}, f32[5120]{0:T(1024)}, u32[]{:S(2)}) copy-start(f32[5120]{0:T(1024)} %param.37) | copy-start | bytes 61444
  1001.7 48.8 %copy-start.64 = (f32[5120]{0:T(1024)S(1)}, f32[5120]{0:T(1024)}, u32[]{:S(2)}) copy-start(f32[5120]{0:T(1024)} %param.38) | copy-start | bytes 61444
  (83 other events, 556.9 us)
Sparse Core Ops, SparseCore 0:
  100.1 22.2 all-gather.7
  123.9 34.4 all-gather.9
  178.3 42.2 all-gather.13
  222.1 43.3 all-gather.11
  266.9 43.3 all-gather.5
  457.0 54.0 reduce-scatter.5
  602.4 54.1 reduce-scatter.7
  700.4 54.4 reduce-scatter.9
  808.2 43.8 reduce-scatter.11
  949.2 42.1 reduce-scatter.13

commit v3 on v2

--- a/solution.py
+++ b/solution.py
@@ -61,12 +61,183 @@
     pl.semaphore_wait(bar, len(names))
 
 
-def push(src, dst, send, recv, name):
-    copy = pltpu.make_async_remote_copy(
+def remote(src, dst, send, recv, name):
+    return pltpu.make_async_remote_copy(
         src_ref=src, dst_ref=dst, send_sem=send, recv_sem=recv, device_id=name, device_id_type=MESH
     )
+
+
+def push(*what):
+    copy = remote(*what)
     copy.start()
     return copy
+
+
+def halves(value):
+    high = value.astype(jnp.bfloat16)
+    return high, (value - high.astype(jnp.float32)).astype(jnp.bfloat16)
+
+
+def padded(shape, size):
+    return shape[0] * -(-shape[1] // 128) * 128 * size
+
+
+class Job:
+    def __init__(self, form, lefts, rights, tile):
+        self.form, self.lefts, self.rights, self.tile = form, lefts, rights, tile
+        self.summed = len(lefts) > 1
+        rows = rights[0].shape[0]
+        self.chunk = next(c for c in (512, 352, 256, 128, 64, 32, 16) if rows % c == 0)
+        if form == "tn":
+            self.chunk = next(c for c in (256, 128) if rows % c == 0)
+            self.extent = lefts[0].shape[1]
+        else:
+            self.extent = lefts[0].shape[0]
+        self.chunks = rows // self.chunk
+        self.prepare = self.chunks * len(rights)
+        self.units = self.prepare + self.extent // tile
+        width = {"nt": 0, "nn": 1, "tn": 1}[form]
+        shapes = [
+            (x.shape[1], self.extent) if form == "tn" else (self.extent, x.shape[width]) for x in rights
+        ]
+        self.outs = shapes[:1] if self.summed else shapes
+        self.splits = [x.shape[::-1] if form == "tn" else x.shape for x in rights]
+
+    def bare(self):
+        kept = object.__new__(Job)
+        kept.__dict__.update(self.__dict__)
+        kept.lefts, kept.rights = len(self.lefts), len(self.rights)
+        return kept
+
+    def scratch(self):
+        made = [pltpu.VMEM(x.shape, jnp.float32) for x in self.lefts + self.rights]
+        for shape in self.splits:
+            made += [pltpu.VMEM(shape, jnp.bfloat16)] * 2
+        made += [pltpu.VMEM(shape, jnp.float32) for shape in self.outs]
+        made += [pltpu.SemaphoreType.DMA((len(self.lefts) + len(self.rights),))]
+        made += [pltpu.SemaphoreType.DMA((len(self.outs), self.extent // self.tile))]
+        return made
+
+    def bytes(self):
+        shapes = [x.shape for x in self.lefts + self.rights] + self.splits + self.outs
+        return sum(padded(shape, 4) for shape in shapes)
+
+
+def limit(jobs, *shapes):
+    return (8 << 20) + sum(job.bytes() for job in jobs) + sum(padded(shape, 4) for shape in shapes)
+
+
+class Work:
+    def __init__(self, plan, refs, firsts):
+        refs = list(refs)
+
+        def take(count):
+            taken = refs[:count]
+            del refs[:count]
+            return taken
+
+        sources = [take(job.lefts + job.rights) for job in plan]
+        self.first = take(firsts)
+        sinks = [take(len(job.outs)) for job in plan]
+        self.jobs = []
+        for job, source, sink in zip(plan, sources, sinks):
+            held = take(job.lefts + job.rights)
+            split = [take(2) for _ in range(job.rights)]
+            outs = take(len(job.outs))
+            in_sem, out_sem = take(2)
+            self.jobs.append((job, source, sink, held, split, outs, in_sem, out_sem))
+        self.rest = refs
+        self.units = sum(job.units for job in plan)
+
+    @staticmethod
+    def operands(jobs):
+        return [x for job in jobs for x in job.lefts + job.rights]
+
+    @staticmethod
+    def outputs(jobs):
+        return [jax.ShapeDtypeStruct(shape, jnp.float32) for job in jobs for shape in job.outs]
+
+    @staticmethod
+    def scratch(jobs):
+        return [x for job in jobs for x in job.scratch()]
+
+    def loads(self):
+        return [
+            pltpu.make_async_copy(source[k], held[k], in_sem.at[k])
+            for _, source, _, held, _, _, in_sem, _ in self.jobs
+            for k in range(len(source))
+        ]
+
+    def load(self):
+        for copy in self.loads():
+            copy.start()
+
+    def ready(self):
+        for copy in self.loads():
+            copy.wait()
+
+    def share(self, steps, step):
+        if not self.jobs:
+            return
+
+        def unit(index, carry):
+            base = 0
+            for entry in self.jobs:
+                job = entry[0]
+                for k in range(job.rights):
+                    self.when(index, base + k * job.chunks, job.chunks, functools.partial(self.split, entry, k))
+                self.when(
+                    index, base + job.prepare, job.units - job.prepare, functools.partial(self.tile, entry)
+                )
+                base += job.units
+            return carry
+
+        lax.fori_loop(step * self.units // steps, (step + 1) * self.units // steps, unit, 0)
+
+    def when(self, index, start, count, act):
+        @pl.when((index >= start) & (index < start + count))
+        def _():
+            act(index - start)
+
+    def split(self, entry, k, chunk):
+        job, held, split = entry[0], entry[3], entry[4]
+        rows = pl.ds(pl.multiple_of(chunk * job.chunk, job.chunk), job.chunk)
+        value = held[job.lefts + k][rows, :]
+        where = (slice(None), rows) if job.form == "tn" else (rows, slice(None))
+        split[k][0][where], split[k][1][where] = halves(value.T if job.form == "tn" else value)
+
+    def tile(self, entry, index):
+        job, _, sink, held, split, outs, _, out_sem = entry
+        rows = pl.ds(pl.multiple_of(index * job.tile, job.tile), job.tile)
+        numbers = (((1,), (1 if job.form == "nt" else 0,)), ((), ()))
+        where = (slice(None), rows) if job.form == "tn" else (rows, slice(None))
+
+        def product(own, other):
+            pair = (other, own) if job.form == "tn" else (own, other)
+            return lax.dot_general(*pair, numbers, preferred_element_type=jnp.float32)
+
+        total = None
+        for k in range(job.lefts):
+            high, low = halves(held[k][where])
+            for j in [k] if job.summed else range(job.rights):
+                right_high, right_low = split[j][0][...], split[j][1][...]
+                made = product(high, right_high) + product(high, right_low) + product(low, right_high)
+                if job.summed:
+                    total = made if total is None else total + made
+                else:
+                    outs[j][where] = made
+        if job.summed:
+            outs[0][where] = total
+        for j, out in enumerate(outs):
+            pltpu.make_async_copy(out.at[where], sink[j].at[where], out_sem.at[j, index]).start()
+
+    def end(self):
+        for job, _, sink, _, _, outs, _, out_sem in self.jobs:
+            for j, out in enumerate(outs):
+                for index in range(job.extent // job.tile):
+                    rows = pl.ds(index * job.tile, job.tile)
+                    where = (slice(None), rows) if job.form == "tn" else (rows, slice(None))
+                    pltpu.make_async_copy(out.at[where], sink[j].at[where], out_sem.at[j, index]).wait()
 
 
 class Ring:
@@ -75,36 +246,56 @@
         self.own_sem, self.send_sem, self.recv_sem = sems
         self.me, self.at = ring_places(n)
         self.sides = ({"heads": self.at(1)}, {"heads": self.at(-1)})
-        self.copies = {}
+        self.rows = x_ref.shape[0]
+        self.piece = self.rows // 2 // cuts
+        self.parts = [(cut, way) for cut in range(cuts) for way in (0, 1)]
+
+    def copy(self, step, cut, way, first=False):
+        off = way * (self.rows // 2) + cut * self.piece
+        origin = self.at(-step) if way == 0 else self.at(step)
+        dst = self.o.at[pl.ds(pl.multiple_of(origin * self.rows + off, 8), self.piece)]
+        src = self.x.at[pl.ds(off, self.piece)] if first else dst
+        sems = self.send_sem.at[way, step, cut], self.recv_sem.at[way, step, cut]
+        return remote(src, dst, *sems, self.sides[way])
+
+    def own(self):
+        here = self.o.at[pl.ds(pl.multiple_of(self.me * self.rows, 8), self.rows)]
+        return pltpu.make_async_copy(self.x, here, self.own_sem)
 
     def begin(self):
-        rows = self.x.shape[0]
-        self.own = pltpu.make_async_copy(self.x, self.o.at[pl.ds(self.me * rows, rows)], self.own_sem)
-        self.own.start()
+        self.own().start()
+        for part in self.parts:
+            self.copy(0, *part, first=True).start()
 
     def step(self, step):
-        rows = self.x.shape[0]
-        half = rows // 2
-        piece = half // self.cuts
-        for cut in range(self.cuts):
-            for way in (0, 1):
-                if step > 0:
-                    self.copies[way, step - 1, cut].wait_recv()
-                off = way * half + cut * piece
-                origin = self.at(-step) if way == 0 else self.at(step)
-                dst = self.o.at[pl.ds(origin * rows + off, piece)]
-                src = self.x.at[pl.ds(off, piece)] if step == 0 else dst
-                self.copies[way, step, cut] = push(
-                    src, dst, self.send_sem.at[way, step, cut], self.recv_sem.at[way, step, cut], self.sides[way]
-                )
+        for part in self.parts:
+            self.copy(step - 1, *part).wait_recv()
+            self.copy(step, *part).start()
 
     def end(self):
-        for cut in range(self.cuts):
-            for way in (0, 1):
-                self.copies[way, self.n - 2, cut].wait_recv()
-        for copy in self.copies.values():
-            copy.wait_send()
-        self.own.wait()
+        for part in self.parts:
+            self.copy(self.n - 2, *part).wait_recv()
+
+        def sent(step, carry):
+            for part in self.parts:
+                self.copy(step, *part).wait_send()
+            return carry
+
+        lax.fori_loop(0, self.n - 1, sent, 0)
+        self.own().wait()
+
+    def run(self, work=None):
+        def body(step, carry):
+            if work is not None:
+                work(step - 1)
+
+            @pl.when(step < self.n - 1)
+            def _():
+                self.step(step)
+
+            return carry
+
+        lax.fori_loop(1, self.n, body, 0)
 
     @staticmethod
     def scratch(n, cuts):
@@ -206,28 +397,35 @@
     return [pl.BlockSpec(memory_space=space)] * count
 
 
-def gather_body(n, cuts, x_ref, o_ref, *sems):
-    ring = Ring(n, cuts, x_ref, o_ref, sems)
+def gather_body(n, cuts, plan, x_ref, *refs):
+    work = Work(plan, refs, 1)
+    ring = Ring(n, cuts, x_ref, work.first[0], work.rest)
+    work.load()
     greet(ring.sides)
     ring.begin()
-    for step in range(n - 1):
-        ring.step(step)
+    work.ready()
+    ring.run(functools.partial(work.share, n - 1))
     ring.end()
-
-
-def ring_gather(x, n, number, cuts=2):
+    work.end()
+
+
+def ring_gather(x, n, number, jobs=(), cuts=2):
     rows, columns = x.shape
     cuts = min(cuts, rows // 16)
-    return pl.pallas_call(
-        functools.partial(gather_body, n, cuts),
-        out_shape=jax.ShapeDtypeStruct((n * rows, columns), x.dtype),
-        in_specs=spaces(1, pltpu.VMEM),
-        out_specs=pl.BlockSpec(memory_space=pl.ANY),
-        scratch_shapes=Ring.scratch(n, cuts),
-        compiler_params=pltpu.CompilerParams(collective_id=number, has_side_effects=True),
+    plan = [job.bare() for job in jobs]
+    result = pl.pallas_call(
+        functools.partial(gather_body, n, cuts, plan),
+        out_shape=(jax.ShapeDtypeStruct((n * rows, columns), x.dtype), *Work.outputs(jobs)),
+        in_specs=spaces(1, pltpu.VMEM) + spaces(len(Work.operands(jobs))),
+        out_specs=tuple(spaces(1 + len(Work.outputs(jobs)))),
+        scratch_shapes=Work.scratch(jobs) + Ring.scratch(n, cuts),
+        compiler_params=pltpu.CompilerParams(
+            collective_id=number, has_side_effects=True, vmem_limit_bytes=limit(jobs, x.shape)
+        ),
         cost_estimate=cost(75.0 * columns / 2048),
         name=f"ring_gather_{number}",
-    )(x)
+    )(x, *Work.operands(jobs))
+    return result if jobs else result[0]
 
 
 def opening_body(n, dp, cuts, grad, down, pair, hidden, grad_all, wide_down, wide_pair, hidden_turn, *sems):
@@ -241,8 +439,7 @@
     for part in parts:
         part.begin()
     ring.begin()
-    for step in range(n - 1):
-        ring.step(step)
+    ring.run()
     for part in parts:
         part.end()
     ring.end()
@@ -291,43 +488,59 @@
         self.send_sem, self.recv_sem = sems
         self.me, self.at = ring_places(n)
         self.sides = ({"heads": self.at(1)}, {"heads": self.at(-1)})
-        self.copies = {}
         self.rows = x_ref.shape[0] // n
         self.half = self.rows // 2
         self.piece = self.half // cuts
-
-    def mine(self, owner, way, cut):
-        return pl.ds(pl.multiple_of(owner * self.rows + way * self.half + cut * self.piece, 8), self.piece)
+        self.parts = [(cut, way) for cut in range(cuts) for way in (0, 1)]
+
+    def mine(self, owner, cut, way):
+        start = owner * self.rows + way * self.half + cut * self.piece
+        return self.x.at[pl.ds(pl.multiple_of(start, 8), self.piece)]
+
+    def slot(self, step, cut, way):
+        return self.held.at[way, step, pl.ds(cut * self.piece, self.piece)]
+
+    def owner(self, step, way):
+        return self.at(-1 - step) if way == 0 else self.at(1 + step)
+
+    def copy(self, step, cut, way, first=False):
+        src = self.mine(self.owner(step, way), cut, way) if first else self.slot(step - 1, cut, way)
+        sems = self.send_sem.at[way, step, cut], self.recv_sem.at[way, step, cut]
+        return remote(src, self.slot(step, cut, way), *sems, self.sides[way])
+
+    def begin(self):
+        for part in self.parts:
+            self.copy(0, *part, first=True).start()
 
     def step(self, step):
-        for cut in range(self.cuts):
-            for way in (0, 1):
-                owner = self.at(-1 - step) if way == 0 else self.at(1 + step)
-                src = self.x.at[self.mine(owner, way, cut)]
-                here = pl.ds(cut * self.piece, self.piece)
-                if step > 0:
-                    self.copies[way, step - 1, cut].wait_recv()
-                    total = self.held.at[way, step - 1, here]
-                    total[...] += src[...]
-                    src = total
-                self.copies[way, step, cut] = push(
-                    src,
-                    self.held.at[way, step, here],
-                    self.send_sem.at[way, step, cut],
-                    self.recv_sem.at[way, step, cut],
-                    self.sides[way],
-                )
+        for cut, way in self.parts:
+            self.arrived(step - 1, cut, way)
+            total = self.slot(step - 1, cut, way)
+            total[...] += self.mine(self.owner(step, way), cut, way)[...]
+            self.copy(step, cut, way).start()
+
+    def arrived(self, step, cut, way):
+        slot = self.slot(step, cut, way)
+        sems = self.send_sem.at[way, step, cut], self.recv_sem.at[way, step, cut]
+        remote(slot, slot, *sems, self.sides[way]).wait_recv()
 
     def end(self):
-        for cut in range(self.cuts):
-            for way in (0, 1):
-                self.copies[way, self.n - 2, cut].wait_recv()
-                self.o[pl.ds(way * self.half + cut * self.piece, self.piece)] = (
-                    self.x[self.mine(self.me, way, cut)]
-                    + self.held[way, self.n - 2, pl.ds(cut * self.piece, self.piece)]
-                )
-        for copy in self.copies.values():
-            copy.wait_send()
+        for cut, way in self.parts:
+            self.arrived(self.n - 2, cut, way)
+            self.o[pl.ds(way * self.half + cut * self.piece, self.piece)] = (
+                self.mine(self.me, cut, way)[...] + self.slot(self.n - 2, cut, way)[...]
+            )
+
+        def sent(step, carry):
+            for cut, way in self.parts:
+                slot = self.slot(step, cut, way)
+                sems = self.send_sem.at[way, step, cut], self.recv_sem.at[way, step, cut]
+                remote(slot, slot, *sems, self.sides[way]).wait_send()
+            return carry
+
+        lax.fori_loop(0, self.n - 1, sent, 0)
+
+    run = Ring.run
 
     @staticmethod
     def scratch(n, cuts, rows, columns):
@@ -338,29 +551,35 @@
         ]
 
 
-def scatter_body(n, cuts, x_ref, o_ref, held, *sems):
-    ring = RingSum(n, cuts, x_ref, o_ref, held, sems)
+def scatter_body(n, cuts, plan, x_ref, *refs):
+    work = Work(plan, refs, 1)
+    ring = RingSum(n, cuts, x_ref, work.first[0], work.rest[0], work.rest[1:])
+    work.load()
     greet(ring.sides)
-    for step in range(n - 1):
-        ring.step(step)
+    ring.begin()
+    work.ready()
+    ring.run(functools.partial(work.share, n - 1))
     ring.end()
-
-
-def ring_scatter(x, n, number, cuts=4):
+    work.end()
+
+
+def ring_scatter(x, n, number, jobs=(), cuts=4):
     rows, columns = x.shape[0] // n, x.shape[1]
     cuts = min(cuts, rows // 16)
-    return pl.pallas_call(
-        functools.partial(scatter_body, n, cuts),
-        out_shape=jax.ShapeDtypeStruct((rows, columns), x.dtype),
-        in_specs=spaces(1, pltpu.VMEM),
-        out_specs=pl.BlockSpec(memory_space=pltpu.VMEM),
-        scratch_shapes=RingSum.scratch(n, cuts, rows, columns),
+    plan = [job.bare() for job in jobs]
+    result = pl.pallas_call(
+        functools.partial(scatter_body, n, cuts, plan),
+        out_shape=(jax.ShapeDtypeStruct((rows, columns), x.dtype), *Work.outputs(jobs)),
+        in_specs=spaces(1, pltpu.VMEM) + spaces(len(Work.operands(jobs))),
+        out_specs=tuple(spaces(1, pltpu.VMEM) + spaces(len(Work.outputs(jobs)))),
+        scratch_shapes=Work.scratch(jobs) + RingSum.scratch(n, cuts, rows, columns),
         compiler_params=pltpu.CompilerParams(
-            collective_id=number, has_side_effects=True, vmem_limit_bytes=40 << 20
+            collective_id=number, has_side_effects=True, vmem_limit_bytes=limit(jobs, x.shape, x.shape, (rows, columns))
         ),
         cost_estimate=cost(75.0 * columns / 2048),
         name=f"ring_scatter_{number}",
-    )(x)
+    )(x, *Work.operands(jobs))
+    return result if jobs else result[0]
 
 
 def turn_body(n, dp, cuts, x_ref, hidden, o_ref, hidden_turn, held, *sems):
@@ -368,8 +587,8 @@
     swap = Swap(dp, False, hidden, hidden_turn, sems[2:])
     greet(list(ring.sides) + [{"dp": other} for other in others("dp")])
     swap.begin()
-    for step in range(n - 1):
-        ring.step(step)
+    ring.begin()
+    ring.run()
     swap.end()
     ring.end()
 
@@ -581,8 +800,8 @@
         jnp.concatenate([latent, key_local, value_local], axis=1), heads_count, 1
     )
     gate_in, upper_in, lower_in, packed_all = lax.optimization_barrier((gate_in, upper_in, lower_in, packed_all))
-    wide_gate = lax.all_gather(gate_in, "dp", axis=0, tiled=True)
-    wide_upper = lax.all_gather(upper_in, "dp", axis=0, tiled=True)
+    turned_gate = lax.all_gather(gate_in.T, "dp", axis=1, tiled=True)
+    turned_upper = lax.all_gather(upper_in.T, "dp", axis=1, tiled=True)
     wide_lower = lax.all_gather(lower_in, "dp", axis=1, tiled=True)
     latent_all = packed_all[:, :latent_dim]
     key_all = packed_all[:, latent_dim : latent_dim + head_dim]
@@ -618,40 +837,48 @@
     inv_two = lax.rsqrt(jnp.mean(middle * middle, axis=1, keepdims=True) + EPS_NORM)
     normed_two = middle * inv_two
     hidden_two = normed_two * gain_ffn
-    hidden_all = ring_gather(hidden_two, heads_count, 3)
-    gate_pre = matmul_high(hidden_all, wide_gate)
-    up_pre = matmul_high(hidden_all, wide_upper)
+    inside = group_rows <= 1024
+
+    def job(form, lefts, rights, tile):
+        return [Job(form, lefts, rights, tile)] if inside else []
+
+    made = ring_gather(hidden_two, heads_count, 3, job("nt", [grad_all], [wide_lower], 256))
+    hidden_all, d_activ = made if inside else (made, matmul_high(grad_all, wide_lower.T))
+    gate_pre = matmul_high(hidden_all, turned_gate.T)
+    up_pre = matmul_high(hidden_all, turned_upper.T)
     sig_gate = jax.nn.sigmoid(gate_pre)
     silu_gate = gate_pre * sig_gate
     activ = silu_gate * up_pre
-    part_output, grad_lower = lax.optimization_barrier(
-        (matmul_high(activ, wide_lower), matmul_high(activ.T, grad_all))
-    )
-    grad_lower = owned(grad_lower, 1)
-    block_output = middle + ring_scatter(part_output, heads_count, 4)
-    d_activ = matmul_high(grad_all, wide_lower.T)
     d_gate_pre = d_activ * up_pre * (sig_gate * (1.0 + gate_pre * (1.0 - sig_gate)))
     d_up_pre = d_activ * silu_gate
-    part_two, grad_gate, block_output = lax.optimization_barrier(
-        (
-            matmul_high(d_gate_pre, wide_gate.T) + matmul_high(d_up_pre, wide_upper.T),
-            matmul_high(hidden_all.T, d_gate_pre),
-            block_output,
+    part_output = matmul_high(activ, wide_lower)
+    if inside:
+        part_output, part_two = ring_scatter(
+            part_output,
+            heads_count,
+            4,
+            job("nn", [d_gate_pre, d_up_pre], [turned_gate, turned_upper], 128),
         )
-    )
-    grad_gate = owned(grad_gate, 0)
-    part_two, grad_lower = lax.optimization_barrier((part_two, grad_lower))
-    d_hidden_two = ring_scatter(part_two, heads_count, 6)
-    d_hidden_two, grad_upper = lax.optimization_barrier(
-        (d_hidden_two, matmul_high(hidden_all.T, d_up_pre))
-    )
-    grad_upper = owned(grad_upper, 0)
+        d_hidden_two, grad_gate, grad_lower = ring_scatter(
+            part_two,
+            heads_count,
+            6,
+            job("tn", [hidden_all], [d_gate_pre], 256) + job("tn", [grad_all], [activ], 256),
+        )
+    else:
+        part_output = ring_scatter(part_output, heads_count, 4)
+        part_two = matmul_high(d_gate_pre, turned_gate) + matmul_high(d_up_pre, turned_upper)
+        d_hidden_two = ring_scatter(part_two, heads_count, 6)
+        grad_gate = matmul_high(d_gate_pre.T, hidden_all)
+        grad_lower = matmul_high(activ.T, grad_all)
+    block_output = middle + part_output
+    grad_gate = owned(grad_gate, 1)
     d_normed_mid, grad_gain_ffn = norm_back(d_hidden_two, normed_two, inv_two, gain_ffn)
     d_middle = output_grad + d_normed_mid
-    d_middle, grad_gate = lax.optimization_barrier((d_middle, grad_gate))
-    middle_all = ring_gather(d_middle, heads_count, 7)
-    part_merge, grad_upper = lax.optimization_barrier((matmul_high(mixed_heads.T, middle_all), grad_upper))
-    grad_merge = owned(part_merge, 1)
+    made = ring_gather(d_middle, heads_count, 7, job("tn", [hidden_all], [d_up_pre], 256))
+    middle_all, grad_upper = made if inside else (made, matmul_high(d_up_pre.T, hidden_all))
+    middle_all, grad_gate, grad_lower = lax.optimization_barrier((middle_all, grad_gate, grad_lower))
+    grad_lower = owned(grad_lower, 1)
     d_mixed = matmul_high(middle_all, wide_merge.T).reshape(
         n_blocks, block_rows, local_heads, head_dim
     )
@@ -678,21 +905,30 @@
         d_query_blocks.reshape(group_rows, local_heads, head_dim), position, -1.0
     ).reshape(group_rows, local_heads * head_dim)
     d_latent_all = matmul_high(d_query_pre, wide_up.T)
-    packed_part, grad_up = lax.optimization_barrier(
-        (
-            jnp.concatenate([d_latent_all, d_key_sum, d_value_sum], axis=1),
-            matmul_high(latent_all.T, d_query_pre),
+    packed_part = jnp.concatenate([d_latent_all, d_key_sum, d_value_sum], axis=1)
+    packed_part, grad_lower, grad_upper = lax.optimization_barrier((packed_part, grad_lower, grad_upper))
+    grad_upper = owned(grad_upper, 1)
+    if inside:
+        packed_grad, grad_merge, grad_up = ring_scatter(
+            packed_part,
+            heads_count,
+            8,
+            job("tn", [middle_all], [mixed_heads], 256) + job("tn", [d_query_pre], [latent_all], 256),
         )
-    )
+    else:
+        packed_grad = ring_scatter(packed_part, heads_count, 8)
+        grad_merge = matmul_high(mixed_heads.T, middle_all)
+        grad_up = matmul_high(latent_all.T, d_query_pre)
+    packed_grad, grad_merge, grad_upper = lax.optimization_barrier((packed_grad, grad_merge, grad_upper))
+    grad_merge = owned(grad_merge, 1)
     grad_up, grad_merge = lax.optimization_barrier((grad_up, grad_merge))
     grad_up = owned(grad_up, 0)
-    packed_grad = ring_scatter(packed_part, heads_count, 8)
     d_latent = packed_grad[:, :latent_dim]
     d_key_local = packed_grad[:, latent_dim : latent_dim + head_dim]
     d_value_local = packed_grad[:, latent_dim + head_dim :]
     d_pair = jnp.concatenate([rotate(d_key_local, local_position, -1.0), d_value_local], axis=1)
     d_latent_raw, grad_gain_query = norm_back(d_latent, latent_hat, inv_query, gain_query)
-    raw, grad_merge = lax.optimization_barrier((jnp.concatenate([d_latent_raw, d_pair], axis=1), grad_merge))
+    raw = jnp.concatenate([d_latent_raw, d_pair], axis=1)
     raw_all = dp_gather(raw, dp_count, 11)
     part_shared = matmul_high(hidden_turn.T, raw_all)
     d_hidden_turn = matmul_high(raw_all, jnp.concatenate([query_down, key_value], axis=1).T)
@@ -738,8 +974,8 @@
         shared[:, latent_dim:],
         grad_up,
         grad_merge,
-        grad_gate,
-        grad_upper,
+        grad_gate.T,
+        grad_upper.T,
         grad_lower,
     )
     stepped = [moments(values[slot], grads[slot], firsts[slot], seconds[slot]) for slot in range(8)]

time: 1170 us -> 1100 us (0.940)
  matrix products: 249 us -> 149 us
  local copies, waits for them, and re-layouts: 50.3 us -> 67 us
  Pallas kernels: 740 us -> 755 us
    dot_general x19 -> x11, matrix products: 209 us -> 95.8 us  [matmul_high(): jnp.dot(left, right, precision=HIGH, preferred_element_type=jnp.float32)]
    unnamed x154 -> x180, local copies, waits for them, and re-layouts: 22.4 us -> 37 us
  transfers between devices with their start and end apart: 10 -> 10, of which waited for: 0 -> 1; matrix products, arithmetic and copies ran while one was open for 28% -> 20% of each run, Pallas kernels for 55% -> 45%
where the time goes in v3:
time: 1100 us; the launch traced here: 1090 us
  Pallas kernels  755 us (69%)
  matrix products  149 us (14%)
  other arithmetic  86.8 us (8%)
  local copies, waits for them, and re-layouts  67 us (6%)
  between operations  26 us (2%)
    pallas_call x4, Pallas kernels, ring_scatter(): pl.pallas_call(functools.partial(scatter_body, n, cuts, plan), out_shape=...  312 us
    pallas_call x4, Pallas kernels, ring_gather(): pl.pallas_call(functools.partial(gather_body, n, cuts, plan), out_shape=(...  257 us
    dot_general x11, matrix products, matmul_high(): jnp.dot(left, right, precision=HIGH, preferred_element_type=jnp.float32)  95.8 us
    pallas_call x1, Pallas kernels, opening(): pl.pallas_call(functools.partial(opening_body, n, dp, cuts), out_shape=(f...  87.5 us
    pallas_call x1, Pallas kernels, dp_gather(): pl.pallas_call(functools.partial(spread_body, dp), out_shape=jax.ShapeDty...  40.8 us
    unnamed x180, local copies, waits for them, and re-layouts  37 us
    pallas_call x1, Pallas kernels, scatter_and_turn(): pl.pallas_call(functools.partial(turn_body, n, dp, cuts), out_shape=(jax....  35.6 us
    reduce_sum x7, other arithmetic, on_device(): jnp.sum(stepped[slot][2] * stepped[slot][2])  31.2 us
  transfers between devices with their start and end apart: 10, of which 1 were waited for; matrix products, arithmetic and copies ran while one was open for 20% of the time, Pallas kernels for 45%

profile of v3, /device:TPU:0, one launch (start us, length us, event | category | flops | bytes accessed | tf_op | source)
XLA Modules:
  0.0 1092.5 jit_solution(11112049408090741225)
XLA Ops:
  12.2 87.5 %opening.1 = (f32[1024,2048]{1,0:T(8,128)}, f32[2048,1024]{1,0:T(8,128)}, f32[2048,512]{1,0:T(8,128)}, f32[512,512]{1,0:T(8,128)}) custom-call(f32[128,2048]{1,0:T(8,128)} %grad.1, f32[512,1024]{1,0:T(8,128)} %down.1, f32[512,512]{1,0:T(8,128)} %pair.1, f32[128,2048]{1,0:T(8,128)} %multiply_multiply_fusion.8.hidden), custom_call_target="tpu_custom_call" | custom-call | bytes 240000000 | tf_op jit(solution)/shard_map/opening/pallas_call | solution.py:453
  112.7 63.2 %ring_gather_1.1 = f32[1024,1536]{1,0:T(8,128)S(1)} custom-call(f32[128,1536]{1,0:T(8,128)S(1)} %pad_maximum_fusion.2.x_ref), custom_call_target="tpu_custom_call" | custom-call | bytes 168750000 | tf_op jit(solution)/shard_map/ring_gather_1/pallas_call | solution.py:416
  186.0 7.0 fusion.92
  200.4 16.2 %while.29 = (s32[]{:T(128)}, f32[2,512,2,256]{3,1,2,0:T(8,128)}, f32[2,2,512]{2,1,0:T(2,128)S(1)}, s32[2,512]{1,0:T(2,128)S(1)}, s32[1024]{0:T(1024)S(1)}, /*ind...) while((s32[]{:T(128)}, f32[2,512,2,256]{3,1,2,0:T(8,128)}, ...), condition=%wide.region_8.9_spmd.clone, body=%wide.region_5.8_spmd.clone.sunk | while | flops 3234331648 | bytes 23118476 | solution.py:834
  221.3 9.5 fusion.107.x_ref
  230.8 81.2 %ring_scatter_2.1 = f32[128,2048]{1,0:T(8,128)S(1)} custom-call(f32[1024,2048]{1,0:T(8,128)S(1)} %fusion.107.x_ref), custom_call_target="tpu_custom_call" | custom-call | bytes 225000000 | tf_op jit(solution)/shard_map/ring_scatter_2/pallas_call | solution.py:570
  316.0 80.7 %ring_gather_3.1 = (f32[1024,2048]{1,0:T(8,128)S(1)}, f32[1024,704]{1,0:T(8,128)S(1)}) custom-call(f32[128,2048]{1,0:T(8,128)S(1)} %multiply_multiply_fusion.7.x_ref, f32[1024,2048]{1,0:T(8,128)} %get-tuple-element.215.refs_0_.refs_2_, f32[704,2048]{1,0:T(8,128)S(1)} %copy-done.8), custom_call_target="tpu_custom_call" | custom-call | bytes 225000000 | tf_op jit(solution)/shard_map/ring_gather_3/pallas_call | solution.py:416
  401.7 16.2 %fusion.108 = f32[1024,704]{1,0:T(8,128)} fusion(f32[1024,2048]{1,0:T(8,128)} %copy-done.1, f32[704,2048]{1,0:T(8,128)} %all-gather.14.cloned.1.call-done.refs_3_), kind=kOutput, calls=%fused_computation.217 | convolution fusion | flops 8858370048 | bytes 17039360 | tf_op jit(solution)/shard_map/dot_general | solution.py:682
  417.9 17.6 %fusion.72 = (f32[1024,704]{1,0:T(8,128)}, f32[1024,704]{1,0:T(8,128)}, f32[1024,704]{1,0:T(8,128)S(1)}) fusion(f32[1024,704]{1,0:T(8,128)S(1)} %copy-done.13, f32[1024,704]{1,0:T(8,128)} %fusion.108, f32[1024,2048]{1,0:T(8,128)} %copy-done.1, f32[704,2048]{1,0:T(8,128)} %all-gather.12.cloned.1.call-done.refs_2_), kind=kOutput, calls=%fused_computation.140 | convolution fusion | flops 8867020800 | bytes 28573696 | tf_op jit(solution)/shard_map/dot_general | solution.py:682
  435.5 12.6 %fusion.109.x_ref = f32[1024,2048]{1,0:T(8,128)} fusion(f32[1024,704]{1,0:T(8,128)S(1)} %get-tuple-element.530.refs_3_, f32[704,2048]{1,0:T(8,128)S(1)} %copy-done.9), kind=kOutput, calls=%fused_computation.218 | convolution fusion | flops 8858370048 | bytes 17039360 | tf_op jit(solution)/shard_map/dot_general | solution.py:682
  448.1 84.2 %ring_scatter_4.1 = (f32[128,2048]{1,0:T(8,128)}, f32[1024,2048]{1,0:T(8,128)}) custom-call(f32[1024,2048]{1,0:T(8,128)} %fusion.109.x_ref, f32[1024,704]{1,0:T(8,128)} %get-tuple-element.529.refs_0_.refs_1_, f32[1024,704]{1,0:T(8,128)} %get-tuple-element.528.refs_1_, f32[704,2048]{1,0:T(8,128)} %all-gather.12.cloned.1.call-done.refs_2_, ...), custom_call_target="tpu_custom_call" | custom-call | bytes 225000000 | tf_op jit(solution)/shard_map/ring_scatter_4/pallas_call | solution.py:570
  532.3 83.5 %ring_scatter_6.1 = (f32[128,2048]{1,0:T(8,128)}, f32[704,2048]{1,0:T(8,128)}, f32[704,2048]{1,0:T(8,128)}) custom-call(f32[1024,2048]{1,0:T(8,128)} %get-tuple-element.222.x_ref, f32[1024,2048]{1,0:T(8,128)} %copy-done.1, f32[1024,704]{1,0:T(8,128)} %get-tuple-element.529.refs_0_.refs_1_, f32[1024,2048]{1,0:T(8,128)} %get-tuple-element.215.refs_0_.refs_2_, ...), custom_call_target="tpu_custom_call" | custom-call | bytes 225000000 | tf_op jit(solution)/shard_map/ring_scatter_6/pallas_call | solution.py:570
  625.4 77.5 %ring_gather_7.1 = (f32[1024,2048]{1,0:T(8,128)S(1)}, f32[704,2048]{1,0:T(8,128)S(1)}) custom-call(f32[128,2048]{1,0:T(8,128)S(1)} %get-tuple-element.552.x_ref, f32[1024,2048]{1,0:T(8,128)S(1)} %copy-done.2, f32[1024,704]{1,0:T(8,128)S(1)} %copy-done.5), custom_call_target="tpu_custom_call" | custom-call | bytes 225000000 | tf_op jit(solution)/shard_map/ring_gather_7/pallas_call | solution.py:416
  708.7 11.4 %fusion.110 = f32[1024,512]{1,0:T(8,128)} fusion(f32[1024,2048]{1,0:T(8,128)} %copy-done.6, f32[512,2048]{1,0:T(8,128)} %all-gather.8.cloned.1.call-done), kind=kOutput, calls=%fused_computation.219 | convolution fusion | flops 6442450944 | bytes 14680064 | tf_op jit(solution)/shard_map/dot_general | solution.py:682
  723.8 53.7 %while.30 = (s32[]{:T(128)}, f32[1024,256]{1,0:T(8,128)}, f32[1024,256]{1,0:T(8,128)}, f32[2,512,2,256]{3,1,0,2:T(8,128)}, s32[2,512]{1,0:T(2,128)S(1)}, /*index...) while((s32[]{:T(128)}, f32[1024,256]{1,0:T(8,128)}, ...), condition=%wide.region_14.15_spmd.clone, body=%wide.region_12.14_spmd.clone.sunk | while | flops 8065121280 | bytes 110667128 | solution.py:899
  737.9 7.1 fusion.172
  763.8 7.4 fusion.172
  795.1 63.5 %ring_scatter_8.1 = (f32[128,1536]{1,0:T(8,128)S(1)}, f32[512,2048]{1,0:T(8,128)}, f32[1024,512]{1,0:T(8,128)}) custom-call(f32[1024,1536]{1,0:T(8,128)} %pad_maximum_fusion.x_ref, f32[1024,2048]{1,0:T(8,128)} %copy-done.6, f32[1024,512]{1,0:T(8,128)S(1)} %bitcast.267, f32[1024,512]{1,0:T(8,128)} %bitcast.269, f32[1024,1024]{1,0:T(8,128)} %slice.139.refs_3_), custom_call_target="tpu_custom_call" | custom-call | bytes 168750000 | tf_op jit(solution)/shard_map/ring_scatter_8/pallas_call | solution.py:570
  859.9 6.7 multiply_reduce_fusion.6
  874.6 40.8 %dp_gather_11.1 = f32[512,1536]{1,0:T(8,128)} custom-call(f32[128,1536]{1,0:T(8,128)} %pad_maximum_fusion.3.x_ref), custom_call_target="tpu_custom_call" | custom-call | bytes 60000000 | tf_op jit(solution)/shard_map/dp_gather_11/pallas_call | solution.py:473
  928.3 35.6 %scatter_and_turn.1 = (f32[64,1536]{1,0:T(8,128)S(1)}, f32[128,2048]{1,0:T(8,128)S(1)}) custom-call(f32[512,1536]{1,0:T(8,128)S(1)} %fusion.112.x_ref, f32[512,512]{1,0:T(8,128)S(1)} %fusion.61.hidden), custom_call_target="tpu_custom_call" | custom-call | bytes 105000000 | tf_op jit(solution)/shard_map/scatter_and_turn/pallas_call | solution.py:599
  965.4 11.3 %sum_all_12.1 = f32[40,128]{1,0:T(8,128)} custom-call(f32[40,128]{1,0:T(8,128)} %maximum_bitcast_fusion.1.x_ref), custom_call_target="tpu_custom_call" | custom-call | bytes 24000000 | tf_op jit(solution)/shard_map/sum_all_12/pallas_call | solution.py:669
  980.7 35.5 %ring_gather_10.1 = f32[512,1536]{1,0:T(8,128)S(1)} custom-call(f32[64,1536]{1,0:T(8,128)S(1)} %get-tuple-element.241.x_ref), custom_call_target="tpu_custom_call" | custom-call | bytes 168750000 | tf_op jit(solution)/shard_map/ring_gather_10/pallas_call | solution.py:416
  1049.7 10.4 sum_all_13.1
  (355 shorter events, 215.4 us)
Async XLA Ops:
  7.2 178.8 %all-gather.6.cloned.1.call-start = ((), (), s32[]{:S(2)}) async-start(), calls=%async_computation.5 | async-start | bytes 2621440 | tf_op jit(solution)/shard_map/all_gather | solution.py:790
  99.8 121.4 %all-gather.8.cloned.1.call-start = ((), (), s32[]{:S(2)}) async-start(), calls=%async_computation.6 | async-start | bytes 5242880 | tf_op jit(solution)/shard_map/all_gather | solution.py:791
  100.6 212.8 %all-gather.10.cloned.1.call-start = ((), (), s32[]{:S(2)}) async-start(), calls=%async_computation.7 | async-start | bytes 7208960 | tf_op jit(solution)/shard_map/all_gather | solution.py:805
  104.8 75.1 %copy-start.83 = (f32[128]{0:T(128)}, f32[128]{0:T(128)S(1)}, u32[]{:S(2)}) copy-start(f32[128]{0:T(128)S(1)} %multiply_power_fusion) | copy-start | bytes 1540
  111.9 64.0 %copy-start.81 = (f32[128]{0:T(128)}, f32[128]{0:T(128)S(1)}, u32[]{:S(2)}) copy-start(f32[128]{0:T(128)S(1)} %add_rsqrt_fusion.1) | copy-start | bytes 1540
  178.5 223.1 %all-gather.14.cloned.1.call-start = ((), (), s32[]{:S(2)}) async-start(), calls=%async_computation.9 | async-start | bytes 7208960 | tf_op jit(solution)/shard_map/all_gather | solution.py:804
  179.1 238.7 %all-gather.12.cloned.1.call-start = ((), (), s32[]{:S(2)}) async-start(), calls=%async_computation.8 | async-start | bytes 7208960 | tf_op jit(solution)/shard_map/all_gather | solution.py:803
  179.7 528.9 %reduce-scatter.6.cloned.1.call-start = ((), (), s32[]{:S(2)}) async-start(), calls=%async_computation.10 | async-start | bytes 7208960 | tf_op jit(solution)/shard_map/reduce_scatter | solution.py:720
  230.8 81.2 %copy-start.30 = (f32[128,2048]{1,0:T(8,128)S(1)}, f32[128,2048]{1,0:T(8,128)}, u32[]{:S(2)}) copy-start(f32[128,2048]{1,0:T(8,128)} %param.33) | copy-start | bytes 3145732
  401.7 16.2 %copy-start.13 = (f32[1024,704]{1,0:T(8,128)S(1)}, f32[1024,704]{1,0:T(8,128)}, u32[]{:S(2)}) copy-start(f32[1024,704]{1,0:T(8,128)} %copy-done.12) | copy-start | bytes 8650756
  417.9 17.6 %copy-start.9 = (f32[704,2048]{1,0:T(8,128)S(1)}, f32[704,2048]{1,0:T(8,128)}, u32[]{:S(2)}) copy-start(f32[704,2048]{1,0:T(8,128)} %all-gather.10.cloned.1.call-done.refs_1_) | copy-start | bytes 17301508
  615.9 174.3 %reduce-scatter.8.cloned.1.call-start = ((), (), s32[]{:S(2)}) async-start(), calls=%async_computation.11 | async-start | bytes 7208960 | tf_op jit(solution)/shard_map/reduce_scatter | solution.py:720
  708.6 150.9 %reduce-scatter.10.cloned.1.call-start = ((), (), s32[]{:S(2)}) async-start(), calls=%async_computation.12 | async-start | bytes 7208960 | tf_op jit(solution)/shard_map/reduce_scatter | solution.py:720
  790.2 130.0 %reduce-scatter.12.cloned.1.call-start = ((), (), s32[]{:S(2)}) async-start(), calls=%async_computation.13 | async-start | bytes 5242880 | tf_op jit(solution)/shard_map/reduce_scatter | solution.py:720
  859.6 183.1 %reduce-scatter.14.cloned.1.call-start = ((), (), s32[]{:S(2)}) async-start(), calls=%async_computation.14 | async-start | bytes 2621440 | tf_op jit(solution)/shard_map/reduce_scatter | solution.py:720
  874.6 45.7 %copy-start.26 = (f32[512,1024]{1,0:T(8,128)S(1)}, f32[512,1024]{1,0:T(8,128)}, u32[]{:S(2)}) copy-start(f32[512,1024]{1,0:T(8,128)} %down.1) | copy-start | bytes 6291460
  928.2 35.6 %copy-start.31 = (f32[128,2048]{1,0:T(8,128)S(1)}, f32[128,2048]{1,0:T(8,128)}, u32[]{:S(2)}) copy-start(f32[128,2048]{1,0:T(8,128)} %param.33) | copy-start | bytes 3145732
  928.3 35.6 %copy-start.75 = (f32[2048]{0:T(1024)S(1)}, f32[2048]{0:T(1024)}, u32[]{:S(2)}) copy-start(f32[2048]{0:T(1024)} %copy-done.74) | copy-start | bytes 24580
  928.3 35.6 %copy-start.86 = (f32[128]{0:T(128)S(1)}, f32[128]{0:T(128)}, u32[]{:S(2)}) copy-start(f32[128]{0:T(128)} %copy-done.85) | copy-start | bytes 1540
  980.7 35.6 %copy-start.40 = (f32[512,704]{0,1:T(8,128)S(1)}, f32[512,704]{0,1:T(8,128)}, u32[]{:S(2)}) copy-start(f32[512,704]{0,1:T(8,128)} %param.54) | copy-start | bytes 4325380
  980.7 35.6 %copy-start.65 = (f32[512,704]{0,1:T(8,128)S(1)}, f32[512,704]{0,1:T(8,128)}, u32[]{:S(2)}) copy-start(f32[512,704]{0,1:T(8,128)} %param.55) | copy-start | bytes 4325380
  1042.6 18.3 %copy-start.92 = (f32[1,2]{0,1:T(2,128)S(1)}, f32[1,2]{0,1:T(2,128)}, u32[]{:S(2)}) copy-start(f32[1,2]{0,1:T(2,128)} %copy.124) | copy-start | bytes 28
  1042.6 29.4 %copy-start.39 = (f32[704,512]{1,0:T(8,128)S(1)}, f32[704,512]{1,0:T(8,128)}, u32[]{:S(2)}) copy-start(f32[704,512]{1,0:T(8,128)} %param.57) | copy-start | bytes 4325380
  1042.6 29.4 %copy-start.50 = (f32[704,512]{1,0:T(8,128)S(1)}, f32[704,512]{1,0:T(8,128)}, u32[]{:S(2)}) copy-start(f32[704,512]{1,0:T(8,128)} %get-tuple-element.500) | copy-start | bytes 4325380
  (90 other events, 381.0 us)
Sparse Core Ops, SparseCore 0:
  99.9 22.2 all-gather.5
  123.8 34.4 all-gather.7
  178.7 42.2 all-gather.9
  222.4 43.3 all-gather.13
  267.3 43.3 all-gather.11
  616.0 54.1 reduce-scatter.5
  708.8 54.7 reduce-scatter.7
  790.3 54.7 reduce-scatter.9
  859.7 60.4 reduce-scatter.11
  922.6 32.7 reduce-scatter.13

commit v4 on v3

--- a/solution.py
+++ b/solution.py
@@ -83,8 +83,12 @@
 
 
 class Job:
-    def __init__(self, form, lefts, rights, tile):
-        self.form, self.lefts, self.rights, self.tile = form, lefts, rights, tile
+    def __init__(self, form, lefts, rights, tile, joined=False):
+        self.joined = joined
+        self.form, self.lefts, self.tile = form, lefts, tile
+        self.whole = [x[0] if isinstance(x, tuple) else x for x in rights]
+        rights = [x[1] if isinstance(x, tuple) else x for x in rights]
+        self.rights = rights
         self.summed = len(lefts) > 1
         rows = rights[0].shape[0]
         self.chunk = next(c for c in (512, 352, 256, 128, 64, 32, 16) if rows % c == 0)
@@ -106,7 +110,7 @@
     def bare(self):
         kept = object.__new__(Job)
         kept.__dict__.update(self.__dict__)
-        kept.lefts, kept.rights = len(self.lefts), len(self.rights)
+        kept.lefts, kept.rights, kept.whole = len(self.lefts), len(self.rights), None
         return kept
 
     def scratch(self):
@@ -138,7 +142,14 @@
 
         sources = [take(job.lefts + job.rights) for job in plan]
         self.first = take(firsts)
-        sinks = [take(len(job.outs)) for job in plan]
+        if plan and plan[0].joined:
+            [together], start, sinks = take(1), 0, []
+            for job in plan:
+                rows = job.outs[0][0]
+                sinks.append([together.at[pl.ds(start, rows)]])
+                start += rows
+        else:
+            sinks = [take(len(job.outs)) for job in plan]
         self.jobs = []
         for job, source, sink in zip(plan, sources, sinks):
             held = take(job.lefts + job.rights)
@@ -151,11 +162,14 @@
 
     @staticmethod
     def operands(jobs):
-        return [x for job in jobs for x in job.lefts + job.rights]
+        return [x for job in jobs for x in job.lefts + job.whole]
 
     @staticmethod
     def outputs(jobs):
-        return [jax.ShapeDtypeStruct(shape, jnp.float32) for job in jobs for shape in job.outs]
+        shapes = [shape for job in jobs for shape in job.outs]
+        if jobs and jobs[0].joined:
+            shapes = [(sum(shape[0] for shape in shapes), shapes[0][1])]
+        return [jax.ShapeDtypeStruct(shape, jnp.float32) for shape in shapes]
 
     @staticmethod
     def scratch(jobs):
@@ -163,7 +177,7 @@
 
     def loads(self):
         return [
-            pltpu.make_async_copy(source[k], held[k], in_sem.at[k])
+            pltpu.make_async_copy(source[k].at[:, : held[k].shape[1]], held[k], in_sem.at[k])
             for _, source, _, held, _, _, in_sem, _ in self.jobs
             for k in range(len(source))
         ]
@@ -307,8 +321,8 @@
 
 
 class Spread:
-    def __init__(self, dp, x_ref, o_ref, sems):
-        self.x, self.o, self.ny = x_ref, o_ref, dp // 2
+    def __init__(self, dp, x_ref, o_ref, sems, pieces=1):
+        self.x, self.o, self.ny, self.pieces = x_ref, o_ref, dp // 2, pieces
         self.own_sem, self.y_send, self.y_recv, self.core_send, self.core_recv = sems
         me = lax.axis_index("dp")
         self.y, self.core = me // 2, me % 2
@@ -317,37 +331,48 @@
         self.next = {"dp": lax.rem(self.y + 1, self.ny) * 2 + self.core}
         self.rows = x_ref.shape[0]
 
-    def block(self, owner):
-        return self.o.at[pl.ds(owner * self.rows, self.rows)]
+    def block(self, owner, piece):
+        size = self.rows // self.pieces
+        return self.o.at[pl.ds(pl.multiple_of(owner * self.rows + piece * size, 8), size)]
 
     def begin(self):
-        self.own = pltpu.make_async_copy(self.x, self.block(self.me), self.own_sem)
+        mine = self.o.at[pl.ds(pl.multiple_of(self.me * self.rows, 8), self.rows)]
+        self.own = pltpu.make_async_copy(self.x, mine, self.own_sem)
         self.own.start()
-        self.y_copies = [push(self.x, self.block(self.me), self.y_send.at[0], self.y_recv.at[0], self.next)]
-        self.core_copies = [push(self.x, self.block(self.me), self.core_send.at[0], self.core_recv.at[0], self.mate)]
+        self.y_copies, self.core_copies = {}, {}
+        for piece in range(self.pieces):
+            size = self.rows // self.pieces
+            src, dst = self.x.at[pl.ds(piece * size, size)], self.block(self.me, piece)
+            self.send(self.y_copies, src, dst, self.y_send, self.y_recv, 0, piece, self.next)
+            self.send(self.core_copies, src, dst, self.core_send, self.core_recv, 0, piece, self.mate)
+
+    def send(self, copies, src, dst, send, recv, k, piece, name):
+        copies[k, piece] = push(src, dst, send.at[k, piece], recv.at[k, piece], name)
 
     def end(self):
         for k in range(1, self.ny):
-            self.y_copies[k - 1].wait_recv()
-            held = self.block(lax.rem(self.y - k + self.ny, self.ny) * 2 + self.core)
-            if k < self.ny - 1:
-                self.y_copies.append(push(held, held, self.y_send.at[k], self.y_recv.at[k], self.next))
-            self.core_copies.append(push(held, held, self.core_send.at[k], self.core_recv.at[k], self.mate))
-        for copy in self.core_copies:
+            owner = lax.rem(self.y - k + self.ny, self.ny) * 2 + self.core
+            for piece in range(self.pieces):
+                self.y_copies[k - 1, piece].wait_recv()
+                held = self.block(owner, piece)
+                if k < self.ny - 1:
+                    self.send(self.y_copies, held, held, self.y_send, self.y_recv, k, piece, self.next)
+                self.send(self.core_copies, held, held, self.core_send, self.core_recv, k, piece, self.mate)
+        for copy in self.core_copies.values():
             copy.wait_recv()
-        for copy in self.y_copies + self.core_copies:
+        for copy in [*self.y_copies.values(), *self.core_copies.values()]:
             copy.wait_send()
         self.own.wait()
 
     @staticmethod
-    def scratch(dp):
+    def scratch(dp, pieces=1):
         ny = dp // 2
         return [
             pltpu.SemaphoreType.DMA,
-            pltpu.SemaphoreType.DMA((ny - 1,)),
-            pltpu.SemaphoreType.DMA((ny - 1,)),
-            pltpu.SemaphoreType.DMA((ny,)),
-            pltpu.SemaphoreType.DMA((ny,)),
+            pltpu.SemaphoreType.DMA((ny - 1, pieces)),
+            pltpu.SemaphoreType.DMA((ny - 1, pieces)),
+            pltpu.SemaphoreType.DMA((ny, pieces)),
+            pltpu.SemaphoreType.DMA((ny, pieces)),
         ]
 
 
@@ -420,7 +445,7 @@
         out_specs=tuple(spaces(1 + len(Work.outputs(jobs)))),
         scratch_shapes=Work.scratch(jobs) + Ring.scratch(n, cuts),
         compiler_params=pltpu.CompilerParams(
-            collective_id=number, has_side_effects=True, vmem_limit_bytes=limit(jobs, x.shape)
+            collective_id=number, has_side_effects=True, vmem_limit_bytes=ATTEND_LIMIT if jobs else limit(jobs, x.shape)
         ),
         cost_estimate=cost(75.0 * columns / 2048),
         name=f"ring_gather_{number}",
@@ -463,7 +488,7 @@
 
 
 def spread_body(dp, x_ref, o_ref, *sems):
-    part = Spread(dp, x_ref, o_ref, sems)
+    part = Spread(dp, x_ref, o_ref, sems, 4)
     greet([{"dp": other} for other in others("dp")])
     part.begin()
     part.end()
@@ -475,7 +500,7 @@
         out_shape=jax.ShapeDtypeStruct((x.shape[0] * dp, x.shape[1]), x.dtype),
         in_specs=spaces(1, pltpu.VMEM),
         out_specs=pl.BlockSpec(memory_space=pl.ANY),
-        scratch_shapes=Spread.scratch(dp),
+        scratch_shapes=Spread.scratch(dp, 4),
         compiler_params=pltpu.CompilerParams(collective_id=number, has_side_effects=True),
         cost_estimate=cost(20.0),
         name=f"dp_gather_{number}",
@@ -665,6 +690,46 @@
     o_ref[...] = in_order("dp", middle[...], held_dp)
 
 
+def gather_and_sum_body(n, cuts, x_ref, gains, o_ref, total, *refs):
+    ring = Ring(n, cuts, x_ref, o_ref, refs[:3])
+    middle, held_heads, hs, hr, held_dp, ds, dr = refs[3:]
+    first = Total("heads", gains, held_heads, (hs, hr))
+    second = Total("dp", middle, held_dp, (ds, dr))
+    greet(first.names + second.names)
+    first.begin()
+    ring.begin()
+    first.end()
+    middle[...] = in_order("heads", gains[...], held_heads)
+    second.begin()
+    ring.run()
+    second.end()
+    total[...] = in_order("dp", middle[...], held_dp)
+    ring.end()
+
+
+def gather_and_sum(x, gains, n, dp, number, cuts=2):
+    rows, columns = x.shape
+    cuts = min(cuts, rows // 16)
+    return pl.pallas_call(
+        functools.partial(gather_and_sum_body, n, cuts),
+        out_shape=(
+            jax.ShapeDtypeStruct((n * rows, columns), x.dtype),
+            jax.ShapeDtypeStruct(gains.shape, gains.dtype),
+        ),
+        in_specs=spaces(2, pltpu.VMEM),
+        out_specs=(pl.BlockSpec(memory_space=pl.ANY), pl.BlockSpec(memory_space=pltpu.VMEM)),
+        scratch_shapes=Ring.scratch(n, cuts)
+        + [pltpu.VMEM(gains.shape, gains.dtype)]
+        + Total.scratch(n, gains.shape)
+        + Total.scratch(dp, gains.shape),
+        compiler_params=pltpu.CompilerParams(
+            collective_id=number, has_side_effects=True, vmem_limit_bytes=16 << 20
+        ),
+        cost_estimate=cost(35.0),
+        name="gather_and_sum",
+    )(x, gains)
+
+
 def sum_all(x, n, dp, number):
     return pl.pallas_call(
         sum_body,
@@ -676,6 +741,147 @@
         cost_estimate=cost(8.0),
         name=f"sum_all_{number}",
     )(x)
+
+
+NT = (((1,), (1,)), ((), ()))
+NN = (((1,), (0,)), ((), ()))
+
+
+def thrice(left, right, numbers):
+    terms = [(left[0], right[0]), (left[0], right[1]), (left[1], right[0])]
+    made = [lax.dot_general(*term, numbers, preferred_element_type=jnp.float32) for term in terms]
+    return made[0] + (made[1] + made[2])
+
+
+def turned(front, back, cosine, sines):
+    return front * cosine - back * sines, back * cosine + front * sines
+
+
+def keep_halves(value, pair, where):
+    pair[0][where], pair[1][where] = halves(value)
+
+
+def allowed_block(start, rows, reach, seg_rows, seg_columns):
+    row = start + lax.broadcasted_iota(jnp.int32, (rows, reach), 0)
+    column = lax.broadcasted_iota(jnp.int32, (rows, reach), 1)
+    return (seg_rows[start : start + rows, :] == seg_columns[:, :reach]) & (column <= row)
+
+
+def attend_body(latent_dim, rows, raw, packed, cosine, sines, seg_rows, seg_columns, mixed, query, lse, *split):
+    total, width = raw.shape
+    dim = (packed.shape[1] - latent_dim) // 2
+    half = dim // 2
+    scale = dim ** (-0.5)
+    key, value = split[:2], split[2:]
+    keep_halves(packed[:, latent_dim : latent_dim + dim], key, (slice(None), slice(None)))
+    keep_halves(packed[:, latent_dim + dim :], value, (slice(None), slice(None)))
+    for start in range(0, total, rows):
+        here = slice(start, start + rows)
+        reach = start + rows
+        allowed = allowed_block(start, rows, reach, seg_rows, seg_columns)
+        for head in range(width // dim):
+            at = head * dim
+            front, back = turned(
+                raw[here, at : at + half], raw[here, at + half : at + dim], cosine[here, :], sines[here, :]
+            )
+            query[here, at : at + half] = front
+            query[here, at + half : at + dim] = back
+            own = halves(query[here, at : at + dim])
+            scores = thrice(own, [ref[:reach, :] for ref in key], NT) * scale
+            scores = jnp.where(allowed, scores, -1e30)
+            top = jnp.max(scores, axis=1, keepdims=True)
+            expo = jnp.exp(scores - top)
+            denom = jnp.sum(expo, axis=1, keepdims=True)
+            made = thrice(halves(expo), [ref[:reach, :] for ref in value], NN)
+            mixed[here, at : at + dim] = made / denom
+            lse[here, head * 128 : head * 128 + 128] = jnp.broadcast_to(top + jnp.log(denom), (rows, 128))
+
+
+def attend(raw, packed, cosine, sines, seg_rows, seg_columns, latent_dim):
+    total, width = raw.shape
+    dim = (packed.shape[1] - latent_dim) // 2
+    shape = jax.ShapeDtypeStruct
+    return pl.pallas_call(
+        functools.partial(attend_body, latent_dim, 256),
+        out_shape=(
+            shape(raw.shape, jnp.float32),
+            shape(raw.shape, jnp.float32),
+            shape((total, width // dim * 128), jnp.float32),
+        ),
+        in_specs=spaces(6, pltpu.VMEM),
+        out_specs=tuple(spaces(3, pltpu.VMEM)),
+        scratch_shapes=[pltpu.VMEM((total, dim), jnp.bfloat16)] * 4,
+        compiler_params=pltpu.CompilerParams(vmem_limit_bytes=ATTEND_LIMIT),
+        cost_estimate=cost(14.0),
+        name="attend",
+    )(raw, packed, cosine, sines, seg_rows, seg_columns)
+
+
+def attend_back_body(
+    latent_dim, rows, query, packed, cosine, sines, seg_rows, seg_columns, lse, mixed, d_mixed, up, d_raw, out, *split
+):
+    total, width = query.shape
+    dim = (packed.shape[1] - latent_dim) // 2
+    half = dim // 2
+    scale = dim ** (-0.5)
+    key, value, weight, made = split[:2], split[2:4], split[4:6], split[6:]
+    every = (slice(None), slice(None))
+    keep_halves(packed[:, latent_dim : latent_dim + dim], key, every)
+    keep_halves(packed[:, latent_dim + dim :], value, every)
+    keep_halves(up[...], weight, every)
+    out[:, latent_dim:] = jnp.zeros((total, 2 * dim), jnp.float32)
+    for start in range(0, total, rows):
+        here = slice(start, start + rows)
+        reach = start + rows
+        allowed = allowed_block(start, rows, reach, seg_rows, seg_columns)
+        for head in range(width // dim):
+            at = head * dim
+            own = halves(query[here, at : at + dim])
+            upstream = d_mixed[here, at : at + dim]
+            grad = halves(upstream)
+            scores = thrice(own, [ref[:reach, :] for ref in key], NT) * scale
+            scores = jnp.where(allowed, scores, -1e30)
+            probs = jnp.exp(scores - lse[here, head * 128 : head * 128 + 1])
+            d_probs = thrice(grad, [ref[:reach, :] for ref in value], NT)
+            delta = jnp.sum(upstream * mixed[here, at : at + dim], axis=1, keepdims=True)
+            d_scores = probs * (d_probs - delta) * scale
+            out[:reach, latent_dim + dim :] += thrice(halves(probs.T), grad, NN)
+            out[:reach, latent_dim : latent_dim + dim] += thrice(halves(d_scores.T), own, NN)
+            d_query = thrice(halves(d_scores), [ref[:reach, :] for ref in key], NN)
+            front, back = turned(d_query[:, :half], d_query[:, half:], cosine[here, :], -sines[here, :])
+            for piece, off in ((front, at), (back, at + half)):
+                d_raw[here, off : off + half] = piece
+                keep_halves(piece, made, (slice(None), slice(off, off + half)))
+        out[here, :latent_dim] = thrice([ref[...] for ref in made], [ref[...] for ref in weight], NT)
+
+
+def attend_back(query, packed, cosine, sines, seg_rows, seg_columns, lse, mixed, d_mixed, up, latent_dim):
+    total, width = query.shape
+    dim = (packed.shape[1] - latent_dim) // 2
+    shape = jax.ShapeDtypeStruct
+    rows = 256
+    return pl.pallas_call(
+        functools.partial(attend_back_body, latent_dim, rows),
+        out_shape=(shape(query.shape, jnp.float32), shape(packed.shape, jnp.float32)),
+        in_specs=spaces(10, pltpu.VMEM),
+        out_specs=tuple(spaces(2, pltpu.VMEM)),
+        scratch_shapes=[pltpu.VMEM((total, dim), jnp.bfloat16)] * 4
+        + [pltpu.VMEM(up.shape, jnp.bfloat16)] * 2
+        + [pltpu.VMEM((rows, width), jnp.bfloat16)] * 2,
+        compiler_params=pltpu.CompilerParams(vmem_limit_bytes=ATTEND_LIMIT),
+        cost_estimate=cost(30.0),
+        name="attend_back",
+    )(query, packed, cosine, sines, seg_rows, seg_columns, lse, mixed, d_mixed, up)
+
+
+def rope_tables(position, head_dim):
+    half_dim = head_dim // 2
+    frequency = ROPE_BASE ** (-jnp.arange(half_dim, dtype=jnp.float32) / half_dim)
+    angles = position.astype(jnp.float32)[:, None] * frequency[None, :]
+    return jnp.cos(angles), jnp.sin(angles)
+
+
+ATTEND_LIMIT = 58 << 20
 
 
 def matmul_high(left, right):
@@ -765,11 +971,9 @@
     model_dim = block_input.shape[1]
     latent_dim = query_down.shape[1]
     head_dim = key_value.shape[1] // 2
-    local_heads = query_up.shape[1] // head_dim
     heads_count = lax.axis_size("heads")
     dp_count = lax.axis_size("dp")
     group_rows = tok_rows * heads_count
-    scale = head_dim ** (-0.5)
     group_index = jnp.arange(group_rows, dtype=jnp.int32)
     segment, position = layout(lengths[0], group_index)
     local_position = lax.dynamic_slice_in_dim(
@@ -804,43 +1008,19 @@
     turned_upper = lax.all_gather(upper_in.T, "dp", axis=1, tiled=True)
     wide_lower = lax.all_gather(lower_in, "dp", axis=1, tiled=True)
     latent_all = packed_all[:, :latent_dim]
-    key_all = packed_all[:, latent_dim : latent_dim + head_dim]
-    value_all = packed_all[:, latent_dim + head_dim :]
-    query_rot = rotate(
-        matmul_high(latent_all, wide_up).reshape(group_rows, local_heads, head_dim), position, 1.0
-    )
-    block_rows = min(512, group_rows)
-    n_blocks = group_rows // block_rows
-    query_blocks = query_rot.reshape(n_blocks, block_rows, local_heads, head_dim)
-    index_blocks = group_index.reshape(n_blocks, block_rows)
-    segment_blocks = segment.reshape(n_blocks, block_rows)
-
-    def block_scores(query_block, row_block, seg_block):
-        scores = jnp.einsum("qhd,kd->hqk", query_block, key_all, precision=HIGH) * scale
-        allowed = (seg_block[:, None] == segment[None, :]) & (
-            group_index[None, :] <= row_block[:, None]
-        )
-        return jnp.where(allowed[None], scores, -1e30)
-
-    def forward_block(inputs):
-        query_block, row_block, seg_block = inputs
-        scores = block_scores(query_block, row_block, seg_block)
-        row_max = jnp.max(scores, axis=2, keepdims=True)
-        expo = jnp.exp(scores - row_max)
-        denom = jnp.sum(expo, axis=2, keepdims=True)
-        mixed_block = jnp.einsum("hqk,kd->qhd", expo / denom, value_all, precision=HIGH)
-        return (mixed_block, (row_max + jnp.log(denom))[..., 0])
-
-    mixed_blocks, lse_blocks = lax.map(forward_block, (query_blocks, index_blocks, segment_blocks))
-    mixed_heads = mixed_blocks.reshape(group_rows, local_heads * head_dim)
+    cosine, sines = rope_tables(position, head_dim)
+    seg_rows, seg_columns = segment[:, None], segment[None, :]
+    mixed_heads, query_rot, lse = attend(
+        matmul_high(latent_all, wide_up), packed_all, cosine, sines, seg_rows, seg_columns, latent_dim
+    )
     middle = block_input + ring_scatter(matmul_high(mixed_heads, wide_merge), heads_count, 2)
     inv_two = lax.rsqrt(jnp.mean(middle * middle, axis=1, keepdims=True) + EPS_NORM)
     normed_two = middle * inv_two
     hidden_two = normed_two * gain_ffn
     inside = group_rows <= 1024
 
-    def job(form, lefts, rights, tile):
-        return [Job(form, lefts, rights, tile)] if inside else []
+    def job(*what):
+        return [Job(*what)] if inside else []
 
     made = ring_gather(hidden_two, heads_count, 3, job("nt", [grad_all], [wide_lower], 256))
     hidden_all, d_activ = made if inside else (made, matmul_high(grad_all, wide_lower.T))
@@ -859,70 +1039,54 @@
             4,
             job("nn", [d_gate_pre, d_up_pre], [turned_gate, turned_upper], 128),
         )
-        d_hidden_two, grad_gate, grad_lower = ring_scatter(
+        d_hidden_two, grad_both = ring_scatter(
             part_two,
             heads_count,
             6,
-            job("tn", [hidden_all], [d_gate_pre], 256) + job("tn", [grad_all], [activ], 256),
+            job("tn", [hidden_all], [d_gate_pre], 256, True) + job("tn", [grad_all], [activ], 256, True),
         )
     else:
         part_output = ring_scatter(part_output, heads_count, 4)
         part_two = matmul_high(d_gate_pre, turned_gate) + matmul_high(d_up_pre, turned_upper)
         d_hidden_two = ring_scatter(part_two, heads_count, 6)
-        grad_gate = matmul_high(d_gate_pre.T, hidden_all)
-        grad_lower = matmul_high(activ.T, grad_all)
+        grad_both = jnp.concatenate(
+            [matmul_high(d_gate_pre.T, hidden_all), matmul_high(activ.T, grad_all)], axis=0
+        )
     block_output = middle + part_output
-    grad_gate = owned(grad_gate, 1)
+    grad_both = owned(grad_both, 1)
     d_normed_mid, grad_gain_ffn = norm_back(d_hidden_two, normed_two, inv_two, gain_ffn)
     d_middle = output_grad + d_normed_mid
     made = ring_gather(d_middle, heads_count, 7, job("tn", [hidden_all], [d_up_pre], 256))
     middle_all, grad_upper = made if inside else (made, matmul_high(d_up_pre.T, hidden_all))
-    middle_all, grad_gate, grad_lower = lax.optimization_barrier((middle_all, grad_gate, grad_lower))
-    grad_lower = owned(grad_lower, 1)
-    d_mixed = matmul_high(middle_all, wide_merge.T).reshape(
-        n_blocks, block_rows, local_heads, head_dim
-    )
-
-    def backward_block(running, inputs):
-        query_block, row_block, seg_block, grad_block, out_block, lse_block = inputs
-        scores = block_scores(query_block, row_block, seg_block)
-        probs = jnp.exp(scores - lse_block[..., None])
-        d_probs = jnp.einsum("qhd,kd->hqk", grad_block, value_all, precision=HIGH)
-        delta = jnp.sum(grad_block * out_block, axis=2)
-        d_scores = probs * (d_probs - delta.T[:, :, None])
-        d_query = jnp.einsum("hqk,kd->qhd", d_scores, key_all, precision=HIGH) * scale
-        d_key = jnp.einsum("hqk,qhd->kd", d_scores, query_block, precision=HIGH) * scale
-        d_value = jnp.einsum("hqk,qhd->kd", probs, grad_block, precision=HIGH)
-        return ((running[0] + d_key, running[1] + d_value), d_query)
-
-    zero_rows = jnp.zeros((group_rows, head_dim), jnp.float32)
-    (d_key_sum, d_value_sum), d_query_blocks = lax.scan(
-        backward_block,
-        (zero_rows, zero_rows),
-        (query_blocks, index_blocks, segment_blocks, d_mixed, mixed_blocks, lse_blocks),
-    )
-    d_query_pre = rotate(
-        d_query_blocks.reshape(group_rows, local_heads, head_dim), position, -1.0
-    ).reshape(group_rows, local_heads * head_dim)
-    d_latent_all = matmul_high(d_query_pre, wide_up.T)
-    packed_part = jnp.concatenate([d_latent_all, d_key_sum, d_value_sum], axis=1)
-    packed_part, grad_lower, grad_upper = lax.optimization_barrier((packed_part, grad_lower, grad_upper))
+    d_mixed = matmul_high(middle_all, wide_merge.T)
+    d_query_pre, packed_part = attend_back(
+        query_rot,
+        packed_all,
+        cosine,
+        sines,
+        seg_rows,
+        seg_columns,
+        lse,
+        mixed_heads,
+        d_mixed,
+        wide_up,
+        latent_dim,
+    )
+    packed_part, grad_both, grad_upper = lax.optimization_barrier((packed_part, grad_both, grad_upper))
+    grad_gate, grad_lower = jnp.split(grad_both, 2, axis=0)
     grad_upper = owned(grad_upper, 1)
     if inside:
         packed_grad, grad_merge, grad_up = ring_scatter(
             packed_part,
             heads_count,
             8,
-            job("tn", [middle_all], [mixed_heads], 256) + job("tn", [d_query_pre], [latent_all], 256),
+            job("tn", [middle_all], [mixed_heads], 256) + job("tn", [d_query_pre], [(packed_all, jax.ShapeDtypeStruct(latent_all.shape, jnp.float32))], 256),
         )
     else:
         packed_grad = ring_scatter(packed_part, heads_count, 8)
         grad_merge = matmul_high(mixed_heads.T, middle_all)
         grad_up = matmul_high(latent_all.T, d_query_pre)
-    packed_grad, grad_merge, grad_upper = lax.optimization_barrier((packed_grad, grad_merge, grad_upper))
-    grad_merge = owned(grad_merge, 1)
-    grad_up, grad_merge = lax.optimization_barrier((grad_up, grad_merge))
-    grad_up = owned(grad_up, 0)
+    packed_grad, grad_upper = lax.optimization_barrier((packed_grad, grad_upper))
     d_latent = packed_grad[:, :latent_dim]
     d_key_local = packed_grad[:, latent_dim : latent_dim + head_dim]
     d_value_local = packed_grad[:, latent_dim + head_dim :]
@@ -930,14 +1094,20 @@
     d_latent_raw, grad_gain_query = norm_back(d_latent, latent_hat, inv_query, gain_query)
     raw = jnp.concatenate([d_latent_raw, d_pair], axis=1)
     raw_all = dp_gather(raw, dp_count, 11)
+    raw_all, grad_merge, grad_up = lax.optimization_barrier((raw_all, grad_merge, grad_up))
+    grad_up = owned(grad_up, 0)
     part_shared = matmul_high(hidden_turn.T, raw_all)
     d_hidden_turn = matmul_high(raw_all, jnp.concatenate([query_down, key_value], axis=1).T)
     shared_cut, d_hidden_one = scatter_and_turn(part_shared, d_hidden_turn, heads_count, dp_count, 9)
-    shared = ring_gather(shared_cut, heads_count, 10)
     d_normed_in, grad_gain_attn = norm_back(d_hidden_one, normed_one, inv_one, gain_attn)
     input_grad = d_middle + d_normed_in
     grad_gains = jnp.concatenate([grad_gain_attn, grad_gain_query, grad_gain_ffn])
-    gains_total = sum_all(grad_gains.reshape(-1, 128), heads_count, dp_count, 12).reshape(-1)
+    shared_cut, grad_merge, grad_up = lax.optimization_barrier((shared_cut, grad_merge, grad_up))
+    grad_merge = owned(grad_merge, 1)
+    shared, gains_total = gather_and_sum(
+        shared_cut, grad_gains.reshape(-1, 128), heads_count, dp_count, 10
+    )
+    gains_total = gains_total.reshape(-1)
     values = (
         norm_gains,
         query_down,

time: 1100 us -> 983 us (0.89)
  matrix products: 149 us -> 92.9 us
  local copies, waits for them, and re-layouts: 67 us -> 16.6 us
  other arithmetic: 86.8 us -> 71.5 us
  Pallas kernels: 755 us -> 768 us
    pallas_call x0 -> x3, Pallas kernels: none -> 75.9 us  [the longest x1 39.2 us: gather_and_sum(): pl.pallas_call(functools.partial(gather_and_sum_body, n, cuts), out_shape...]
    dot_general x14 -> x0, matrix products: 53.7 us -> none  [the longest x2 14.4 us: backward_block(): jnp.einsum('hqk,qhd->kd', d_scores, query_block, precision=HIGH) * scale]
    pallas_call x4 -> x3, Pallas kernels: 257 us -> 225 us  [ring_gather(): pl.pallas_call(functools.partial(gather_body, n, cuts, plan), out_shape=(...]
    unnamed x180 -> x114, local copies, waits for them, and re-layouts: 37 us -> 10.7 us
    pallas_call x1, Pallas kernels: 40.8 us -> 22.9 us  [dp_gather(): pl.pallas_call(functools.partial(spread_body, dp), out_shape=jax.ShapeDty...]
    pallas_call x2 -> x1, Pallas kernels: 21.6 us -> 10.2 us  [sum_all(): pl.pallas_call(sum_body, out_shape=jax.ShapeDtypeStruct(x.shape, x.dtype)...]
    dot_general x11 -> x10, matrix products: 95.8 us -> 92.9 us  [matmul_high(): jnp.dot(left, right, precision=HIGH, preferred_element_type=jnp.float32)]
  transfers between devices with their start and end apart: 10 -> 9, of which waited for: 1 -> 0; matrix products, arithmetic and copies ran while one was open for 20% -> 11% of each run, Pallas kernels for 45% -> 49%
where the time goes in v4:
time: 983 us; the launch traced here: 977 us
  Pallas kernels  768 us (78%)
  matrix products  92.9 us (9%)
  other arithmetic  71.5 us (7%)
  between operations  25.3 us (3%)
  local copies, waits for them, and re-layouts  16.6 us (2%)
    pallas_call x4, Pallas kernels, ring_scatter(): pl.pallas_call(functools.partial(scatter_body, n, cuts, plan), out_shape=...  311 us
    pallas_call x3, Pallas kernels, ring_gather(): pl.pallas_call(functools.partial(gather_body, n, cuts, plan), out_shape=(...  225 us
    dot_general x10, matrix products, matmul_high(): jnp.dot(left, right, precision=HIGH, preferred_element_type=jnp.float32)  92.9 us
    pallas_call x1, Pallas kernels, opening(): pl.pallas_call(functools.partial(opening_body, n, dp, cuts), out_shape=(f...  87.5 us
    pallas_call x1, Pallas kernels, gather_and_sum(): pl.pallas_call(functools.partial(gather_and_sum_body, n, cuts), out_shape...  39.2 us
    pallas_call x1, Pallas kernels, scatter_and_turn(): pl.pallas_call(functools.partial(turn_body, n, dp, cuts), out_shape=(jax....  35.7 us
    reduce_sum x7, other arithmetic, on_device(): jnp.sum(stepped[slot][2] * stepped[slot][2])  31.2 us
    pallas_call x1, Pallas kernels, attend_back(): pl.pallas_call(functools.partial(attend_back_body, latent_dim, rows), out...  25.4 us
  transfers between devices with their start and end apart: 9, of which 0 were waited for; matrix products, arithmetic and copies ran while one was open for 11% of the time, Pallas kernels for 49%

profile of v4, /device:TPU:0, one launch (start us, length us, event | category | flops | bytes accessed | tf_op | source)
XLA Modules:
  0.0 977.1 jit_solution(9393100110526619228)
XLA Ops:
  11.7 87.5 %opening.1 = (f32[1024,2048]{1,0:T(8,128)}, f32[2048,1024]{1,0:T(8,128)}, f32[2048,512]{1,0:T(8,128)}, f32[512,512]{1,0:T(8,128)}) custom-call(f32[128,2048]{1,0:T(8,128)} %grad.1, f32[512,1024]{1,0:T(8,128)} %down.1, f32[512,512]{1,0:T(8,128)} %pair.1, f32[128,2048]{1,0:T(8,128)} %multiply_multiply_fusion.8.hidden), custom_call_target="tpu_custom_call" | custom-call | bytes 240000000 | tf_op jit(solution)/shard_map/opening/pallas_call | solution.py:478
  104.7 6.6 multiply_reduce_fusion.22
  112.2 63.2 %ring_gather_1.1.packed.refs_3_ = f32[1024,1536]{1,0:T(8,128)S(1)} custom-call(f32[128,1536]{1,0:T(8,128)S(1)} %pad_maximum_fusion.x_ref), custom_call_target="tpu_custom_call" | custom-call | bytes 168750000 | tf_op jit(solution)/shard_map/ring_gather_1/pallas_call | solution.py:441
  183.5 8.3 fusion.raw
  191.8 11.3 %attend.1 = (f32[1024,512]{1,0:T(8,128)}, f32[1024,512]{1,0:T(8,128)}, f32[1024,256]{1,0:T(8,128)}) custom-call(f32[1024,512]{1,0:T(8,128)} %fusion.raw, f32[1024,1536]{1,0:T(8,128)} %copy-done, f32[1024,128]{1,0:T(8,128)} %get-tuple-element.243.cosine, f32[1024,128]{1,0:T(8,128)} %get-tuple-element.242.sines, s32[1024,1]{1,0:T(8,128)} %copy.83.seg_rows, ...), custom_call_target="tpu_custom_call" | custom-call | bytes 42000000 | tf_op jit(solution)/shard_map/attend/pallas_call | solution.py:804
  203.1 9.7 fusion.44.x_ref
  212.8 81.2 %ring_scatter_2.1 = f32[128,2048]{1,0:T(8,128)S(1)} custom-call(f32[1024,2048]{1,0:T(8,128)S(1)} %fusion.44.x_ref), custom_call_target="tpu_custom_call" | custom-call | bytes 225000000 | tf_op jit(solution)/shard_map/ring_scatter_2/pallas_call | solution.py:595
  296.4 81.2 %ring_gather_3.1 = (f32[1024,2048]{1,0:T(8,128)}, f32[1024,704]{1,0:T(8,128)}) custom-call(f32[128,2048]{1,0:T(8,128)} %multiply_multiply_fusion.7.x_ref, f32[1024,2048]{1,0:T(8,128)} %get-tuple-element.94.refs_0_.refs_2_, f32[704,2048]{1,0:T(8,128)} %all-gather.10.cloned.1.call-done.refs_1_), custom_call_target="tpu_custom_call" | custom-call | bytes 225000000 | tf_op jit(solution)/shard_map/ring_gather_3/pallas_call | solution.py:441
  377.6 16.3 %fusion.45 = f32[1024,704]{1,0:T(8,128)} fusion(f32[1024,2048]{1,0:T(8,128)} %get-tuple-element.96.refs_0_, f32[704,2048]{1,0:T(8,128)} %all-gather.14.cloned.1.call-done.refs_3_), kind=kOutput, calls=%fused_computation.140 | convolution fusion | flops 8858370048 | bytes 17039360 | tf_op jit(solution)/shard_map/dot_general | solution.py:888
  393.9 17.6 %fusion.13 = (f32[1024,704]{1,0:T(8,128)}, f32[1024,704]{1,0:T(8,128)}, f32[1024,704]{1,0:T(8,128)S(1)}) fusion(f32[1024,704]{1,0:T(8,128)S(1)} %copy-done.55, f32[1024,704]{1,0:T(8,128)} %fusion.45, f32[1024,2048]{1,0:T(8,128)} %get-tuple-element.96.refs_0_, f32[704,2048]{1,0:T(8,128)} %all-gather.12.cloned.1.call-done.refs_2_), kind=kOutput, calls=%fused_computation.69 | convolution fusion | flops 8867020800 | bytes 28573696 | tf_op jit(solution)/shard_map/dot_general | solution.py:888
  411.5 12.7 %fusion.46.x_ref = f32[1024,2048]{1,0:T(8,128)} fusion(f32[1024,704]{1,0:T(8,128)S(1)} %get-tuple-element.217.refs_3_, f32[704,2048]{1,0:T(8,128)S(1)} %copy-done.26), kind=kOutput, calls=%fused_computation.141 | convolution fusion | flops 8858370048 | bytes 17039360 | tf_op jit(solution)/shard_map/dot_general | solution.py:888
  424.2 83.9 %ring_scatter_4.1 = (f32[128,2048]{1,0:T(8,128)}, f32[1024,2048]{1,0:T(8,128)}) custom-call(f32[1024,2048]{1,0:T(8,128)} %fusion.46.x_ref, f32[1024,704]{1,0:T(8,128)} %get-tuple-element.216.refs_0_.refs_1_, f32[1024,704]{1,0:T(8,128)} %get-tuple-element.215.refs_1_, f32[704,2048]{1,0:T(8,128)} %all-gather.12.cloned.1.call-done.refs_2_, ...), custom_call_target="tpu_custom_call" | custom-call | bytes 225000000 | tf_op jit(solution)/shard_map/ring_scatter_4/pallas_call | solution.py:595
  508.1 83.0 %ring_scatter_6.1 = (f32[128,2048]{1,0:T(8,128)}, f32[1408,2048]{1,0:T(8,128)}) custom-call(f32[1024,2048]{1,0:T(8,128)} %get-tuple-element.101.x_ref, f32[1024,2048]{1,0:T(8,128)} %get-tuple-element.96.refs_0_, f32[1024,704]{1,0:T(8,128)} %get-tuple-element.216.refs_0_.refs_1_, f32[1024,2048]{1,0:T(8,128)} %get-tuple-element.94.refs_0_.refs_2_, ...), custom_call_target="tpu_custom_call" | custom-call | bytes 225000000 | tf_op jit(solution)/shard_map/ring_scatter_6/pallas_call | solution.py:595
  595.1 80.5 %ring_gather_7.1 = (f32[1024,2048]{1,0:T(8,128)}, f32[704,2048]{1,0:T(8,128)}) custom-call(f32[128,2048]{1,0:T(8,128)} %get-tuple-element.231.x_ref, f32[1024,2048]{1,0:T(8,128)} %get-tuple-element.96.refs_0_, f32[1024,704]{1,0:T(8,128)} %get-tuple-element.215.refs_1_), custom_call_target="tpu_custom_call" | custom-call | bytes 225000000 | tf_op jit(solution)/shard_map/ring_gather_7/pallas_call | solution.py:441
  675.6 10.5 %fusion.47.d_mixed = f32[1024,512]{1,0:T(8,128)} fusion(f32[1024,2048]{1,0:T(8,128)} %get-tuple-element.106.refs_0_, f32[512,2048]{1,0:T(8,128)S(1)} %copy-done.32), kind=kOutput, calls=%fused_computation.142 | convolution fusion | flops 6442450944 | bytes 14680064 | tf_op jit(solution)/shard_map/dot_general | solution.py:888
  686.1 25.4 %attend_back.1 = (f32[1024,512]{1,0:T(8,128)}, f32[1024,1536]{1,0:T(8,128)}) custom-call(f32[1024,512]{1,0:T(8,128)} %get-tuple-element.104.query, f32[1024,1536]{1,0:T(8,128)} %copy-done, f32[1024,128]{1,0:T(8,128)} %get-tuple-element.243.cosine, f32[1024,128]{1,0:T(8,128)} %get-tuple-element.242.sines, s32[1024,1]{1,0:T(8,128)} %copy.83.seg_rows, ...), custom_call_target="tpu_custom_call" | custom-call | bytes 90000000 | tf_op jit(solution)/shard_map/attend_back/pallas_call | solution.py:863
  713.2 63.0 %ring_scatter_8.1 = (f32[128,1536]{1,0:T(8,128)S(1)}, f32[512,2048]{1,0:T(8,128)}, f32[1024,512]{1,0:T(8,128)}) custom-call(f32[1024,1536]{1,0:T(8,128)} %get-tuple-element.110.x_ref, f32[1024,2048]{1,0:T(8,128)} %get-tuple-element.106.refs_0_, f32[1024,512]{1,0:T(8,128)S(1)} %copy-done.1, f32[1024,512]{1,0:T(8,128)} %get-tuple-element.111.refs_2_, ...), custom_call_target="tpu_custom_call" | custom-call | bytes 168750000 | tf_op jit(solution)/shard_map/ring_scatter_8/pallas_call | solution.py:595
  777.9 22.9 %dp_gather_11.1 = f32[512,1536]{1,0:T(8,128)} custom-call(f32[128,1536]{1,0:T(8,128)} %pad_maximum_fusion.1.x_ref), custom_call_target="tpu_custom_call" | custom-call | bytes 60000000 | tf_op jit(solution)/shard_map/dp_gather_11/pallas_call | solution.py:498
  808.7 35.7 %scatter_and_turn.1 = (f32[64,1536]{1,0:T(8,128)S(1)}, f32[128,2048]{1,0:T(8,128)S(1)}) custom-call(f32[512,1536]{1,0:T(8,128)S(1)} %fusion.48.x_ref, f32[512,512]{1,0:T(8,128)S(1)} %fusion.2.hidden), custom_call_target="tpu_custom_call" | custom-call | bytes 105000000 | tf_op jit(solution)/shard_map/scatter_and_turn/pallas_call | solution.py:624
  845.8 6.6 multiply_reduce_fusion.2
  866.6 39.2 %gather_and_sum.1 = (f32[512,1536]{1,0:T(8,128)S(1)}, f32[40,128]{1,0:T(8,128)S(1)}) custom-call(f32[64,1536]{1,0:T(8,128)S(1)} %get-tuple-element.122.x_ref, f32[40,128]{1,0:T(8,128)S(1)} %maximum_bitcast_fusion.gains), custom_call_target="tpu_custom_call" | custom-call | bytes 105000000 | tf_op jit(solution)/shard_map/gather_and_sum/pallas_call | solution.py:713
  909.1 5.1 multiply_reduce_fusion.10
  914.3 5.0 multiply_reduce_fusion
  933.9 10.2 %sum_all_13.1 = f32[8,128]{1,0:T(8,128)} custom-call(f32[8,128]{1,0:T(8,128)} %scatter.4.x_ref), custom_call_target="tpu_custom_call" | custom-call | bytes 24000000 | tf_op jit(solution)/shard_map/sum_all_13/pallas_call | solution.py:734
  (203 shorter events, 85.0 us)
Async XLA Ops:
  7.2 176.3 %all-gather.6.cloned.1.call-start = ((), (), s32[]{:S(2)}) async-start(), calls=%async_computation.4 | async-start | bytes 2621440 | tf_op jit(solution)/shard_map/all_gather | solution.py:994
  99.3 103.8 %all-gather.8.cloned.1.call-start = ((), (), s32[]{:S(2)}) async-start(), calls=%async_computation.5 | async-start | bytes 5242880 | tf_op jit(solution)/shard_map/all_gather | solution.py:995
  100.0 196.3 %all-gather.10.cloned.1.call-start = ((), (), s32[]{:S(2)}) async-start(), calls=%async_computation.6 | async-start | bytes 7208960 | tf_op jit(solution)/shard_map/all_gather | solution.py:1009
  104.5 74.9 %copy-start.50 = (s32[1024]{0:T(1024)}, s32[1024]{0:T(1024)S(1)}, u32[]{:S(2)}) copy-start(s32[1024]{0:T(1024)S(1)} %convert_reduce_fusion) | copy-start | bytes 12292
  178.0 199.5 %all-gather.14.cloned.1.call-start = ((), (), s32[]{:S(2)}) async-start(), calls=%async_computation.8 | async-start | bytes 7208960 | tf_op jit(solution)/shard_map/all_gather | solution.py:1008
  178.6 215.3 %all-gather.12.cloned.1.call-start = ((), (), s32[]{:S(2)}) async-start(), calls=%async_computation.7 | async-start | bytes 7208960 | tf_op jit(solution)/shard_map/all_gather | solution.py:1007
  179.2 532.4 %reduce-scatter.5.cloned.1.call-start = ((), (), s32[]{:S(2)}) async-start(), calls=%async_computation.9 | async-start | bytes 14417920 | tf_op jit(solution)/shard_map/reduce_scatter | solution.py:926
  212.8 81.3 %copy-start.6 = (f32[128,2048]{1,0:T(8,128)S(1)}, f32[128,2048]{1,0:T(8,128)}, u32[]{:S(2)}) copy-start(f32[128,2048]{1,0:T(8,128)} %param.29) | copy-start | bytes 3145732
  377.6 16.3 %copy-start.55 = (f32[1024,704]{1,0:T(8,128)S(1)}, f32[1024,704]{1,0:T(8,128)}, u32[]{:S(2)}) copy-start(f32[1024,704]{1,0:T(8,128)} %get-tuple-element.99) | copy-start | bytes 8650756
  393.9 17.6 %copy-start.26 = (f32[704,2048]{1,0:T(8,128)S(1)}, f32[704,2048]{1,0:T(8,128)}, u32[]{:S(2)}) copy-start(f32[704,2048]{1,0:T(8,128)} %all-gather.10.cloned.1.call-done.refs_1_) | copy-start | bytes 17301508
  411.5 12.7 %copy-start.33 = (f32[1024,704]{1,0:T(8,128)}, f32[1024,704]{1,0:T(8,128)S(1)}, u32[]{:S(2)}) copy-start(f32[1024,704]{1,0:T(8,128)S(1)} %get-tuple-element.217.refs_3_) | copy-start | bytes 8650756
  591.2 185.0 %reduce-scatter.7.cloned.1.call-start = ((), (), s32[]{:S(2)}) async-start(), calls=%async_computation.10 | async-start | bytes 7208960 | tf_op jit(solution)/shard_map/reduce_scatter | solution.py:926
  595.1 80.6 %copy-start.32 = (f32[512,2048]{1,0:T(8,128)S(1)}, f32[512,2048]{1,0:T(8,128)}, u32[]{:S(2)}) copy-start(f32[512,2048]{1,0:T(8,128)} %all-gather.8.cloned.1.call-done) | copy-start | bytes 12582916
  711.6 132.8 %reduce-scatter.9.cloned.1.call-start = ((), (), s32[]{:S(2)}) async-start(), calls=%async_computation.11 | async-start | bytes 2621440 | tf_op jit(solution)/shard_map/reduce_scatter | solution.py:926
  713.2 63.0 %copy-start.22 = (f32[128,1024]{1,0:T(8,128)S(1)}, f32[128,1024]{1,0:T(8,128)}, u32[]{:S(2)}) copy-start(f32[128,1024]{1,0:T(8,128)} %copy-done.21) | copy-start | bytes 1572868
  777.9 23.0 %copy-start.2 = (f32[512,1024]{1,0:T(8,128)S(1)}, f32[512,1024]{1,0:T(8,128)}, u32[]{:S(2)}) copy-start(f32[512,1024]{1,0:T(8,128)} %down.1) | copy-start | bytes 6291460
  777.9 23.0 %copy-start.9 = (f32[512,512]{1,0:T(8,128)S(1)}, f32[512,512]{1,0:T(8,128)}, u32[]{:S(2)}) copy-start(f32[512,512]{1,0:T(8,128)} %pair.1) | copy-start | bytes 3145732
  800.9 123.8 %reduce-scatter.11.cloned.1.call-start = ((), (), s32[]{:S(2)}) async-start(), calls=%async_computation.12 | async-start | bytes 5242880 | tf_op jit(solution)/shard_map/reduce_scatter | solution.py:926
  845.8 8.6 copy-start.39
  865.3 40.5 %copy-start.48 = (f32[5120]{0:T(1024)S(1)}, f32[5120]{0:T(1024)}, u32[]{:S(2)}) copy-start(f32[5120]{0:T(1024)} %param.32) | copy-start | bytes 61444
  865.3 40.5 %copy-start.53 = (f32[5120]{0:T(1024)S(1)}, f32[5120]{0:T(1024)}, u32[]{:S(2)}) copy-start(f32[5120]{0:T(1024)} %param.33) | copy-start | bytes 61444
  865.3 40.5 %copy-start.54 = (f32[5120]{0:T(1024)S(1)}, f32[5120]{0:T(1024)}, u32[]{:S(2)}) copy-start(f32[5120]{0:T(1024)} %param.34) | copy-start | bytes 61444
  924.7 32.1 %copy-start.14 = (f32[704,512]{1,0:T(8,128)S(1)}, f32[704,512]{1,0:T(8,128)}, u32[]{:S(2)}) copy-start(f32[704,512]{1,0:T(8,128)} %param.53) | copy-start | bytes 4325380
  945.7 14.2 %copy-start.51 = (f32[8,2]{0,1:T(2,128)}, f32[8,2]{0,1:T(2,128)S(1)}, u32[]{:S(2)}) copy-start(f32[8,2]{0,1:T(2,128)S(1)} %maximum_sqrt_fusion) | copy-start | bytes 196
  (42 other events, 158.7 us)
Sparse Core Ops, SparseCore 0:
  99.4 22.2 all-gather.5
  123.3 34.4 all-gather.7
  178.1 42.3 all-gather.9
  221.9 43.3 all-gather.13
  266.8 43.3 all-gather.11
  591.3 91.5 reduce-scatter.4
  711.7 54.3 reduce-scatter.6
  801.0 34.8 reduce-scatter.8
  844.6 43.8 reduce-scatter.10

commit v5 on v4

--- a/solution.py
+++ b/solution.py
@@ -286,10 +286,15 @@
             self.copy(step - 1, *part).wait_recv()
             self.copy(step, *part).start()
 
-    def end(self):
+    def received(self):
         for part in self.parts:
             self.copy(self.n - 2, *part).wait_recv()
 
+    def end(self):
+        self.received()
+        self.sent()
+
+    def sent(self):
         def sent(step, carry):
             for part in self.parts:
                 self.copy(step, *part).wait_send()
@@ -422,35 +427,165 @@
     return [pl.BlockSpec(memory_space=space)] * count
 
 
-def gather_body(n, cuts, plan, x_ref, *refs):
-    work = Work(plan, refs, 1)
-    ring = Ring(n, cuts, x_ref, work.first[0], work.rest)
+class Arrive:
+    def __init__(self, ring, rights, refs):
+        count = len(rights)
+        self.ring, self.sources, self.sinks = ring, rights, refs[:count]
+        self.buffer, self.stage = refs[count : count + 2]
+        self.split = [refs[count + 2 + 2 * k : count + 4 + 2 * k] for k in range(count)]
+        self.made = refs[count + 2 + 2 * count : count + 2 + 3 * count]
+        self.load_sem, self.stage_sem, self.out_sem = refs[count + 2 + 3 * count :]
+
+    def load(self, unit):
+        height = self.buffer.shape[1]
+        source = self.sources[unit // 4].at[pl.ds(unit % 4 * height, height)]
+        return pltpu.make_async_copy(source, self.buffer.at[unit % 2], self.load_sem.at[unit % 2])
+
+    def prepare(self):
+        units = 4 * len(self.sources)
+        for unit in range(units):
+            if unit + 1 < units:
+                self.load(unit + 1).start()
+            self.load(unit).wait()
+            height = self.buffer.shape[1]
+            high, low = self.split[unit // 4]
+
+            def part(index, carry, unit=unit, high=high, low=low, height=height):
+                here = pl.multiple_of(index * 16, 16)
+                rows = pl.ds(pl.multiple_of(unit % 4 * height + index * 16, 16), 16)
+                high[rows, :], low[rows, :] = halves(self.buffer[unit % 2, pl.ds(here, 16), :])
+                return carry
+
+            lax.fori_loop(0, height // 16, part, 0)
+
+    def places(self, index):
+        rows = self.ring.rows
+        half = rows // 2
+        return [
+            (pl.ds(pl.multiple_of(self.ring.at(-index) * rows, 8), half), pl.ds(0, half)),
+            (pl.ds(pl.multiple_of(self.ring.at(index) * rows + half, 8), half), pl.ds(half, half)),
+        ]
+
+    def outgoing(self, index):
+        return [
+            pltpu.make_async_copy(made.at[index % 2, here], sink.at[there], self.out_sem.at[k, index % 2, way])
+            for k, (made, sink) in enumerate(zip(self.made, self.sinks))
+            for way, (there, here) in enumerate(self.places(index))
+        ]
+
+    def take(self, index, own):
+        if own:
+            self.stage[...] = self.ring.x[...]
+        else:
+            copies = [
+                pltpu.make_async_copy(self.ring.o.at[there], self.stage.at[here], self.stage_sem.at[way])
+                for way, (there, here) in enumerate(self.places(index))
+            ]
+            for copy in copies:
+                copy.start()
+            for copy in copies:
+                copy.wait()
+
+    def work(self, index):
+        def free():
+            for copy in self.outgoing(index - 2):
+                copy.wait()
+
+        pl.when(index >= 2)(free)
+        high, low = halves(self.stage[...])
+        for made, split in zip(self.made, self.split):
+            made[index % 2] = thrice((high, low), (split[0][...], split[1][...]), NT)
+        for copy in self.outgoing(index):
+            copy.start()
+
+    def step(self, index):
+        @pl.when(index == 0)
+        def _():
+            self.take(index, True)
+
+        @pl.when(index > 0)
+        def _():
+            self.take(index, False)
+
+        self.work(index)
+
+    def end(self):
+        for index in (self.ring.n - 2, self.ring.n - 1):
+            for copy in self.outgoing(index):
+                copy.wait()
+
+    @staticmethod
+    def outputs(n, x, rights):
+        return [jax.ShapeDtypeStruct((n * x.shape[0], right.shape[0]), jnp.float32) for right in rights]
+
+    @staticmethod
+    def scratch(n, x, rights):
+        if not rights:
+            return []
+        height, columns = rights[0].shape
+        made = [pltpu.VMEM((2, height // 4, columns), jnp.float32), pltpu.VMEM(x.shape, jnp.float32)]
+        for right in rights:
+            made += [pltpu.VMEM(right.shape, jnp.bfloat16)] * 2
+        made += [pltpu.VMEM((2, x.shape[0], right.shape[0]), jnp.float32) for right in rights]
+        return made + [
+            pltpu.SemaphoreType.DMA((2,)),
+            pltpu.SemaphoreType.DMA((2,)),
+            pltpu.SemaphoreType.DMA((len(rights), 2, 2)),
+        ]
+
+
+def gather_body(n, cuts, plan, count, x_ref, *refs):
+    rights, refs = refs[:count], refs[count:]
+    work = Work(plan, refs, 1 + count)
+    rest = list(work.rest)
+    ring = Ring(n, cuts, x_ref, work.first[0], rest[:3])
+    arrive = Arrive(ring, rights, work.first[1:] + rest[3:]) if count else None
     work.load()
+    if count:
+        arrive.load(0).start()
     greet(ring.sides)
     ring.begin()
+    if count:
+        arrive.prepare()
     work.ready()
-    ring.run(functools.partial(work.share, n - 1))
-    ring.end()
+
+    def share(step):
+        if count:
+            arrive.step(step)
+        work.share(n - 1, step)
+
+    ring.run(share)
+    ring.received()
+    if count:
+        arrive.take(n - 1, False)
+        arrive.work(n - 1)
+    ring.sent()
     work.end()
-
-
-def ring_gather(x, n, number, jobs=(), cuts=2):
+    if count:
+        arrive.end()
+
+
+def ring_gather(x, n, number, jobs=(), rights=(), cuts=2):
     rows, columns = x.shape
     cuts = min(cuts, rows // 16)
     plan = [job.bare() for job in jobs]
+    rights = list(rights)
+    made = [jax.ShapeDtypeStruct((n * rows, columns), x.dtype), *Arrive.outputs(n, x, rights)]
     result = pl.pallas_call(
-        functools.partial(gather_body, n, cuts, plan),
-        out_shape=(jax.ShapeDtypeStruct((n * rows, columns), x.dtype), *Work.outputs(jobs)),
-        in_specs=spaces(1, pltpu.VMEM) + spaces(len(Work.operands(jobs))),
-        out_specs=tuple(spaces(1 + len(Work.outputs(jobs)))),
-        scratch_shapes=Work.scratch(jobs) + Ring.scratch(n, cuts),
+        functools.partial(gather_body, n, cuts, plan, len(rights)),
+        out_shape=(*made, *Work.outputs(jobs)),
+        in_specs=spaces(1, pltpu.VMEM) + spaces(len(rights) + len(Work.operands(jobs))),
+        out_specs=tuple(spaces(len(made) + len(Work.outputs(jobs)))),
+        scratch_shapes=Work.scratch(jobs) + Ring.scratch(n, cuts) + Arrive.scratch(n, x, rights),
         compiler_params=pltpu.CompilerParams(
-            collective_id=number, has_side_effects=True, vmem_limit_bytes=ATTEND_LIMIT if jobs else limit(jobs, x.shape)
+            collective_id=number,
+            has_side_effects=True,
+            vmem_limit_bytes=(60 << 20) if jobs or rights else limit(jobs, x.shape),
         ),
         cost_estimate=cost(75.0 * columns / 2048),
         name=f"ring_gather_{number}",
-    )(x, *Work.operands(jobs))
-    return result if jobs else result[0]
+    )(x, *rights, *Work.operands(jobs))
+    return result if jobs or rights else result[0]
 
 
 def opening_body(n, dp, cuts, grad, down, pair, hidden, grad_all, wide_down, wide_pair, hidden_turn, *sems):
@@ -931,11 +1066,98 @@
     second_new = BETA_TWO * second + (1.0 - BETA_TWO) * grad * grad
     update = (
         first_new
-        / (1.0 - BETA_ONE**STEP_COUNT)
-        / (jnp.sqrt(second_new / (1.0 - BETA_TWO**STEP_COUNT)) + ADAM_EPS)
+        * (1.0 / (1.0 - BETA_ONE**STEP_COUNT))
+        / (jnp.sqrt(second_new * (1.0 / (1.0 - BETA_TWO**STEP_COUNT))) + ADAM_EPS)
         + DECAY * value
     )
     return (first_new, second_new, update)
+
+
+def chunk_of(rows):
+    return next(c for c in (64, 32, 16, 8) if rows % c == 0)
+
+
+def moments_body(slots, shares, offsets, count_grads, *refs):
+    count = len(slots)
+    values, firsts, seconds = refs[:count], refs[count : 2 * count], refs[2 * count : 3 * count]
+    grads = refs[3 * count : 3 * count + count_grads]
+    outs = refs[3 * count + count_grads : -1]
+    table = refs[-1]
+    row = lax.broadcasted_iota(jnp.int32, table.shape, 0)
+    lane = lax.broadcasted_iota(jnp.int32, table.shape, 1)
+    sums = jnp.zeros(table.shape, jnp.float32)
+    for k, slot in enumerate(slots):
+        height, width = values[k].shape
+        chunk = chunk_of(height)
+        which, offset, below = offsets[k]
+
+        def part(index, carry, k=k, chunk=chunk, width=width, which=which, offset=offset, below=below):
+            rows = pl.ds(pl.multiple_of(index * chunk, chunk), chunk)
+            under = pl.ds(pl.multiple_of(below + index * chunk, 8), chunk)
+            value = values[k][rows, :]
+            first, second, update = moments(
+                value, grads[which][under, offset : offset + width], firsts[k][rows, :], seconds[k][rows, :]
+            )
+            for out, made in zip(outs[3 * k : 3 * k + 3], (first, second, update)):
+                out[rows, :] = made
+
+            def folded(x):
+                return jnp.sum((x * x).reshape(chunk // 8, 8, width), axis=0)
+
+            return carry[0] + folded(value), carry[1] + folded(update)
+
+        zero = jnp.zeros((8, width), jnp.float32)
+        for at, square in enumerate(lax.fori_loop(0, height // chunk, part, (zero, zero))):
+            total = jnp.sum(jnp.sum(square, axis=1, keepdims=True), axis=0, keepdims=True) * shares[k]
+            sums += jnp.where((row == slot) & (lane == at), total, 0.0)
+    table[...] = sums
+
+
+def all_moments(slots, shares, offsets, values, firsts, seconds, grads):
+    shape = jax.ShapeDtypeStruct
+    made = pl.pallas_call(
+        functools.partial(moments_body, slots, shares, offsets, len(grads)),
+        out_shape=(
+            *[shape(value.shape, jnp.float32) for value in values for _ in range(3)],
+            shape((8, 128), jnp.float32),
+        ),
+        in_specs=spaces(3 * len(values) + len(grads), pltpu.VMEM),
+        out_specs=tuple(spaces(3 * len(values) + 1, pltpu.VMEM)),
+        compiler_params=pltpu.CompilerParams(vmem_limit_bytes=52 << 20),
+        cost_estimate=cost(12.0),
+        name=f"moments_{slots[0]}",
+    )(*values, *firsts, *seconds, *grads)
+    return [made[3 * k : 3 * k + 3] for k in range(len(values))], made[-1]
+
+
+def finish_body(count, table, *refs):
+    values, updates, outs, norms = refs[:count], refs[count : 2 * count], refs[2 * count : -1], refs[-1]
+    norms[...] = jnp.sqrt(table[...])
+    for k in range(count):
+        ratio = RATE * (norms[k : k + 1, 0:1] / norms[k : k + 1, 1:2])
+        height = values[k].shape[0]
+        chunk = chunk_of(height)
+
+        def part(index, carry, k=k, chunk=chunk, ratio=ratio):
+            rows = pl.ds(pl.multiple_of(index * chunk, chunk), chunk)
+            outs[k][rows, :] = values[k][rows, :] - ratio * updates[k][rows, :]
+            return carry
+
+        lax.fori_loop(0, height // chunk, part, 0)
+
+
+def finish(table, values, updates):
+    shape = jax.ShapeDtypeStruct
+    made = pl.pallas_call(
+        functools.partial(finish_body, len(values)),
+        out_shape=(*[shape(value.shape, jnp.float32) for value in values], shape(table.shape, jnp.float32)),
+        in_specs=spaces(2 * len(values) + 1, pltpu.VMEM),
+        out_specs=tuple(spaces(len(values) + 1, pltpu.VMEM)),
+        compiler_params=pltpu.CompilerParams(vmem_limit_bytes=48 << 20),
+        cost_estimate=cost(9.0),
+        name="finish",
+    )(table, *values, *updates)
+    return made[:-1], made[-1]
 
 
 def on_device(
@@ -1000,32 +1222,44 @@
     pair_local = matmul_high(hidden_one, wide_pair)
     key_local = rotate(pair_local[:, :head_dim], local_position, 1.0)
     value_local = pair_local[:, head_dim:]
-    packed_all = ring_gather(
-        jnp.concatenate([latent, key_local, value_local], axis=1), heads_count, 1
-    )
-    gate_in, upper_in, lower_in, packed_all = lax.optimization_barrier((gate_in, upper_in, lower_in, packed_all))
+    packed = jnp.concatenate([latent, key_local, value_local], axis=1)
+    lower_in, packed = lax.optimization_barrier((lower_in, packed))
+    wide_lower = lax.all_gather(lower_in, "dp", axis=1, tiled=True)
+    packed_all = ring_gather(packed, heads_count, 1)
+    gate_in, upper_in, packed_all = lax.optimization_barrier((gate_in, upper_in, packed_all))
     turned_gate = lax.all_gather(gate_in.T, "dp", axis=1, tiled=True)
     turned_upper = lax.all_gather(upper_in.T, "dp", axis=1, tiled=True)
-    wide_lower = lax.all_gather(lower_in, "dp", axis=1, tiled=True)
     latent_all = packed_all[:, :latent_dim]
     cosine, sines = rope_tables(position, head_dim)
     seg_rows, seg_columns = segment[:, None], segment[None, :]
     mixed_heads, query_rot, lse = attend(
         matmul_high(latent_all, wide_up), packed_all, cosine, sines, seg_rows, seg_columns, latent_dim
     )
-    middle = block_input + ring_scatter(matmul_high(mixed_heads, wide_merge), heads_count, 2)
+    inside = group_rows <= 1024
+
+    def job(*what):
+        return [Job(*what)] if inside else []
+
+    part_middle = matmul_high(mixed_heads, wide_merge)
+    if inside:
+        part_middle, d_activ = ring_scatter(
+            part_middle, heads_count, 2, job("nt", [grad_all], [wide_lower], 256)
+        )
+    else:
+        part_middle = ring_scatter(part_middle, heads_count, 2)
+        d_activ = matmul_high(grad_all, wide_lower.T)
+    middle = block_input + part_middle
     inv_two = lax.rsqrt(jnp.mean(middle * middle, axis=1, keepdims=True) + EPS_NORM)
     normed_two = middle * inv_two
     hidden_two = normed_two * gain_ffn
-    inside = group_rows <= 1024
-
-    def job(*what):
-        return [Job(*what)] if inside else []
-
-    made = ring_gather(hidden_two, heads_count, 3, job("nt", [grad_all], [wide_lower], 256))
-    hidden_all, d_activ = made if inside else (made, matmul_high(grad_all, wide_lower.T))
-    gate_pre = matmul_high(hidden_all, turned_gate.T)
-    up_pre = matmul_high(hidden_all, turned_upper.T)
+    if inside:
+        hidden_all, gate_pre, up_pre = ring_gather(
+            hidden_two, heads_count, 3, rights=[turned_gate, turned_upper]
+        )
+    else:
+        hidden_all = ring_gather(hidden_two, heads_count, 3)
+        gate_pre = matmul_high(hidden_all, turned_gate.T)
+        up_pre = matmul_high(hidden_all, turned_upper.T)
     sig_gate = jax.nn.sigmoid(gate_pre)
     silu_gate = gate_pre * sig_gate
     activ = silu_gate * up_pre
@@ -1056,9 +1290,14 @@
     grad_both = owned(grad_both, 1)
     d_normed_mid, grad_gain_ffn = norm_back(d_hidden_two, normed_two, inv_two, gain_ffn)
     d_middle = output_grad + d_normed_mid
-    made = ring_gather(d_middle, heads_count, 7, job("tn", [hidden_all], [d_up_pre], 256))
-    middle_all, grad_upper = made if inside else (made, matmul_high(d_up_pre.T, hidden_all))
-    d_mixed = matmul_high(middle_all, wide_merge.T)
+    if inside:
+        middle_all, d_mixed, grad_upper = ring_gather(
+            d_middle, heads_count, 7, job("tn", [hidden_all], [d_up_pre], 256), [wide_merge]
+        )
+    else:
+        middle_all = ring_gather(d_middle, heads_count, 7)
+        d_mixed = matmul_high(middle_all, wide_merge.T)
+        grad_upper = matmul_high(d_up_pre.T, hidden_all)
     d_query_pre, packed_part = attend_back(
         query_rot,
         packed_all,
@@ -1073,7 +1312,6 @@
         latent_dim,
     )
     packed_part, grad_both, grad_upper = lax.optimization_barrier((packed_part, grad_both, grad_upper))
-    grad_gate, grad_lower = jnp.split(grad_both, 2, axis=0)
     grad_upper = owned(grad_upper, 1)
     if inside:
         packed_grad, grad_merge, grad_up = ring_scatter(
@@ -1108,96 +1346,53 @@
         shared_cut, grad_gains.reshape(-1, 128), heads_count, dp_count, 10
     )
     gains_total = gains_total.reshape(-1)
-    values = (
-        norm_gains,
-        query_down,
-        key_value,
-        query_up,
-        head_merge,
-        gate_weight,
-        up_weight,
-        down_weight,
-    )
-    firsts = (
-        norm_gains_first,
-        query_down_first,
-        key_value_first,
-        query_up_first,
-        head_merge_first,
-        gate_weight_first,
-        up_weight_first,
-        down_weight_first,
-    )
-    seconds = (
-        norm_gains_second,
-        query_down_second,
-        key_value_second,
-        query_up_second,
-        head_merge_second,
-        gate_weight_second,
-        up_weight_second,
-        down_weight_second,
-    )
-    grads = (
-        gains_total,
-        shared[:, :latent_dim],
-        shared[:, latent_dim:],
-        grad_up,
-        grad_merge,
-        grad_gate.T,
-        grad_upper.T,
-        grad_lower,
-    )
-    stepped = [moments(values[slot], grads[slot], firsts[slot], seconds[slot]) for slot in range(8)]
-    replica_share = [1.0, 1.0 / heads_count, 1.0 / heads_count, 1.0, 1.0, 1.0, 1.0, 1.0]
-    square_rows = jnp.stack(
-        [
-            jnp.stack(
-                [jnp.sum(values[slot] * values[slot]), jnp.sum(stepped[slot][2] * stepped[slot][2])]
-            )
-            * replica_share[slot]
-            for slot in range(1, 8)
-        ]
-    )
-    square_tile = jnp.zeros((8, 128), jnp.float32).at[:7, :2].set(square_rows)
-    summed = sum_all(square_tile, heads_count, dp_count, 13)[:7, :2]
-    gains_row = jnp.stack(
-        [jnp.sum(norm_gains * norm_gains), jnp.sum(stepped[0][2] * stepped[0][2])]
-    )
-    norm_table = jnp.sqrt(jnp.concatenate([gains_row[None, :], summed], axis=0))
-    new_values = [
-        values[slot] - RATE * (norm_table[slot, 0] / norm_table[slot, 1]) * stepped[slot][2]
-        for slot in range(8)
-    ]
-    return (
-        block_output,
-        input_grad,
-        stepped[0][0],
-        stepped[0][1],
-        new_values[0],
-        stepped[1][0],
-        stepped[1][1],
-        new_values[1],
-        stepped[2][0],
-        stepped[2][1],
-        new_values[2],
-        stepped[3][0],
-        stepped[3][1],
-        new_values[3],
-        stepped[4][0],
-        stepped[4][1],
-        new_values[4],
-        stepped[5][0],
-        stepped[5][1],
-        new_values[5],
-        stepped[6][0],
-        stepped[6][1],
-        new_values[6],
-        stepped[7][0],
-        stepped[7][1],
-        new_values[7],
-        norm_table,
-    )
+    def flat(gains):
+        return gains.reshape(-1, 128)
+
+    everyone = 1.0 / (heads_count * dp_count)
+    early, early_sums = all_moments(
+        (5, 6, 7),
+        (1.0, 1.0, 1.0),
+        ((0, 0, 0), (1, 0, 0), (0, 0, down_weight.shape[0])),
+        (gate_weight.T, up_weight.T, down_weight),
+        (gate_weight_first.T, up_weight_first.T, down_weight_first),
+        (gate_weight_second.T, up_weight_second.T, down_weight_second),
+        (grad_both, grad_upper),
+    )
+    late, late_sums = all_moments(
+        (0, 1, 2, 3, 4),
+        (everyone, 1.0 / heads_count, 1.0 / heads_count, 1.0, 1.0),
+        ((0, 0, 0), (1, 0, 0), (1, latent_dim, 0), (2, 0, 0), (3, 0, 0)),
+        (flat(norm_gains), query_down, key_value, query_up, head_merge),
+        (flat(norm_gains_first), query_down_first, key_value_first, query_up_first, head_merge_first),
+        (flat(norm_gains_second), query_down_second, key_value_second, query_up_second, head_merge_second),
+        (flat(gains_total), shared, grad_up, grad_merge),
+    )
+    stepped = late + early
+    table = sum_all(early_sums + late_sums, heads_count, dp_count, 13)
+    new_values, norms = finish(
+        table,
+        (
+            flat(norm_gains),
+            query_down,
+            key_value,
+            query_up,
+            head_merge,
+            gate_weight.T,
+            up_weight.T,
+            down_weight,
+        ),
+        [entry[2] for entry in stepped],
+    )
+    results = []
+    for slot in range(8):
+        entry = (stepped[slot][0], stepped[slot][1], new_values[slot])
+        if slot == 0:
+            entry = tuple(x.reshape(-1) for x in entry)
+        if slot in (5, 6):
+            entry = tuple(x.T for x in entry)
+        results.extend(entry)
+    return (block_output, input_grad, *results, norms[:, :2])
 
 
 def solution(mesh):

time: 983 us -> 948 us (0.964)
  Pallas kernels: 768 us -> 833 us
  other arithmetic: 71.5 us -> 23.5 us
  matrix products: 92.9 us -> 52.6 us
  between operations: 25.3 us -> 14.7 us
    pallas_call x3 -> x6, Pallas kernels: 225 us -> 283 us  [the longest x3 238 us: ring_gather(): pl.pallas_call(functools.partial(gather_body, n, cuts, plan, len(rights))...]
    dot_general x10 -> x7, matrix products: 92.9 us -> 52.6 us  [matmul_high(): jnp.dot(left, right, precision=HIGH, preferred_element_type=jnp.float32)]
    reduce_sum x8 -> x0, other arithmetic: 32.5 us -> none  [the longest x7 31.2 us: on_device(): jnp.sum(stepped[slot][2] * stepped[slot][2])]
    sub x8 -> x0, other arithmetic: 11.4 us -> none  [on_device(): values[slot]]
  transfers between devices with their start and end apart: 9 -> 9, of which waited for: 0 -> 0; matrix products, arithmetic and copies ran while one was open for 11% -> 5% of each run, Pallas kernels for 49% -> 45%
where the time goes in v5:
time: 948 us; the launch traced here: 942 us
  Pallas kernels  833 us (88%)
  matrix products  52.6 us (6%)
  other arithmetic  23.5 us (2%)
  local copies, waits for them, and re-layouts  15.7 us (2%)
  between operations  14.7 us (2%)
    pallas_call x4, Pallas kernels, ring_scatter(): pl.pallas_call(functools.partial(scatter_body, n, cuts, plan), out_shape=...  317 us
    pallas_call x3, Pallas kernels, ring_gather(): pl.pallas_call(functools.partial(gather_body, n, cuts, plan, len(rights))...  238 us
    pallas_call x1, Pallas kernels, opening(): pl.pallas_call(functools.partial(opening_body, n, dp, cuts), out_shape=(f...  87.6 us
    dot_general x7, matrix products, matmul_high(): jnp.dot(left, right, precision=HIGH, preferred_element_type=jnp.float32)  52.6 us
    pallas_call x1, Pallas kernels, gather_and_sum(): pl.pallas_call(functools.partial(gather_and_sum_body, n, cuts), out_shape...  37.9 us
    pallas_call x1, Pallas kernels, scatter_and_turn(): pl.pallas_call(functools.partial(turn_body, n, dp, cuts), out_shape=(jax....  35.8 us
    pallas_call x2, Pallas kernels, all_moments(): pl.pallas_call(functools.partial(moments_body, slots, shares, offsets, le...  33.3 us
    pallas_call x1, Pallas kernels, attend_back(): pl.pallas_call(functools.partial(attend_back_body, latent_dim, rows), out...  25.6 us
  transfers between devices with their start and end apart: 9, of which 0 were waited for; matrix products, arithmetic and copies ran while one was open for 5% of the time, Pallas kernels for 45%

profile of v5, /device:TPU:0, one launch (start us, length us, event | category | flops | bytes accessed | tf_op | source)
XLA Modules:
  0.0 941.7 jit_solution(7424601088811820652)
XLA Ops:
  11.7 87.6 %opening.1 = (f32[1024,2048]{1,0:T(8,128)}, f32[2048,1024]{1,0:T(8,128)}, f32[2048,512]{1,0:T(8,128)}, f32[512,512]{1,0:T(8,128)}) custom-call(f32[128,2048]{1,0:T(8,128)} %grad.1, f32[512,1024]{1,0:T(8,128)} %refs_1_.3, f32[512,512]{1,0:T(8,128)} %refs_2_.5, f32[128,2048]{1,0:T(8,128)} %multiply_multiply_fusion.2.hidden), custom_call_target="tpu_custom_call" | custom-call | bytes 240000000 | tf_op jit(solution)/shard_map/opening/pallas_call | solution.py:613
  100.2 3.5 fusion.26
  104.1 6.7 multiply_reduce_fusion.8
  111.5 62.7 %ring_gather_1.1.packed.refs_3_ = f32[1024,1536]{1,0:T(8,128)S(1)} custom-call(f32[128,1536]{1,0:T(8,128)S(1)} %pad_maximum_fusion.x_ref), custom_call_target="tpu_custom_call" | custom-call | bytes 168750000 | tf_op jit(solution)/shard_map/ring_gather_1/pallas_call | solution.py:574
  182.1 7.7 fusion.raw
  189.7 11.3 %attend.1 = (f32[1024,512]{1,0:T(8,128)}, f32[1024,512]{1,0:T(8,128)}, f32[1024,256]{1,0:T(8,128)}) custom-call(f32[1024,512]{1,0:T(8,128)} %fusion.raw, f32[1024,1536]{1,0:T(8,128)} %copy-done, f32[1024,128]{1,0:T(8,128)} %get-tuple-element.298.cosine, f32[1024,128]{1,0:T(8,128)} %get-tuple-element.297.sines, s32[1024,1]{1,0:T(8,128)} %copy.58.seg_rows, ...), custom_call_target="tpu_custom_call" | custom-call | bytes 42000000 | tf_op jit(solution)/shard_map/attend/pallas_call | solution.py:939
  201.0 11.9 %fusion.27.x_ref = f32[1024,2048]{1,0:T(8,128)} fusion(f32[1024,512]{1,0:T(8,128)} %get-tuple-element.121.mixed.refs_1_, f32[512,2048]{1,0:T(8,128)} %all-gather.8.cloned.1.call-done.refs_0_), kind=kOutput, calls=%fused_computation.67 | convolution fusion | flops 6442450944 | bytes 14680064 | tf_op jit(solution)/shard_map/dot_general | solution.py:1023
  212.9 86.7 %ring_scatter_2.1 = (f32[128,2048]{1,0:T(8,128)S(1)}, f32[1024,704]{1,0:T(8,128)S(1)}) custom-call(f32[1024,2048]{1,0:T(8,128)} %fusion.27.x_ref, f32[1024,2048]{1,0:T(8,128)} %get-tuple-element.123.refs_0_.refs_2_, f32[704,2048]{1,0:T(8,128)} %all-gather.10.cloned.1.call-done.refs_1_), custom_call_target="tpu_custom_call" | custom-call | bytes 225000000 | tf_op jit(solution)/shard_map/ring_scatter_2/pallas_call | solution.py:730
  302.0 91.2 %ring_gather_3.1 = (f32[1024,2048]{1,0:T(8,128)}, f32[1024,704]{1,0:T(8,128)}, f32[1024,704]{1,0:T(8,128)}) custom-call(f32[128,2048]{1,0:T(8,128)} %multiply_multiply_fusion.1.x_ref, f32[704,2048]{1,0:T(8,128)} %all-gather.12.cloned.1.call-done.refs_0_.refs_2_, f32[704,2048]{1,0:T(8,128)} %all-gather.14.cloned.1.call-done.refs_1_.refs_3_), custom_call_target="tpu_custom_call" | custom-call | bytes 225000000 | tf_op jit(solution)/shard_map/ring_gather_3/pallas_call | solution.py:574
  393.2 5.3 fusion.7
  398.5 15.2 %fusion.28.x_ref = f32[1024,2048]{1,0:T(8,128)} fusion(f32[1024,704]{1,0:T(8,128)S(1)} %get-tuple-element.288.refs_3_, f32[704,2048]{1,0:T(8,128)} %all-gather.10.cloned.1.call-done.refs_1_), kind=kOutput, calls=%fused_computation.68 | convolution fusion | flops 8858370048 | bytes 17039360 | tf_op jit(solution)/shard_map/dot_general | solution.py:1023
  413.7 84.4 %ring_scatter_4.1 = (f32[128,2048]{1,0:T(8,128)}, f32[1024,2048]{1,0:T(8,128)}) custom-call(f32[1024,2048]{1,0:T(8,128)} %fusion.28.x_ref, f32[1024,704]{1,0:T(8,128)} %get-tuple-element.287.refs_0_.refs_1_, f32[1024,704]{1,0:T(8,128)} %get-tuple-element.286.refs_1_.refs_2_, f32[704,2048]{1,0:T(8,128)} %all-gather.12.cloned.1.call-done.refs_0_.refs_2_, ...), custom_call_target="tpu_custom_call" | custom-call | bytes 225000000 | tf_op jit(solution)/shard_map/ring_scatter_4/pallas_call | solution.py:730
  498.1 83.6 %ring_scatter_6.1 = (f32[128,2048]{1,0:T(8,128)}, f32[1408,2048]{1,0:T(8,128)}) custom-call(f32[1024,2048]{1,0:T(8,128)} %get-tuple-element.132.x_ref, f32[1024,2048]{1,0:T(8,128)} %get-tuple-element.133.refs_0_.refs_1_, f32[1024,704]{1,0:T(8,128)} %get-tuple-element.287.refs_0_.refs_1_, f32[1024,2048]{1,0:T(8,128)} %get-tuple-element.123.refs_0_.refs_2_, ...), custom_call_target="tpu_custom_call" | custom-call | bytes 225000000 | tf_op jit(solution)/shard_map/ring_scatter_6/pallas_call | solution.py:730
  586.5 84.0 %ring_gather_7.1 = (f32[1024,2048]{1,0:T(8,128)}, f32[1024,512]{1,0:T(8,128)}, f32[704,2048]{1,0:T(8,128)}) custom-call(f32[128,2048]{1,0:T(8,128)} %get-tuple-element.289.x_ref, f32[512,2048]{1,0:T(8,128)} %all-gather.8.cloned.1.call-done.refs_0_, f32[1024,2048]{1,0:T(8,128)} %get-tuple-element.133.refs_0_.refs_1_, ...), custom_call_target="tpu_custom_call" | custom-call | bytes 225000000 | tf_op jit(solution)/shard_map/ring_gather_7/pallas_call | solution.py:574
  670.5 25.6 %attend_back.1 = (f32[1024,512]{1,0:T(8,128)}, f32[1024,1536]{1,0:T(8,128)}) custom-call(f32[1024,512]{1,0:T(8,128)} %get-tuple-element.136.query, f32[1024,1536]{1,0:T(8,128)} %copy-done, f32[1024,128]{1,0:T(8,128)} %get-tuple-element.298.cosine, f32[1024,128]{1,0:T(8,128)} %get-tuple-element.297.sines, s32[1024,1]{1,0:T(8,128)} %copy.58.seg_rows, ...), custom_call_target="tpu_custom_call" | custom-call | bytes 90000000 | tf_op jit(solution)/shard_map/attend_back/pallas_call | solution.py:998
  697.7 62.8 %ring_scatter_8.1 = (f32[128,1536]{1,0:T(8,128)S(1)}, f32[512,2048]{1,0:T(8,128)}, f32[1024,512]{1,0:T(8,128)}) custom-call(f32[1024,1536]{1,0:T(8,128)} %get-tuple-element.142.x_ref, f32[1024,2048]{1,0:T(8,128)} %get-tuple-element.143.refs_0_, f32[1024,512]{1,0:T(8,128)S(1)} %copy-done.1, f32[1024,512]{1,0:T(8,128)} %get-tuple-element.144.refs_2_, ...), custom_call_target="tpu_custom_call" | custom-call | bytes 168750000 | tf_op jit(solution)/shard_map/ring_scatter_8/pallas_call | solution.py:730
  764.3 23.7 %dp_gather_11.1 = f32[512,1536]{1,0:T(8,128)} custom-call(f32[128,1536]{1,0:T(8,128)} %pad_maximum_fusion.1.x_ref), custom_call_target="tpu_custom_call" | custom-call | bytes 60000000 | tf_op jit(solution)/shard_map/dp_gather_11/pallas_call | solution.py:633
  788.4 4.7 fusion.2.hidden
  796.1 35.8 %scatter_and_turn.1 = (f32[64,1536]{1,0:T(8,128)S(1)}, f32[128,2048]{1,0:T(8,128)S(1)}) custom-call(f32[512,1536]{1,0:T(8,128)S(1)} %fusion.29.x_ref, f32[512,512]{1,0:T(8,128)S(1)} %fusion.2.hidden), custom_call_target="tpu_custom_call" | custom-call | bytes 105000000 | tf_op jit(solution)/shard_map/scatter_and_turn/pallas_call | solution.py:759
  832.0 16.6 %moments_5.1 = (f32[704,512]{1,0:T(8,128)}, f32[704,512]{1,0:T(8,128)}, f32[704,512]{1,0:T(8,128)S(1)}, f32[704,512]{1,0:T(8,128)}, f32[704,512]{1,0:T(8,128)}, ...) custom-call(f32[704,512]{1,0:T(8,128)} %bitcast.53, ...), custom_call_target="tpu_custom_call" | custom-call | bytes 36000000 | tf_op jit(solution)/shard_map/moments_5/pallas_call | solution.py:1118
  850.3 37.9 %gather_and_sum.1 = (f32[512,1536]{1,0:T(8,128)S(1)}, f32[40,128]{1,0:T(8,128)S(1)}) custom-call(f32[64,1536]{1,0:T(8,128)S(1)} %get-tuple-element.155.x_ref, f32[40,128]{1,0:T(8,128)S(1)} %maximum_bitcast_fusion.gains), custom_call_target="tpu_custom_call" | custom-call | bytes 105000000 | tf_op jit(solution)/shard_map/gather_and_sum/pallas_call | solution.py:848
  889.9 16.7 %moments_0.1 = (f32[40,128]{1,0:T(8,128)}, f32[40,128]{1,0:T(8,128)}, f32[40,128]{1,0:T(8,128)S(1)}, f32[512,1024]{1,0:T(8,128)}, f32[512,1024]{1,0:T(8,128)}, /...) custom-call(f32[40,128]{1,0:T(8,128)S(1)} %bitcast.44, ...), custom_call_target="tpu_custom_call" | custom-call | bytes 36000000 | tf_op jit(solution)/shard_map/moments_0/pallas_call | solution.py:1118
  908.1 10.0 %sum_all_13.1.table = f32[8,128]{1,0:T(8,128)} custom-call(f32[8,128]{1,0:T(8,128)} %add.74.x_ref), custom_call_target="tpu_custom_call" | custom-call | bytes 24000000 | tf_op jit(solution)/shard_map/sum_all_13/pallas_call | solution.py:869
  922.2 12.1 %finish.1 = (f32[40,128]{1,0:T(8,128)}, f32[512,1024]{1,0:T(8,128)}, f32[512,512]{1,0:T(8,128)}, f32[256,512]{1,0:T(8,128)}, f32[512,512]{1,0:T(8,128)}, /*index...) custom-call(f32[8,128]{1,0:T(8,128)S(1)} %copy-done.16, f32[40,128]{1,0:T(8,128)S(1)} %bitcast.45, ...), custom_call_target="tpu_custom_call" | custom-call | bytes 27000000 | tf_op jit(solution)/shard_map/finish/pallas_call | solution.py:1151
  (129 shorter events, 39.4 us)
Async XLA Ops:
  7.2 174.9 %all-gather.6.cloned.1.call-start = ((), (), s32[]{:S(2)}) async-start(), calls=%async_computation.4 | async-start | bytes 2621440 | tf_op jit(solution)/shard_map/all_gather | solution.py:1216
  11.7 88.5 %copy-start.13 = (f32[5120]{0:T(1024)S(1)}, f32[5120]{0:T(1024)}, u32[]{:S(2)}) copy-start(f32[5120]{0:T(1024)} %param.30) | copy-start | bytes 61444
  11.7 88.5 %copy-start.21 = (f32[128,2048]{1,0:T(8,128)S(1)}, f32[128,2048]{1,0:T(8,128)}, u32[]{:S(2)}) copy-start(f32[128,2048]{1,0:T(8,128)} %multiply_multiply_fusion.2.hidden) | copy-start | bytes 3145732
  99.4 101.7 %all-gather.8.cloned.1.call-start = ((), (), s32[]{:S(2)}) async-start(), calls=%async_computation.5 | async-start | bytes 5242880 | tf_op jit(solution)/shard_map/all_gather | solution.py:1217
  100.1 112.8 %all-gather.10.cloned.1.call-start = ((), (), s32[]{:S(2)}) async-start(), calls=%async_computation.6 | async-start | bytes 7208960 | tf_op jit(solution)/shard_map/all_gather | solution.py:1227
  103.9 74.1 %copy-start.30 = (s32[1024]{0:T(1024)}, s32[1024]{0:T(1024)S(1)}, u32[]{:S(2)}) copy-start(s32[1024]{0:T(1024)S(1)} %convert_reduce_fusion) | copy-start | bytes 12292
  110.8 63.3 %copy-start.26 = (f32[128,1024]{1,0:T(8,128)}, f32[128,1024]{1,0:T(8,128)S(1)}, u32[]{:S(2)}) copy-start(f32[128,1024]{1,0:T(8,128)S(1)} %get-tuple-element.302) | copy-start | bytes 1572868
  111.4 190.6 %all-gather.14.cloned.1.call-start = ((), (), s32[]{:S(2)}) async-start(), calls=%async_computation.8 | async-start | bytes 7208960 | tf_op jit(solution)/shard_map/all_gather | solution.py:1231
  176.8 125.1 %all-gather.12.cloned.1.call-start = ((), (), s32[]{:S(2)}) async-start(), calls=%async_computation.7 | async-start | bytes 7208960 | tf_op jit(solution)/shard_map/all_gather | solution.py:1230
  177.4 518.7 %reduce-scatter.5.cloned.1.call-start = ((), (), s32[]{:S(2)}) async-start(), calls=%async_computation.9 | async-start | bytes 14417920 | tf_op jit(solution)/shard_map/reduce_scatter | solution.py:1061
  212.9 86.7 %copy-start.19 = (f32[128,2048]{1,0:T(8,128)S(1)}, f32[128,2048]{1,0:T(8,128)}, u32[]{:S(2)}) copy-start(f32[128,2048]{1,0:T(8,128)} %param.27) | copy-start | bytes 3145732
  581.7 178.8 %reduce-scatter.7.cloned.1.call-start = ((), (), s32[]{:S(2)}) async-start(), calls=%async_computation.10 | async-start | bytes 7208960 | tf_op jit(solution)/shard_map/reduce_scatter | solution.py:1061
  696.2 135.8 %reduce-scatter.9.cloned.1.call-start = ((), (), s32[]{:S(2)}) async-start(), calls=%async_computation.11 | async-start | bytes 2621440 | tf_op jit(solution)/shard_map/reduce_scatter | solution.py:1061
  764.3 24.0 %copy-start.2 = (f32[512,512]{1,0:T(8,128)S(1)}, f32[512,512]{1,0:T(8,128)}, u32[]{:S(2)}) copy-start(f32[512,512]{1,0:T(8,128)} %refs_2_.5) | copy-start | bytes 3145732
  764.3 24.0 %copy-start.17 = (f32[512,1024]{1,0:T(8,128)S(1)}, f32[512,1024]{1,0:T(8,128)}, u32[]{:S(2)}) copy-start(f32[512,1024]{1,0:T(8,128)} %refs_1_.3) | copy-start | bytes 6291460
  788.1 101.8 %reduce-scatter.11.cloned.1.call-start = ((), (), s32[]{:S(2)}) async-start(), calls=%async_computation.12 | async-start | bytes 5242880 | tf_op jit(solution)/shard_map/reduce_scatter | solution.py:1061
  832.0 16.6 %copy-start.20 = (f32[128,2048]{1,0:T(8,128)S(1)}, f32[128,2048]{1,0:T(8,128)}, u32[]{:S(2)}) copy-start(f32[128,2048]{1,0:T(8,128)} %param.27) | copy-start | bytes 3145732
  832.0 17.0 %copy-start.25 = (f32[128,2048]{1,0:T(8,128)S(1)}, f32[128,2048]{1,0:T(8,128)}, u32[]{:S(2)}) copy-start(f32[128,2048]{1,0:T(8,128)} %get-tuple-element.289.x_ref) | copy-start | bytes 3145732
  848.6 41.3 %copy-start.5 = (f32[256,512]{1,0:T(8,128)S(1)}, f32[256,512]{1,0:T(8,128)}, u32[]{:S(2)}) copy-start(f32[256,512]{1,0:T(8,128)} %refs_3_.3) | copy-start | bytes 1572868
  848.6 41.3 %copy-start.10 = (f32[256,512]{1,0:T(8,128)S(1)}, f32[256,512]{1,0:T(8,128)}, u32[]{:S(2)}) copy-start(f32[256,512]{1,0:T(8,128)} %refs_8_.2) | copy-start | bytes 1572868
  848.6 41.3 %copy-start.14 = (f32[5120]{0:T(1024)S(1)}, f32[5120]{0:T(1024)}, u32[]{:S(2)}) copy-start(f32[5120]{0:T(1024)} %param.31) | copy-start | bytes 61444
  848.6 41.3 %copy-start.15 = (f32[5120]{0:T(1024)S(1)}, f32[5120]{0:T(1024)}, u32[]{:S(2)}) copy-start(f32[5120]{0:T(1024)} %param.32) | copy-start | bytes 61444
  889.9 28.1 %copy-start.3 = (f32[512,512]{1,0:T(8,128)S(1)}, f32[512,512]{1,0:T(8,128)}, u32[]{:S(2)}) copy-start(f32[512,512]{1,0:T(8,128)} %refs_2_.5) | copy-start | bytes 3145732
  889.9 28.1 %copy-start.4 = (f32[512,512]{1,0:T(8,128)S(1)}, f32[512,512]{1,0:T(8,128)}, u32[]{:S(2)}) copy-start(f32[512,512]{1,0:T(8,128)} %refs_4_.3) | copy-start | bytes 3145732
  (17 other events, 46.4 us)
Sparse Core Ops, SparseCore 0:
  99.5 22.2 all-gather.5
  123.4 34.4 all-gather.7
  159.5 43.3 all-gather.9
  204.3 43.3 all-gather.13
  249.2 43.3 all-gather.11
  581.9 92.6 reduce-scatter.4
  696.3 55.1 reduce-scatter.6
  788.2 35.0 reduce-scatter.8
  832.1 43.5 reduce-scatter.10

commit v6 on v5

--- a/solution.py
+++ b/solution.py
@@ -753,7 +753,7 @@
     ring.end()
 
 
-def scatter_and_turn(x, hidden, n, dp, number, cuts=2):
+def scatter_and_turn(x, hidden, n, dp, number, cuts=4):
     rows, columns = x.shape[0] // n, x.shape[1]
     cuts = min(cuts, rows // 16)
     return pl.pallas_call(
@@ -1077,6 +1077,11 @@
     return next(c for c in (64, 32, 16, 8) if rows % c == 0)
 
 
+def lamb_limit(times, values, grads):
+    sizes = [times * padded(x.shape, 4) for x in values] + [padded(x.shape, 4) for x in grads]
+    return (4 << 20) + sum(sizes)
+
+
 def moments_body(slots, shares, offsets, count_grads, *refs):
     count = len(slots)
     values, firsts, seconds = refs[:count], refs[count : 2 * count], refs[2 * count : 3 * count]
@@ -1123,7 +1128,7 @@
         ),
         in_specs=spaces(3 * len(values) + len(grads), pltpu.VMEM),
         out_specs=tuple(spaces(3 * len(values) + 1, pltpu.VMEM)),
-        compiler_params=pltpu.CompilerParams(vmem_limit_bytes=52 << 20),
+        compiler_params=pltpu.CompilerParams(vmem_limit_bytes=lamb_limit(6, values, grads)),
         cost_estimate=cost(12.0),
         name=f"moments_{slots[0]}",
     )(*values, *firsts, *seconds, *grads)
@@ -1153,7 +1158,7 @@
         out_shape=(*[shape(value.shape, jnp.float32) for value in values], shape(table.shape, jnp.float32)),
         in_specs=spaces(2 * len(values) + 1, pltpu.VMEM),
         out_specs=tuple(spaces(len(values) + 1, pltpu.VMEM)),
-        compiler_params=pltpu.CompilerParams(vmem_limit_bytes=48 << 20),
+        compiler_params=pltpu.CompilerParams(vmem_limit_bytes=lamb_limit(3, values, ())),
         cost_estimate=cost(9.0),
         name="finish",
     )(table, *values, *updates)

time: 948 us -> 981 us (1.035)
  local copies, waits for them, and re-layouts: 15.7 us -> 67.2 us
  Pallas kernels: 833 us -> 814 us
    unnamed x65 -> x149, local copies, waits for them, and re-layouts: 13.9 us -> 64.7 us
    pallas_call x2, Pallas kernels: 33.3 us -> 20.1 us  [all_moments(): pl.pallas_call(functools.partial(moments_body, slots, shares, offsets, le...]
  transfers between devices with their start and end apart: 9 -> 9, of which waited for: 0 -> 0; matrix products, arithmetic and copies ran while one was open for 5% -> 5% of each run, Pallas kernels for 45% -> 43%
where the time goes in v6:
time: 981 us; the launch traced here: 973 us
  Pallas kernels  814 us (83%)
  local copies, waits for them, and re-layouts  67.2 us (7%)
  matrix products  52.5 us (5%)
  other arithmetic  22.5 us (2%)
  between operations  14.6 us (1%)
    pallas_call x4, Pallas kernels, ring_scatter(): pl.pallas_call(functools.partial(scatter_body, n, cuts, plan), out_shape=...  316 us
    pallas_call x3, Pallas kernels, ring_gather(): pl.pallas_call(functools.partial(gather_body, n, cuts, plan, len(rights))...  239 us
    pallas_call x1, Pallas kernels, opening(): pl.pallas_call(functools.partial(opening_body, n, dp, cuts), out_shape=(f...  87.6 us
    unnamed x149, local copies, waits for them, and re-layouts  64.7 us
    dot_general x7, matrix products, matmul_high(): jnp.dot(left, right, precision=HIGH, preferred_element_type=jnp.float32)  52.5 us
    pallas_call x1, Pallas kernels, gather_and_sum(): pl.pallas_call(functools.partial(gather_and_sum_body, n, cuts), out_shape...  38.9 us
    pallas_call x1, Pallas kernels, scatter_and_turn(): pl.pallas_call(functools.partial(turn_body, n, dp, cuts), out_shape=(jax....  34.4 us
    pallas_call x1, Pallas kernels, attend_back(): pl.pallas_call(functools.partial(attend_back_body, latent_dim, rows), out...  25.8 us
  transfers between devices with their start and end apart: 9, of which 0 were waited for; matrix products, arithmetic and copies ran while one was open for 5% of the time, Pallas kernels for 43%

profile of v6, /device:TPU:0, one launch (start us, length us, event | category | flops | bytes accessed | tf_op | source)
XLA Modules:
  0.0 973.1 jit_solution(12931484217068808232)
XLA Ops:
  11.7 87.6 %opening.1 = (f32[1024,2048]{1,0:T(8,128)}, f32[2048,1024]{1,0:T(8,128)}, f32[2048,512]{1,0:T(8,128)}, f32[512,512]{1,0:T(8,128)}) custom-call(f32[128,2048]{1,0:T(8,128)} %grad.1, f32[512,1024]{1,0:T(8,128)} %refs_1_.3, f32[512,512]{1,0:T(8,128)} %refs_2_.5, f32[128,2048]{1,0:T(8,128)} %multiply_multiply_fusion.2.hidden), custom_call_target="tpu_custom_call" | custom-call | bytes 240000000 | tf_op jit(solution)/shard_map/opening/pallas_call | solution.py:613
  100.9 3.5 fusion.26
  104.8 6.6 multiply_reduce_fusion.8
  112.4 63.2 %ring_gather_1.1.packed.refs_3_ = f32[1024,1536]{1,0:T(8,128)S(1)} custom-call(f32[128,1536]{1,0:T(8,128)S(1)} %pad_maximum_fusion.x_ref), custom_call_target="tpu_custom_call" | custom-call | bytes 168750000 | tf_op jit(solution)/shard_map/ring_gather_1/pallas_call | solution.py:574
  183.1 7.6 fusion.raw
  190.7 11.2 %attend.1 = (f32[1024,512]{1,0:T(8,128)}, f32[1024,512]{1,0:T(8,128)}, f32[1024,256]{1,0:T(8,128)}) custom-call(f32[1024,512]{1,0:T(8,128)} %fusion.raw, f32[1024,1536]{1,0:T(8,128)} %copy-done, f32[1024,128]{1,0:T(8,128)} %get-tuple-element.298.cosine, f32[1024,128]{1,0:T(8,128)} %get-tuple-element.297.sines, s32[1024,1]{1,0:T(8,128)} %copy.58.seg_rows, ...), custom_call_target="tpu_custom_call" | custom-call | bytes 42000000 | tf_op jit(solution)/shard_map/attend/pallas_call | solution.py:939
  201.9 11.9 %fusion.27.x_ref = f32[1024,2048]{1,0:T(8,128)} fusion(f32[1024,512]{1,0:T(8,128)} %get-tuple-element.121.mixed.refs_1_, f32[512,2048]{1,0:T(8,128)} %all-gather.8.cloned.1.call-done.refs_0_), kind=kOutput, calls=%fused_computation.67 | convolution fusion | flops 6442450944 | bytes 14680064 | tf_op jit(solution)/shard_map/dot_general | solution.py:1023
  213.8 86.5 %ring_scatter_2.1 = (f32[128,2048]{1,0:T(8,128)S(1)}, f32[1024,704]{1,0:T(8,128)S(1)}) custom-call(f32[1024,2048]{1,0:T(8,128)} %fusion.27.x_ref, f32[1024,2048]{1,0:T(8,128)} %get-tuple-element.123.refs_0_.refs_2_, f32[704,2048]{1,0:T(8,128)} %all-gather.10.cloned.1.call-done.refs_1_), custom_call_target="tpu_custom_call" | custom-call | bytes 225000000 | tf_op jit(solution)/shard_map/ring_scatter_2/pallas_call | solution.py:730
  302.6 91.5 %ring_gather_3.1 = (f32[1024,2048]{1,0:T(8,128)}, f32[1024,704]{1,0:T(8,128)}, f32[1024,704]{1,0:T(8,128)}) custom-call(f32[128,2048]{1,0:T(8,128)} %multiply_multiply_fusion.1.x_ref, f32[704,2048]{1,0:T(8,128)} %all-gather.12.cloned.1.call-done.refs_0_.refs_2_, f32[704,2048]{1,0:T(8,128)} %all-gather.14.cloned.1.call-done.refs_1_.refs_3_), custom_call_target="tpu_custom_call" | custom-call | bytes 225000000 | tf_op jit(solution)/shard_map/ring_gather_3/pallas_call | solution.py:574
  394.1 5.3 fusion.7
  399.5 15.2 %fusion.28.x_ref = f32[1024,2048]{1,0:T(8,128)} fusion(f32[1024,704]{1,0:T(8,128)S(1)} %get-tuple-element.288.refs_3_, f32[704,2048]{1,0:T(8,128)} %all-gather.10.cloned.1.call-done.refs_1_), kind=kOutput, calls=%fused_computation.68 | convolution fusion | flops 8858370048 | bytes 17039360 | tf_op jit(solution)/shard_map/dot_general | solution.py:1023
  414.7 84.5 %ring_scatter_4.1 = (f32[128,2048]{1,0:T(8,128)}, f32[1024,2048]{1,0:T(8,128)}) custom-call(f32[1024,2048]{1,0:T(8,128)} %fusion.28.x_ref, f32[1024,704]{1,0:T(8,128)} %get-tuple-element.287.refs_0_.refs_1_, f32[1024,704]{1,0:T(8,128)} %get-tuple-element.286.refs_1_.refs_2_, f32[704,2048]{1,0:T(8,128)} %all-gather.12.cloned.1.call-done.refs_0_.refs_2_, ...), custom_call_target="tpu_custom_call" | custom-call | bytes 225000000 | tf_op jit(solution)/shard_map/ring_scatter_4/pallas_call | solution.py:730
  499.2 83.7 %ring_scatter_6.1 = (f32[128,2048]{1,0:T(8,128)}, f32[1408,2048]{1,0:T(8,128)}) custom-call(f32[1024,2048]{1,0:T(8,128)} %get-tuple-element.132.x_ref, f32[1024,2048]{1,0:T(8,128)} %get-tuple-element.133.refs_0_.refs_1_, f32[1024,704]{1,0:T(8,128)} %get-tuple-element.287.refs_0_.refs_1_, f32[1024,2048]{1,0:T(8,128)} %get-tuple-element.123.refs_0_.refs_2_, ...), custom_call_target="tpu_custom_call" | custom-call | bytes 225000000 | tf_op jit(solution)/shard_map/ring_scatter_6/pallas_call | solution.py:730
  588.3 84.0 %ring_gather_7.1 = (f32[1024,2048]{1,0:T(8,128)}, f32[1024,512]{1,0:T(8,128)}, f32[704,2048]{1,0:T(8,128)}) custom-call(f32[128,2048]{1,0:T(8,128)} %get-tuple-element.289.x_ref, f32[512,2048]{1,0:T(8,128)} %all-gather.8.cloned.1.call-done.refs_0_, f32[1024,2048]{1,0:T(8,128)} %get-tuple-element.133.refs_0_.refs_1_, ...), custom_call_target="tpu_custom_call" | custom-call | bytes 225000000 | tf_op jit(solution)/shard_map/ring_gather_7/pallas_call | solution.py:574
  672.3 25.8 %attend_back.1 = (f32[1024,512]{1,0:T(8,128)}, f32[1024,1536]{1,0:T(8,128)}) custom-call(f32[1024,512]{1,0:T(8,128)} %get-tuple-element.136.query, f32[1024,1536]{1,0:T(8,128)} %copy-done, f32[1024,128]{1,0:T(8,128)} %get-tuple-element.298.cosine, f32[1024,128]{1,0:T(8,128)} %get-tuple-element.297.sines, s32[1024,1]{1,0:T(8,128)} %copy.58.seg_rows, ...), custom_call_target="tpu_custom_call" | custom-call | bytes 90000000 | tf_op jit(solution)/shard_map/attend_back/pallas_call | solution.py:998
  699.7 61.7 %ring_scatter_8.1 = (f32[128,1536]{1,0:T(8,128)S(1)}, f32[512,2048]{1,0:T(8,128)}, f32[1024,512]{1,0:T(8,128)S(1)}) custom-call(f32[1024,1536]{1,0:T(8,128)} %get-tuple-element.142.x_ref, f32[1024,2048]{1,0:T(8,128)} %get-tuple-element.143.refs_0_, f32[1024,512]{1,0:T(8,128)S(1)} %copy-done.2, f32[1024,512]{1,0:T(8,128)} %get-tuple-element.144.refs_2_, ...), custom_call_target="tpu_custom_call" | custom-call | bytes 168750000 | tf_op jit(solution)/shard_map/ring_scatter_8/pallas_call | solution.py:730
  764.5 23.2 %dp_gather_11.1 = f32[512,1536]{1,0:T(8,128)} custom-call(f32[128,1536]{1,0:T(8,128)} %pad_maximum_fusion.1.x_ref), custom_call_target="tpu_custom_call" | custom-call | bytes 60000000 | tf_op jit(solution)/shard_map/dp_gather_11/pallas_call | solution.py:633
  788.0 4.7 fusion.2.hidden
  795.8 34.4 %scatter_and_turn.1 = (f32[64,1536]{1,0:T(8,128)S(1)}, f32[128,2048]{1,0:T(8,128)S(1)}) custom-call(f32[512,1536]{1,0:T(8,128)S(1)} %fusion.29.x_ref, f32[512,512]{1,0:T(8,128)S(1)} %fusion.2.hidden), custom_call_target="tpu_custom_call" | custom-call | bytes 105000000 | tf_op jit(solution)/shard_map/scatter_and_turn/pallas_call | solution.py:759
  847.4 8.3 moments_5.1
  858.0 38.9 %gather_and_sum.1 = (f32[512,1536]{1,0:T(8,128)S(1)}, f32[40,128]{1,0:T(8,128)S(1)}) custom-call(f32[64,1536]{1,0:T(8,128)S(1)} %get-tuple-element.155.x_ref, f32[40,128]{1,0:T(8,128)S(1)} %maximum_bitcast_fusion.gains), custom_call_target="tpu_custom_call" | custom-call | bytes 105000000 | tf_op jit(solution)/shard_map/gather_and_sum/pallas_call | solution.py:848
  915.2 11.8 %moments_0.1 = (f32[40,128]{1,0:T(8,128)}, f32[40,128]{1,0:T(8,128)}, f32[40,128]{1,0:T(8,128)S(1)}, f32[512,1024]{1,0:T(8,128)}, f32[512,1024]{1,0:T(8,128)}, /...) custom-call(f32[40,128]{1,0:T(8,128)S(1)} %bitcast.54, ...), custom_call_target="tpu_custom_call" | custom-call | bytes 36000000 | tf_op jit(solution)/shard_map/moments_0/pallas_call | solution.py:1123
  931.6 10.5 %sum_all_13.1.table = f32[8,128]{1,0:T(8,128)} custom-call(f32[8,128]{1,0:T(8,128)} %add.74.x_ref), custom_call_target="tpu_custom_call" | custom-call | bytes 24000000 | tf_op jit(solution)/shard_map/sum_all_13/pallas_call | solution.py:869
  958.4 7.4 finish.1
  (213 shorter events, 89.4 us)
Async XLA Ops:
  7.2 175.9 %all-gather.6.cloned.1.call-start = ((), (), s32[]{:S(2)}) async-start(), calls=%async_computation.4 | async-start | bytes 2621440 | tf_op jit(solution)/shard_map/all_gather | solution.py:1221
  8.6 90.7 %copy-start.71 = (f32[128]{0:T(128)}, f32[128]{0:T(128)S(1)}, u32[]{:S(2)}) copy-start(f32[128]{0:T(128)S(1)} %add_rsqrt_fusion.2) | copy-start | bytes 1540
  11.7 89.2 %copy-start.59 = (f32[128,2048]{1,0:T(8,128)S(1)}, f32[128,2048]{1,0:T(8,128)}, u32[]{:S(2)}) copy-start(f32[128,2048]{1,0:T(8,128)} %multiply_multiply_fusion.2.hidden) | copy-start | bytes 3145732
  99.4 102.5 %all-gather.8.cloned.1.call-start = ((), (), s32[]{:S(2)}) async-start(), calls=%async_computation.5 | async-start | bytes 5242880 | tf_op jit(solution)/shard_map/all_gather | solution.py:1222
  100.1 113.7 %all-gather.10.cloned.1.call-start = ((), (), s32[]{:S(2)}) async-start(), calls=%async_computation.6 | async-start | bytes 7208960 | tf_op jit(solution)/shard_map/all_gather | solution.py:1232
  104.6 74.4 %copy-start.69 = (s32[1024]{0:T(1024)}, s32[1024]{0:T(1024)S(1)}, u32[]{:S(2)}) copy-start(s32[1024]{0:T(1024)S(1)} %convert_reduce_fusion) | copy-start | bytes 12292
  112.3 190.3 %all-gather.14.cloned.1.call-start = ((), (), s32[]{:S(2)}) async-start(), calls=%async_computation.8 | async-start | bytes 7208960 | tf_op jit(solution)/shard_map/all_gather | solution.py:1236
  178.2 124.4 %all-gather.12.cloned.1.call-start = ((), (), s32[]{:S(2)}) async-start(), calls=%async_computation.7 | async-start | bytes 7208960 | tf_op jit(solution)/shard_map/all_gather | solution.py:1235
  178.8 519.4 %reduce-scatter.5.cloned.1.call-start = ((), (), s32[]{:S(2)}) async-start(), calls=%async_computation.9 | async-start | bytes 14417920 | tf_op jit(solution)/shard_map/reduce_scatter | solution.py:1061
  213.8 86.5 %copy-start.57 = (f32[128,2048]{1,0:T(8,128)S(1)}, f32[128,2048]{1,0:T(8,128)}, u32[]{:S(2)}) copy-start(f32[128,2048]{1,0:T(8,128)} %param.27) | copy-start | bytes 3145732
  399.5 15.2 %copy-start.62 = (f32[1024,704]{1,0:T(8,128)}, f32[1024,704]{1,0:T(8,128)S(1)}, u32[]{:S(2)}) copy-start(f32[1024,704]{1,0:T(8,128)S(1)} %get-tuple-element.288.refs_3_) | copy-start | bytes 8650756
  583.0 179.8 %reduce-scatter.7.cloned.1.call-start = ((), (), s32[]{:S(2)}) async-start(), calls=%async_computation.10 | async-start | bytes 7208960 | tf_op jit(solution)/shard_map/reduce_scatter | solution.py:1061
  698.2 133.0 %reduce-scatter.9.cloned.1.call-start = ((), (), s32[]{:S(2)}) async-start(), calls=%async_computation.11 | async-start | bytes 2621440 | tf_op jit(solution)/shard_map/reduce_scatter | solution.py:1061
  699.7 63.1 %copy-start.65 = (f32[128,1024]{1,0:T(8,128)S(1)}, f32[128,1024]{1,0:T(8,128)}, u32[]{:S(2)}) copy-start(f32[128,1024]{1,0:T(8,128)} %copy-done.64) | copy-start | bytes 1572868
  764.5 23.5 %copy-start.1 = (f32[512,1024]{1,0:T(8,128)S(1)}, f32[512,1024]{1,0:T(8,128)}, u32[]{:S(2)}) copy-start(f32[512,1024]{1,0:T(8,128)} %refs_1_.3) | copy-start | bytes 6291460
  764.5 23.5 %copy-start.3 = (f32[512,512]{1,0:T(8,128)S(1)}, f32[512,512]{1,0:T(8,128)}, u32[]{:S(2)}) copy-start(f32[512,512]{1,0:T(8,128)} %refs_2_.5) | copy-start | bytes 3145732
  787.8 111.4 %reduce-scatter.11.cloned.1.call-start = ((), (), s32[]{:S(2)}) async-start(), calls=%async_computation.12 | async-start | bytes 5242880 | tf_op jit(solution)/shard_map/reduce_scatter | solution.py:1061
  788.0 4.7 copy-start.56
  847.3 8.3 copy-start.15
  847.3 8.3 copy-start.58
  847.3 8.3 copy-start.72
  847.3 8.7 copy-start.70
  847.3 8.7 copy-start.63
  915.2 27.0 %copy-start.50 = (f32[5120]{0:T(1024)S(1)}, f32[5120]{0:T(1024)}, u32[]{:S(2)}) copy-start(f32[5120]{0:T(1024)} %param.30) | copy-start | bytes 61444
  (59 other events, 83.8 us)
Sparse Core Ops, SparseCore 0:
  99.5 22.2 all-gather.5
  123.4 34.4 all-gather.7
  159.4 43.3 all-gather.9
  204.3 43.3 all-gather.13
  249.1 43.3 all-gather.11
  583.1 91.4 reduce-scatter.4
  698.3 54.4 reduce-scatter.6
  787.9 35.0 reduce-scatter.8
  831.3 44.1 reduce-scatter.10
